TPU v7x, 32 devices: a whole 2x2x4 slice. The times are simulated.
32 devices in a mesh: vel: 8 (over y, x, core), space: 4 (over z).
Axes of the slice: x: 2, y: 2, z: 4, core: 2. Of those that a mesh axis runs over, the one named last changes fastest.
Arguments:
- distribution: float32 [1024, 64, 512], P('vel', 'space'), may hold values from -6 to 6
- courant: float32 [1024], replicated, may hold values from -0.9 to 0.9
- gain_matrix: bfloat16 [1024, 1024], replicated, may hold values from -0.1875 to 0.1875
- product_matrix: bfloat16 [1024, 1024], replicated, may hold values from -0.1875 to 0.1875
- collision_rate: float32 [64, 512], P('space'), may hold values from 0.5 to 2
Outputs:
- final_state: float32 [1024, 64, 512], P('vel', 'space')
All inputs are finite; a program needn't handle non-finite values.
Results may differ from a plain program's by a relative error of at most 0.0016.
Values may be sent and summed in bfloat16 or wider, within the bound.
No kernel may reach another device: no remote copies, remote signals or barrier semaphores. Data moves between devices by JAX's collectives and lax.ppermute only.
A program may use at most 64 MiB of HBM per device.

v0:
```python
import jax
import jax.numpy as jnp
from jax import lax
from jax.sharding import PartitionSpec as P

STEPS = 2


time_step = 0.2


def with_halo(block, sides, width):
    for axis, dim in sides:
        count = lax.axis_size(axis)
        forward = [(i, i + 1) for i in range(count - 1)]
        forward.append((count - 1, 0))
        backward = [(target, source) for source, target in forward]
        low = lax.ppermute(
            lax.slice_in_dim(block, block.shape[dim] - width, None, axis=dim), axis, forward
        )
        high = lax.ppermute(lax.slice_in_dim(block, 0, width, axis=dim), axis, backward)
        block = jnp.concatenate([low, block, high], axis=dim)
    return block


def minmod(first, second):
    return jnp.maximum(jnp.minimum(first, second), 0.0) + jnp.minimum(
        jnp.maximum(first, second), 0.0
    )


def change(widened, speeds):
    differ = widened[:, 1:] - widened[:, :-1]
    slopes = minmod(differ[:, 1:], differ[:, :-1])
    inner = widened.shape[1] - 4
    left_value = widened[:, 1 : inner + 2]
    right_value = widened[:, 2 : inner + 3]
    left_slope = slopes[:, 0 : inner + 1]
    right_slope = slopes[:, 1 : inner + 2]
    upward = jnp.maximum(speeds, 0.0)
    downward = jnp.minimum(speeds, 0.0)
    fluxes = upward * (left_value + 0.5 * (1.0 - speeds) * left_slope) + downward * (
        right_value - 0.5 * (1.0 + speeds) * right_slope
    )
    return -(fluxes[:, 1:] - fluxes[:, :-1])


def extend(field):
    return with_halo(field, (("space", 1),), 2)


def advect(field, speeds):
    section = field + change(extend(field), speeds)
    return 0.5 * field + 0.5 * (section + change(extend(section), speeds))


def collide(pieces, gain_matrix, product_matrix):
    columns = pieces.reshape(pieces.shape[0], -1)
    first_term = jnp.dot(gain_matrix, columns, preferred_element_type=jnp.float32)
    second_term = jnp.dot(product_matrix, columns, preferred_element_type=jnp.float32)
    return (first_term * second_term).astype(jnp.bfloat16).reshape(pieces.shape)


def update(smoothed, rounded, gained, rate):
    return smoothed + time_step * (gained.astype(jnp.float32) - rate * rounded.astype(jnp.float32))


def body(distribution, courant, gain_matrix, product_matrix, collision_rate):
    local_count = distribution.shape[0]
    groups = lax.axis_size("vel")
    member = lax.axis_index("vel")
    own_speeds = lax.dynamic_slice_in_dim(courant, member * local_count, local_count, 0)[
        :, None, None
    ]
    field = distribution
    for step_index in range(STEPS):
        smoothed = advect(field, own_speeds)
        rounded = smoothed.astype(jnp.bfloat16)
        grouped = rounded.reshape(local_count, groups, -1)
        gained = lax.all_to_all(
            collide(
                lax.all_to_all(grouped, "vel", split_axis=1, concat_axis=0, tiled=True),
                gain_matrix,
                product_matrix,
            ),
            "vel",
            split_axis=0,
            concat_axis=1,
            tiled=True,
        )
        field = update(smoothed, rounded, gained.reshape(rounded.shape), collision_rate[None])
    return field


def solution(mesh):
    in_specs = (P("vel", "space", None), P(), P(), P(), P("space", None))
    out_specs = P("vel", "space", None)
    return jax.shard_map(body, mesh=mesh, in_specs=in_specs, out_specs=out_specs, check_vma=False)
```

profile of v0, /device:TPU:0, one launch (start us, length us, event | category | flops | bytes accessed | tf_op | source)
XLA Modules:
  0.0 399.8 jit_solution(6998099878804276208)
XLA Ops:
  0.0 5.4 %copy.28 = f32[128,16,512]{0,2,1:T(8,128)} copy(f32[128,16,512]{2,1,0:T(8,128)} %param.5) | data formatting | bytes 8388608 | tf_op args[0]
  13.5 12.2 %collective-permute-done = f32[128,2,512]{0,2,1:T(8,128)S(1)} collective-permute-done((f32[128,2,512]{0,2,1:T(8,128)}, f32[128,2,512]{0,2,1:T(8,128)S(1)}, u32[]{:S(2)}, u32[]{:S(2)}) %collective-permute-start) | collective-permute-done | bytes 524320 | tf_op jit(solution)/shard_map/ppermute | solution.py:18
  25.8 9.8 %collective-permute-done.1 = f32[128,2,512]{0,2,1:T(8,128)S(1)} collective-permute-done((f32[128,2,512]{0,2,1:T(8,128)}, f32[128,2,512]{0,2,1:T(8,128)S(1)}, u32[]{:S(2)}, u32[]{:S(2)}) %collective-permute-start.1) | collective-permute-done | bytes 524320 | tf_op jit(solution)/shard_map/ppermute | solution.py:21
  52.1 12.8 %collective-permute-done.2 = f32[128,2,512]{0,2,1:T(8,128)S(1)} collective-permute-done((f32[128,2,512]{0,2,1:T(8,128)S(1)}, f32[128,2,512]{0,2,1:T(8,128)S(1)}, u32[]{:S(2)}, u32[]{:S(2)}) %collective-permute-start.2) | collective-permute-done | bytes 524320 | tf_op jit(solution)/shard_map/ppermute | solution.py:18
  65.0 9.3 %collective-permute-done.3 = f32[128,2,512]{0,2,1:T(8,128)S(1)} collective-permute-done((f32[128,2,512]{0,2,1:T(8,128)S(1)}, f32[128,2,512]{0,2,1:T(8,128)S(1)}, u32[]{:S(2)}, u32[]{:S(2)}) %collective-permute-start.3) | collective-permute-done | bytes 524320 | tf_op jit(solution)/shard_map/ppermute | solution.py:21
  84.7 8.0 %fusion.36 = (bf16[128,16,512]{0,2,1:T(8,128)(2,1)S(1)}, f32[128,16,512]{0,2,1:T(8,128)}) fusion(f32[128,16,512]{0,2,1:T(8,128)S(1)} %copy-done.1, f32[128,16,512]{0,2,1:T(8,128)} %copy-done.3, f32[128,17,512]{0,2,1:T(8,128)} %fusion.12), kind=kLoop, calls=%fused_computation.75 | loop fusion | flops 6291456 | bytes 23068672 | tf_op jit(solution)/shard_map/convert_element_type | solution.py:78
  94.2 30.2 %all_to_all.48 = bf16[128,8,1024]{0,2,1:T(8,128)(2,1)} all-to-all(bf16[128,8,1024]{0,2,1:T(8,128)(2,1)S(1)} %bitcast.36), channel_id=1, replica_groups=mesh['vel'=8,'space'=4] {'vel'}, dimensions={1} | all-to-all | bytes 4194304 | tf_op jit(solution)/shard_map/all_to_all | solution.py:82
  145.3 6.3 %reshape.53 = bf16[8,2,65536]{2,1,0:T(2,128)(2,1)} reshape(bf16[1024,1024]{1,0:T(8,128)(2,1)} %copy.36) | data formatting | bytes 4194304
  151.6 30.9 %all_to_all.49 = bf16[8,2,65536]{2,1,0:T(2,128)(2,1)} all-to-all(bf16[8,2,65536]{2,1,0:T(2,128)(2,1)} %reshape.53), channel_id=1, replica_groups=mesh['vel'=8,'space'=4] {'vel'}, dimensions={0} | all-to-all | bytes 4194304 | tf_op jit(solution)/shard_map/all_to_all | solution.py:80
  182.5 6.8 %reshape.54 = bf16[1024,1,1024]{2,1,0:T(2,128)(2,1)} reshape(bf16[8,2,65536]{2,1,0:T(2,128)(2,1)} %all_to_all.49) | data formatting | bytes 4194304
  189.3 11.1 %copy.31 = f32[8,128,1,1024]{1,3,0,2:T(8,128)} copy(bf16[8,128,1,1024]{3,2,1,0:T(2,128)(2,1)} %bitcast.40) | data formatting | bytes 6291456 | tf_op jit(solution)/shard_map/convert_element_type | solution.py:65
  200.4 4.6 %multiply_add_fusion.1 = f32[128,16,512]{0,2,1:T(8,128)S(1)} fusion(f32[128,16,512]{0,2,1:T(8,128)} %get-tuple-element.8, f32[128,16,512]{0,2,1:T(8,128)} %bitcast.38, bf16[128,16,512]{0,2,1:T(8,128)(2,1)} %copy-done.4, f32[16,512]{1,0:T(8,128)S(1)} %copy-done.8), kind=kLoop, calls=%fused_computation.66 | loop fusion | flops 5242880 | bytes 14712832 | tf_op jit(solution)/shard_map/add | solution.py:65
  209.0 12.8 %collective-permute-done.4 = f32[128,2,512]{0,2,1:T(8,128)S(1)} collective-permute-done((f32[128,2,512]{0,2,1:T(8,128)S(1)}, f32[128,2,512]{0,2,1:T(8,128)S(1)}, u32[]{:S(2)}, u32[]{:S(2)}) %collective-permute-start.4) | collective-permute-done | bytes 524320 | tf_op jit(solution)/shard_map/ppermute | solution.py:18
  221.8 7.7 %collective-permute-done.5 = f32[128,2,512]{0,2,1:T(8,128)S(1)} collective-permute-done((f32[128,2,512]{0,2,1:T(8,128)S(1)}, f32[128,2,512]{0,2,1:T(8,128)S(1)}, u32[]{:S(2)}, u32[]{:S(2)}) %collective-permute-start.5) | collective-permute-done | bytes 524320 | tf_op jit(solution)/shard_map/ppermute | solution.py:21
  242.4 12.8 %collective-permute-done.6 = f32[128,2,512]{0,2,1:T(8,128)S(1)} collective-permute-done((f32[128,2,512]{0,2,1:T(8,128)S(1)}, f32[128,2,512]{0,2,1:T(8,128)S(1)}, u32[]{:S(2)}, u32[]{:S(2)}) %collective-permute-start.6) | collective-permute-done | bytes 524320 | tf_op jit(solution)/shard_map/ppermute | solution.py:18
  255.2 8.1 %collective-permute-done.7 = f32[128,2,512]{0,2,1:T(8,128)S(1)} collective-permute-done((f32[128,2,512]{0,2,1:T(8,128)S(1)}, f32[128,2,512]{0,2,1:T(8,128)S(1)}, u32[]{:S(2)}, u32[]{:S(2)}) %collective-permute-start.7) | collective-permute-done | bytes 524320 | tf_op jit(solution)/shard_map/ppermute | solution.py:21
  273.9 8.0 %fusion.34 = (bf16[128,16,512]{0,2,1:T(8,128)(2,1)S(1)}, f32[128,16,512]{0,2,1:T(8,128)}) fusion(f32[128,16,512]{0,2,1:T(8,128)S(1)} %multiply_add_fusion.1, f32[128,16,512]{0,2,1:T(8,128)} %copy-done.2, f32[128,17,512]{0,2,1:T(8,128)} %fusion.2), kind=kLoop, calls=%fused_computation.74 | loop fusion | flops 6291456 | bytes 23068672 | tf_op jit(solution)/shard_map/convert_element_type | solution.py:78
  283.3 29.7 %all_to_all.50 = bf16[128,8,1024]{0,2,1:T(8,128)(2,1)} all-to-all(bf16[128,8,1024]{0,2,1:T(8,128)(2,1)S(1)} %bitcast.37), channel_id=1, replica_groups=mesh['vel'=8,'space'=4] {'vel'}, dimensions={1} | all-to-all | bytes 4194304 | tf_op jit(solution)/shard_map/all_to_all | solution.py:82
  333.3 6.3 %reshape.55 = bf16[8,2,65536]{2,1,0:T(2,128)(2,1)} reshape(bf16[1024,1024]{1,0:T(8,128)(2,1)} %copy.37) | data formatting | bytes 4194304
  339.6 30.9 %all_to_all.51 = bf16[8,2,65536]{2,1,0:T(2,128)(2,1)} all-to-all(bf16[8,2,65536]{2,1,0:T(2,128)(2,1)} %reshape.55), channel_id=1, replica_groups=mesh['vel'=8,'space'=4] {'vel'}, dimensions={0} | all-to-all | bytes 4194304 | tf_op jit(solution)/shard_map/all_to_all | solution.py:80
  370.5 6.8 %reshape.56 = bf16[1024,1,1024]{2,1,0:T(2,128)(2,1)} reshape(bf16[8,2,65536]{2,1,0:T(2,128)(2,1)} %all_to_all.51) | data formatting | bytes 4194304
  377.3 11.0 %copy.34 = f32[8,128,1,1024]{1,3,0,2:T(8,128)} copy(bf16[8,128,1,1024]{3,2,1,0:T(2,128)(2,1)} %bitcast.41) | data formatting | bytes 6291456 | tf_op jit(solution)/shard_map/convert_element_type | solution.py:65
  388.4 6.0 %multiply_add_fusion = f32[128,16,512]{0,2,1:T(8,128)} fusion(f32[128,16,512]{0,2,1:T(8,128)} %get-tuple-element.6, f32[128,16,512]{0,2,1:T(8,128)} %bitcast.39, bf16[128,16,512]{0,2,1:T(8,128)(2,1)} %copy-done.5, f32[16,512]{1,0:T(8,128)S(1)} %copy-done.8), kind=kLoop, calls=%fused_computation.64 | loop fusion | flops 5242880 | bytes 14712832 | tf_op jit(solution)/shard_map/add | solution.py:65
  394.3 5.4 %copy.35 = f32[128,16,512]{2,1,0:T(8,128)} copy(f32[128,16,512]{0,2,1:T(8,128)} %multiply_add_fusion) | data formatting | bytes 8388608 | tf_op jit(solution)/shard_map/add | solution.py:65
  (65 shorter events, 106.4 us)
Async XLA Ops:
  0.0 128.3 %copy-start = (bf16[1024,1024]{1,0:T(8,128)(2,1)S(1)}, bf16[1024,1024]{1,0:T(8,128)(2,1)}, u32[]{:S(2)}) copy-start(bf16[1024,1024]{1,0:T(8,128)(2,1)} %param.7) | copy-start | bytes 6291460
  7.7 18.1 %collective-permute-start = (f32[128,2,512]{0,2,1:T(8,128)}, f32[128,2,512]{0,2,1:T(8,128)S(1)}, u32[]{:S(2)}, u32[]{:S(2)}) collective-permute-start(f32[128,2,512]{0,2,1:T(8,128)} %get-tuple-element.17), channel_id=1, source_target_pairs={{0,1},{1,2},{2,3},{3,0},{4,5},{5,6},{6,7},{7,4},{8,9},{9,10},{10,1... | collective-permute-start | bytes 1572872 | tf_op jit(solution)/shard_map/ppermute | solution.py:18
  10.7 24.8 %collective-permute-start.1 = (f32[128,2,512]{0,2,1:T(8,128)}, f32[128,2,512]{0,2,1:T(8,128)S(1)}, u32[]{:S(2)}, u32[]{:S(2)}) collective-permute-start(f32[128,2,512]{0,2,1:T(8,128)} %get-tuple-element.18), channel_id=1, source_target_pairs={{1,0},{2,1},{3,2},{0,3},{5,4},{6,5},{7,6},{4,7},{9,8},{10,9},{11,1... | collective-permute-start | bytes 1572872 | tf_op jit(solution)/shard_map/ppermute | solution.py:21
  38.6 2.2 copy-start.1
  48.2 33.6 %copy-start.3 = (f32[128,16,512]{0,2,1:T(8,128)}, f32[128,16,512]{0,2,1:T(8,128)S(1)}, u32[]{:S(2)}) copy-start(f32[128,16,512]{0,2,1:T(8,128)S(1)} %fusion.31) | copy-start | bytes 12582916
  48.2 16.7 %collective-permute-start.2 = (f32[128,2,512]{0,2,1:T(8,128)S(1)}, f32[128,2,512]{0,2,1:T(8,128)S(1)}, u32[]{:S(2)}, u32[]{:S(2)}) collective-permute-start(f32[128,2,512]{0,2,1:T(8,128)S(1)} %get-tuple-element.15), channel_id=1, source_target_pairs={{0,1},{1,2},{2,3},{3,0},{4,5},{5,6},{6,7},{7,4},{8,9},{9,10},{10,1... | collective-permute-start | bytes 1572872 | tf_op jit(solution)/shard_map/ppermute | solution.py:18
  49.4 24.8 %collective-permute-start.3 = (f32[128,2,512]{0,2,1:T(8,128)S(1)}, f32[128,2,512]{0,2,1:T(8,128)S(1)}, u32[]{:S(2)}, u32[]{:S(2)}) collective-permute-start(f32[128,2,512]{0,2,1:T(8,128)S(1)} %get-tuple-element.16), channel_id=1, source_target_pairs={{1,0},{2,1},{3,2},{0,3},{5,4},{6,5},{7,6},{4,7},{9,8},{10,9},{11,1... | collective-permute-start | bytes 1572872 | tf_op jit(solution)/shard_map/ppermute | solution.py:21
  92.8 1.4 copy-start.4
  128.3 4.1 %copy-start.6 = (bf16[8,128,1,1024]{3,1,0,2:T(8,128)(2,1)S(1)}, bf16[8,128,1,1024]{3,1,0,2:T(8,128)(2,1)}, u32[]{:S(2)}) copy-start(bf16[8,128,1,1024]{3,1,0,2:T(8,128)(2,1)} %copy.29) | copy-start | bytes 6291460
  128.3 4.1 %copy-start.9 = (bf16[1024,1024]{1,0:T(8,128)(2,1)S(1)}, bf16[1024,1024]{1,0:T(8,128)(2,1)}, u32[]{:S(2)}) copy-start(bf16[1024,1024]{1,0:T(8,128)(2,1)} %param.8) | copy-start | bytes 6291460
  189.3 11.1 %copy-start.8 = (f32[16,512]{1,0:T(8,128)S(1)}, f32[16,512]{1,0:T(8,128)}, u32[]{:S(2)}) copy-start(f32[16,512]{1,0:T(8,128)} %param.9) | copy-start | bytes 98308
  205.1 16.7 %collective-permute-start.4 = (f32[128,2,512]{0,2,1:T(8,128)S(1)}, f32[128,2,512]{0,2,1:T(8,128)S(1)}, u32[]{:S(2)}, u32[]{:S(2)}) collective-permute-start(f32[128,2,512]{0,2,1:T(8,128)S(1)} %get-tuple-element.13), channel_id=1, source_target_pairs={{0,1},{1,2},{2,3},{3,0},{4,5},{5,6},{6,7},{7,4},{8,9},{9,10},{10,1... | collective-permute-start | bytes 1572872 | tf_op jit(solution)/shard_map/ppermute | solution.py:18
  205.5 24.0 %collective-permute-start.5 = (f32[128,2,512]{0,2,1:T(8,128)S(1)}, f32[128,2,512]{0,2,1:T(8,128)S(1)}, u32[]{:S(2)}, u32[]{:S(2)}) collective-permute-start(f32[128,2,512]{0,2,1:T(8,128)S(1)} %get-tuple-element.14), channel_id=1, source_target_pairs={{1,0},{2,1},{3,2},{0,3},{5,4},{6,5},{7,6},{4,7},{9,8},{10,9},{11,1... | collective-permute-start | bytes 1572872 | tf_op jit(solution)/shard_map/ppermute | solution.py:21
  238.4 32.5 %copy-start.2 = (f32[128,16,512]{0,2,1:T(8,128)}, f32[128,16,512]{0,2,1:T(8,128)S(1)}, u32[]{:S(2)}) copy-start(f32[128,16,512]{0,2,1:T(8,128)S(1)} %fusion.25) | copy-start | bytes 12582916
  238.5 16.7 %collective-permute-start.6 = (f32[128,2,512]{0,2,1:T(8,128)S(1)}, f32[128,2,512]{0,2,1:T(8,128)S(1)}, u32[]{:S(2)}, u32[]{:S(2)}) collective-permute-start(f32[128,2,512]{0,2,1:T(8,128)S(1)} %get-tuple-element.11), channel_id=1, source_target_pairs={{0,1},{1,2},{2,3},{3,0},{4,5},{5,6},{6,7},{7,4},{8,9},{9,10},{10,1... | collective-permute-start | bytes 1572872 | tf_op jit(solution)/shard_map/ppermute | solution.py:18
  239.7 23.6 %collective-permute-start.7 = (f32[128,2,512]{0,2,1:T(8,128)S(1)}, f32[128,2,512]{0,2,1:T(8,128)S(1)}, u32[]{:S(2)}, u32[]{:S(2)}) collective-permute-start(f32[128,2,512]{0,2,1:T(8,128)S(1)} %get-tuple-element.12), channel_id=1, source_target_pairs={{1,0},{2,1},{3,2},{0,3},{5,4},{6,5},{7,6},{4,7},{9,8},{10,9},{11,1... | collective-permute-start | bytes 1572872 | tf_op jit(solution)/shard_map/ppermute | solution.py:21
  281.9 1.4 copy-start.5
  317.0 4.1 %copy-start.7 = (bf16[8,128,1,1024]{3,1,0,2:T(8,128)(2,1)S(1)}, bf16[8,128,1,1024]{3,1,0,2:T(8,128)(2,1)}, u32[]{:S(2)}) copy-start(bf16[8,128,1,1024]{3,1,0,2:T(8,128)(2,1)} %copy.32) | copy-start | bytes 6291460
  317.0 4.1 %copy-start.10 = (bf16[1024,1024]{1,0:T(8,128)(2,1)S(1)}, bf16[1024,1024]{1,0:T(8,128)(2,1)}, u32[]{:S(2)}) copy-start(bf16[1024,1024]{1,0:T(8,128)(2,1)} %param.8) | copy-start | bytes 6291460
where the time goes:
time: 402 us; the launch traced here: 400 us
  blocking collectives  122 us (30%)
  waiting for transfers between devices  85.6 us (21%)
  local copies, waits for them, and re-layouts  82 us (20%)
  other arithmetic  77.7 us (19%)
  starting transfers between devices  16.7 us (4%)
  matrix products  15.7 us (4%)
    all_to_all x2, blocking collectives, body(): lax.all_to_all(collide(lax.all_to_all(grouped, 'vel', split_axis=1, conca...  61.9 us
    all_to_all x2, blocking collectives, body(): lax.all_to_all(grouped, 'vel', split_axis=1, concat_axis=0, tiled=True)  60 us
    ppermute x4, waiting for transfers between devices, with_halo(): lax.ppermute(lax.slice_in_dim(block, block.shape[dim] - width, None, axis...  50.8 us
    unnamed x29, local copies, waits for them, and re-layouts  43.7 us
    ppermute x4, waiting for transfers between devices, with_halo(): lax.ppermute(lax.slice_in_dim(block, 0, width, axis=dim), axis, backward)  34.8 us
    convert_element_type x2, local copies, waits for them, and re-layouts, update(): gained.astype(jnp.float32) - rate * rounded.astype(jnp.float32)  22.1 us
    convert_element_type x2, other arithmetic, body(): rounded = smoothed.astype(jnp.bfloat16)  16.1 us
    add x4, other arithmetic, change(): upward * (left_value + 0.5 * (1.0 - speeds) * left_slope)  12.1 us
  transfers between devices with their start and end apart: 8, of which 8 were waited for; matrix products, arithmetic and copies ran while one was open for 0% of the time, Pallas kernels for 0%

commit v1 on v0

--- a/solution.py
+++ b/solution.py
@@ -1,10 +1,18 @@
+import functools
+
 import jax
 import jax.numpy as jnp
 from jax import lax
+from jax.experimental import pallas as pl
+from jax.experimental.pallas import tpu as pltpu
 from jax.sharding import PartitionSpec as P
 
 STEPS = 2
-
+HALO = 4
+HEAD = 8
+CHUNKS = 2
+LANES = 128
+VMEM = 48 * 1024 * 1024
 
 time_step = 0.2
 
@@ -65,7 +73,7 @@
     return smoothed + time_step * (gained.astype(jnp.float32) - rate * rounded.astype(jnp.float32))
 
 
-def body(distribution, courant, gain_matrix, product_matrix, collision_rate):
+def general_body(distribution, courant, gain_matrix, product_matrix, collision_rate):
     local_count = distribution.shape[0]
     groups = lax.axis_size("vel")
     member = lax.axis_index("vel")
@@ -92,7 +100,460 @@
     return field
 
 
+def params(count=1):
+    return pltpu.CompilerParams(
+        dimension_semantics=("arbitrary",) * count, vmem_limit_bytes=VMEM
+    )
+
+
+def cost(flops, moved):
+    return pl.CostEstimate(flops=int(flops), bytes_accessed=int(moved), transcendentals=0)
+
+
+def exponent_of(largest):
+    power = jnp.floor(14.0 - jnp.log2(jnp.maximum(largest, 1e-36)))
+    return jnp.clip(power, -115.0, 120.0)
+
+
+def pack_kernel(order, planes, cells, chip_ref, d_ref, *refs):
+    outs, scratch = refs[:-1], refs[-1]
+    chip = chip_ref[0]
+    step = pl.program_id(0)
+    rows = d_ref.reshape(LANES * planes, LANES)
+    for x in range(planes):
+        part = rows[pl.ds(x, LANES, stride=planes), :]
+        scratch[x, pl.ds(pl.multiple_of(step * LANES, LANES), LANES), :] = part.T
+
+    @pl.when(step == pl.num_programs(0) - 1)
+    def _():
+        for mask, out in zip(order, outs):
+            first = pl.multiple_of((chip ^ mask) * cells, cells)
+
+            def peak(x, carry):
+                return jnp.maximum(carry, jnp.abs(scratch[x, pl.ds(first, cells), :]))
+
+            top = lax.fori_loop(0, planes, peak, jnp.zeros((cells, LANES), jnp.float32))
+            power = exponent_of(jnp.max(top, axis=0, keepdims=True))
+            scale = jnp.exp2(power)
+
+            def write(x, carry):
+                out[pl.ds(pl.multiple_of(x * cells, cells), cells), :] = (
+                    scratch[x, pl.ds(first, cells), :] * scale
+                )
+                return carry
+
+            lax.fori_loop(0, planes, write, 0)
+            out[planes * cells :, :] = jnp.broadcast_to(power, (HEAD, LANES))
+
+
+def pack(distribution, chip, order, chunk, cells):
+    planes = distribution.shape[1]
+    width = cells * len(order)
+    steps = width // LANES
+    shape = (planes * cells + HEAD, LANES)
+    return pl.pallas_call(
+        functools.partial(pack_kernel, order, planes, cells),
+        grid_spec=pltpu.PrefetchScalarGridSpec(
+            num_scalar_prefetch=1,
+            grid=(steps,),
+            in_specs=[
+                pl.BlockSpec((LANES, planes, LANES), lambda i, s: (0, 0, chunk * steps + i))
+            ],
+            out_specs=[pl.BlockSpec(shape, lambda i, s: (0, 0)) for _ in order],
+            scratch_shapes=[pltpu.VMEM((planes, width, LANES), jnp.float32)],
+        ),
+        out_shape=[jax.ShapeDtypeStruct(shape, jnp.float32) for _ in order],
+        compiler_params=params(),
+        cost_estimate=cost(1e6, 8 * LANES * planes * width),
+        name="pack",
+    )(chip, distribution)
+
+
+def stage(values, speed, bend, positive):
+    differ = [b - a for a, b in zip(values[:-1], values[1:])]
+    slopes = [
+        jnp.maximum(jnp.minimum(a, b), jnp.minimum(jnp.maximum(a, b), 0.0))
+        for a, b in zip(differ[:-1], differ[1:])
+    ]
+    inner = [speed * u + bend * s for u, s in zip(values[1:-1], slopes)]
+    faces = [jnp.where(positive, a, b) for a, b in zip(inner[:-1], inner[1:])]
+    return [u - (b - a) for u, a, b in zip(values[2:-2], faces[:-1], faces[1:])]
+
+
+def advect_kernel(planes, cells, tile, scaled, c_ref, low_ref, high_ref, *refs):
+    bodies, smoothed_ref, rounded_ref = refs[:-2], refs[-2], refs[-1]
+    speed = c_ref[0:1, :]
+    size = jnp.abs(speed)
+    bend = 0.5 * size * (1.0 - size)
+    positive = jnp.broadcast_to(speed, (tile, LANES)) > 0.0
+
+    def back(ref):
+        return jnp.exp2(-ref[HALO * cells : HALO * cells + 1, :])
+
+    back_low, back_high = back(low_ref), back(high_ref)
+    if scaled:
+        back_body = jnp.exp2(-bodies[0][planes * cells : planes * cells + 1, :])
+
+    def at(ref, x, t):
+        return ref[pl.ds(pl.multiple_of(x * cells + t * tile, tile), tile), :]
+
+    def body(t, carry):
+        values = [at(low_ref, x, t) * back_low for x in range(HALO)]
+        if scaled:
+            values += [at(bodies[0], x, t) * back_body for x in range(planes)]
+        else:
+            low, middle, high = bodies
+            values += [at(low, x, t) for x in range(HALO)]
+            values += [at(middle, x, t) for x in range(planes - 2 * HALO)]
+            values += [at(high, x, t) for x in range(HALO)]
+        values += [at(high_ref, x, t) * back_high for x in range(HALO)]
+        section = stage(values, speed, bend, positive)
+        moved = stage(section, speed, bend, positive)
+        for x in range(planes):
+            result = 0.5 * values[x + HALO] + 0.5 * moved[x]
+            where = pl.ds(pl.multiple_of(x * cells + t * tile, tile), tile)
+            smoothed_ref[where, :] = result
+            rounded_ref[where, :] = result.astype(jnp.bfloat16)
+        return carry
+
+    lax.fori_loop(0, cells // tile, body, 0)
+
+
+def transport(speeds, low, high, bodies, planes, cells, scaled):
+    rows, width = planes * cells, low.shape[1]
+
+    def spec(a):
+        return pl.BlockSpec((a.shape[0], LANES), lambda j: (0, j))
+
+    return pl.pallas_call(
+        functools.partial(advect_kernel, planes, cells, 16, scaled),
+        grid=(width // LANES,),
+        in_specs=[spec(a) for a in (speeds, low, high, *bodies)],
+        out_specs=[pl.BlockSpec((rows, LANES), lambda j: (0, j))] * 2,
+        out_shape=[
+            jax.ShapeDtypeStruct((rows, width), jnp.float32),
+            jax.ShapeDtypeStruct((rows, width), jnp.bfloat16),
+        ],
+        compiler_params=params(),
+        cost_estimate=cost(40 * rows * width, 12 * rows * width),
+        name="transport",
+    )(speeds, low, high, *bodies)
+
+
+def gains(own, other, matrix_ref, columns):
+    half = own.shape[1]
+    dims = (((1,), (1,)), ((), ()))
+    return lax.dot_general(
+        own, matrix_ref[columns, :half], dims, preferred_element_type=jnp.float32
+    ) + lax.dot_general(
+        other, matrix_ref[columns, half:], dims, preferred_element_type=jnp.float32
+    )
+
+
+def collided(own_ref, other_ref, smoothed, rounded, rate_ref, gain_ref, product_ref, columns):
+    own, other = own_ref[...], other_ref[...]
+    gained = gains(own, other, gain_ref, columns) * gains(own, other, product_ref, columns)
+    gained = gained.astype(jnp.bfloat16).astype(jnp.float32)
+    rate = rate_ref[...]
+    rate = jnp.concatenate([rate] * (rounded.shape[1] // LANES), axis=1)
+    return smoothed + time_step * (gained - rate * rounded.astype(jnp.float32))
+
+
+def faces_kernel(own_ref, other_ref, smoothed_ref, rate_ref, gain_ref, product_ref, state_ref, message_ref):
+    rows, width = own_ref.shape
+    group = 2 * LANES
+    for start in range(0, width, group):
+        columns = slice(start, start + group)
+        state = collided(
+            own_ref, other_ref, smoothed_ref[:, columns], own_ref[:, columns], rate_ref,
+            gain_ref, product_ref, columns,
+        )
+        state_ref[0, :, columns] = state
+        power = exponent_of(jnp.max(jnp.abs(state), axis=0, keepdims=True))
+        message_ref[0, :rows, columns] = state * jnp.exp2(power)
+        message_ref[0, rows:, columns] = jnp.broadcast_to(power, (HEAD, group))
+
+
+def faces(own, other, smoothed, rate, gain, product, planes, cells):
+    rows, width = HALO * cells, own.shape[1]
+    last = planes // HALO - 1
+    block = pl.BlockSpec((rows, width), lambda i: (i * last, 0))
+    whole = pl.BlockSpec(gain.shape, lambda i: (0, 0))
+    return pl.pallas_call(
+        faces_kernel,
+        grid=(2,),
+        in_specs=[block, block, block, pl.BlockSpec((rows, LANES), lambda i: (i * last, 0)), whole, whole],
+        out_specs=[
+            pl.BlockSpec((1, rows, width), lambda i: (i, 0, 0)),
+            pl.BlockSpec((1, rows + HEAD, width), lambda i: (i, 0, 0)),
+        ],
+        out_shape=[
+            jax.ShapeDtypeStruct((2, rows, width), jnp.float32),
+            jax.ShapeDtypeStruct((2, rows + HEAD, width), jnp.float32),
+        ],
+        compiler_params=params(),
+        cost_estimate=cost(16 * rows * width * width, 30 * rows * width),
+        name="faces",
+    )(own, other, smoothed, rate, gain, product)
+
+
+def inside_kernel(own_ref, other_ref, smoothed_ref, rate_ref, gain_ref, product_ref, state_ref):
+    width = own_ref.shape[1]
+    group = 2 * LANES
+    for start in range(0, width, group):
+        columns = slice(start, start + group)
+        state_ref[:, columns] = collided(
+            own_ref, other_ref, smoothed_ref[:, columns], own_ref[:, columns], rate_ref,
+            gain_ref, product_ref, columns,
+        )
+
+
+def inside(own, other, smoothed, rate, gain, product, planes, cells):
+    rows, width = HALO * cells, own.shape[1]
+    count = planes // HALO - 2
+    block = pl.BlockSpec((rows, width), lambda i: (i + 1, 0))
+    whole = pl.BlockSpec(gain.shape, lambda i: (0, 0))
+    return pl.pallas_call(
+        inside_kernel,
+        grid=(count,),
+        in_specs=[block, block, block, pl.BlockSpec((rows, LANES), lambda i: (i + 1, 0)), whole, whole],
+        out_specs=pl.BlockSpec((rows, width), lambda i: (i, 0)),
+        out_shape=jax.ShapeDtypeStruct((count * rows, width), jnp.float32),
+        compiler_params=params(),
+        cost_estimate=cost(8 * count * rows * width * width, 20 * count * rows * width),
+        name="inside",
+    )(own, other, smoothed, rate, gain, product)
+
+
+def final_kernel(blocks, own_ref, other_ref, rounded_ref, smoothed_ref, rate_ref, gain_ref, product_ref, *refs):
+    outs, scratch = refs[:-1], refs[-1]
+    step = pl.program_id(0)
+    rows, group = smoothed_ref.shape
+    state = collided(
+        own_ref, other_ref, smoothed_ref[...], rounded_ref[...], rate_ref,
+        gain_ref, product_ref, slice(0, group),
+    )
+    scratch[pl.ds(pl.multiple_of(step * rows, rows), rows), :] = state
+
+    @pl.when(step == blocks - 1)
+    def _():
+        for index, out in enumerate(outs):
+            columns = slice(index * LANES, (index + 1) * LANES)
+
+            def peak(i, carry):
+                return jnp.maximum(
+                    carry, jnp.abs(scratch[pl.ds(pl.multiple_of(i * LANES, LANES), LANES), columns])
+                )
+
+            top = lax.fori_loop(0, blocks * rows // LANES, peak, jnp.zeros((LANES, LANES), jnp.float32))
+            power = exponent_of(jnp.max(top, axis=0, keepdims=True))
+            scale = jnp.exp2(power)
+
+            def write(i, carry):
+                where = pl.ds(pl.multiple_of(i * LANES, LANES), LANES)
+                out[where, :] = scratch[where, columns] * scale
+                return carry
+
+            lax.fori_loop(0, blocks * rows // LANES, write, 0)
+            out[blocks * rows :, :] = jnp.broadcast_to(power, (HEAD, LANES))
+
+
+def final(own, other, smoothed, rate, gain, product, planes, cells, part):
+    rows, width = HALO * cells, own.shape[1]
+    blocks = planes // HALO
+    group = 2 * LANES
+    block = pl.BlockSpec((rows, width), lambda i: (i, 0))
+    narrow = pl.BlockSpec((rows, group), lambda i: (i, part))
+    matrix = pl.BlockSpec((group, gain.shape[1]), lambda i: (part, 0))
+    shape = (blocks * rows + HEAD, LANES)
+    return pl.pallas_call(
+        functools.partial(final_kernel, blocks),
+        grid=(blocks,),
+        in_specs=[block, block, narrow, narrow, pl.BlockSpec((rows, LANES), lambda i: (i, 0)), matrix, matrix],
+        out_specs=[pl.BlockSpec(shape, lambda i: (0, 0))] * 2,
+        out_shape=[jax.ShapeDtypeStruct(shape, jnp.float32)] * 2,
+        scratch_shapes=[pltpu.VMEM((blocks * rows, group), jnp.float32)],
+        compiler_params=params(),
+        cost_estimate=cost(8 * blocks * rows * width * group, 20 * blocks * rows * group),
+        name="final",
+    )(own, other, own, smoothed, rate, gain, product)
+
+
+def unpack_kernel(order, planes, cells, chip_ref, *refs):
+    count = len(order)
+    pieces, out, scratch = refs[:count], refs[-2], refs[-1]
+    chip = chip_ref[0]
+    step = pl.program_id(0)
+    flat = out.reshape(LANES * planes, LANES)
+
+    @pl.when(step == 0)
+    def _():
+        for mask, piece in zip(order, pieces):
+            first = pl.multiple_of((chip ^ mask) * cells, cells)
+            scale = jnp.exp2(-piece[planes * cells : planes * cells + 1, :])
+
+            def place(x, carry):
+                scratch[x, pl.ds(first, cells), :] = (
+                    piece[pl.ds(pl.multiple_of(x * cells, cells), cells), :] * scale
+                )
+                return carry
+
+            lax.fori_loop(0, planes, place, 0)
+
+    for x in range(planes):
+        part = scratch[x, pl.ds(pl.multiple_of(step * LANES, LANES), LANES), :]
+        flat[pl.ds(x, LANES, stride=planes), :] = part.T
+
+
+def unpack(pieces, target, chip, order, chunk, planes, cells):
+    width = cells * len(order)
+    steps = width // LANES
+    shape = (LANES, planes, width * CHUNKS)
+    specs = [pl.BlockSpec(p.shape, lambda i, s: (0, 0)) for p in pieces]
+    operands = list(pieces)
+    aliases = {}
+    if target is not None:
+        specs.append(pl.BlockSpec(memory_space=pl.ANY))
+        operands.append(target)
+        aliases = {len(operands): 0}
+    return pl.pallas_call(
+        functools.partial(unpack_kernel, order, planes, cells),
+        grid_spec=pltpu.PrefetchScalarGridSpec(
+            num_scalar_prefetch=1,
+            grid=(steps,),
+            in_specs=specs,
+            out_specs=pl.BlockSpec((LANES, planes, LANES), lambda i, s: (0, 0, chunk * steps + i)),
+            scratch_shapes=[pltpu.VMEM((planes, width, LANES), jnp.float32)],
+        ),
+        out_shape=jax.ShapeDtypeStruct(shape, jnp.float32),
+        input_output_aliases=aliases,
+        compiler_params=params(),
+        cost_estimate=cost(1e6, 8 * LANES * planes * width),
+        name="unpack",
+    )(chip, *operands)
+
+
+def exchange(array, mask):
+    count = lax.axis_size("vel")
+    return lax.ppermute(array, "vel", [(i, i ^ mask) for i in range(count)])
+
+
+def shift(array, step):
+    count = lax.axis_size("space")
+    return lax.ppermute(array, "space", [(i, (i + step) % count) for i in range(count)])
+
+
+def half(array):
+    return array.astype(jnp.float16)
+
+
+def full(array):
+    return array.astype(jnp.float32)
+
+
+def first_faces(pieces, cells, planes):
+    body = HALO * cells
+    top = planes * cells
+
+    def message(start):
+        return jnp.concatenate(
+            [jnp.concatenate([p[start : start + body], p[top:]], axis=0) for p in pieces], axis=1
+        )
+
+    return message(top - body), message(0)
+
+
+def body(distribution, courant, gain_matrix, product_matrix, collision_rate):
+    planes, plane = distribution.shape[1:]
+    chips = lax.axis_size("vel") // 2
+    member = lax.axis_index("vel")
+    chip, core = member // 2, member % 2
+    order = list(range(1, chips)) + [0]
+    cells = plane // (chips * CHUNKS)
+    span = cells * chips
+    chip_word = chip.astype(jnp.int32).reshape(1)
+
+    pieces = [pack(distribution, chip_word, order, k, cells) for k in range(CHUNKS)]
+    sent = [
+        [half(a) if mask == 0 else exchange(half(a), 2 * mask) for a, mask in zip(pieces[k], order)]
+        for k in range(CHUNKS)
+    ]
+
+    own_blocks = [2 * (chip ^ mask) + core for mask in order]
+    other_blocks = [2 * (chip ^ mask) + 1 - core for mask in order]
+
+    def arranged(matrix):
+        lines = jnp.concatenate(
+            [lax.dynamic_slice_in_dim(matrix, b * LANES, LANES, 0) for b in own_blocks], axis=0
+        )
+        return jnp.concatenate(
+            [lax.dynamic_slice_in_dim(lines, b * LANES, LANES, 1) for b in own_blocks + other_blocks],
+            axis=1,
+        )
+
+    gain, product = arranged(gain_matrix), arranged(product_matrix)
+    speeds = jnp.concatenate(
+        [lax.dynamic_slice_in_dim(courant, b * LANES, LANES, 0) for b in own_blocks]
+    )
+    speeds = jnp.broadcast_to(speeds[None], (8, speeds.shape[0]))
+    rates = []
+    for k in range(CHUNKS):
+        own = lax.dynamic_slice_in_dim(collision_rate, k * span + chip * cells, cells, 1)
+        rates.append(jnp.broadcast_to(own.reshape(planes * cells, 1), (planes * cells, LANES)))
+
+    result = None
+    states = []
+    for k in range(CHUNKS):
+        up, down = first_faces(sent[k], cells, planes)
+        low, high = full(shift(up, 1)), full(shift(down, -1))
+        local = jnp.concatenate(
+            [a if mask == 0 else full(b) for a, b, mask in zip(pieces[k], sent[k], order)], axis=1
+        )
+        smoothed, rounded = transport(speeds, low, high, [local], planes, cells, True)
+        other = exchange(rounded, 1)
+        ends, messages = faces(rounded, other, smoothed, rates[k], gain, product, planes, cells)
+        messages = half(messages)
+        low, high = full(shift(messages[1], 1)), full(shift(messages[0], -1))
+        middle = inside(rounded, other, smoothed, rates[k], gain, product, planes, cells)
+        states.append((low, high, [ends[0], middle, ends[1]]))
+    for k in range(CHUNKS):
+        low, high, parts = states[k]
+        smoothed, rounded = transport(speeds, low, high, parts, planes, cells, False)
+        other = exchange(rounded, 1)
+        ready = []
+        for part in range(chips // 2):
+            ready += final(rounded, other, smoothed, rates[k], gain, product, planes, cells, part)
+        back = [
+            a if mask == 0 else full(exchange(half(a), 2 * mask)) for a, mask in zip(ready, order)
+        ]
+        result = unpack(back, result, chip_word, order, k, planes, cells)
+    return result
+
+
+def fits(mesh, shape, spaces):
+    groups = mesh.shape["vel"]
+    local, planes = shape[0] // groups, shape[1] // spaces
+    chips = groups // 2
+    return (
+        groups % 4 == 0
+        and chips & (chips - 1) == 0
+        and local == LANES
+        and planes % HALO == 0
+        and planes >= 3 * HALO
+        and shape[2] % (CHUNKS * LANES) == 0
+        and shape[2] % (CHUNKS * chips * 16) == 0
+    )
+
+
 def solution(mesh):
     in_specs = (P("vel", "space", None), P(), P(), P(), P("space", None))
     out_specs = P("vel", "space", None)
-    return jax.shard_map(body, mesh=mesh, in_specs=in_specs, out_specs=out_specs, check_vma=False)
+
+    def run(distribution, courant, gain_matrix, product_matrix, collision_rate):
+        special = fits(mesh, distribution.shape, mesh.shape["space"])
+        return jax.shard_map(
+            body if special else general_body,
+            mesh=mesh, in_specs=in_specs, out_specs=out_specs, check_vma=False,
+        )(distribution, courant, gain_matrix, product_matrix, collision_rate)
+
+    return run

time: 402 us -> 155 us (0.39)
  blocking collectives: 122 us -> 0 us
  waiting for transfers between devices: 85.6 us -> 17.5 us
  other arithmetic: 77.7 us -> 19.7 us
  Pallas kernels: 0 us -> 55.5 us
  local copies, waits for them, and re-layouts: 82 us -> 28.5 us
  matrix products: 15.7 us -> 0 us
  starting transfers between devices: 16.7 us -> 31.3 us
    all_to_all x4 -> x0, blocking collectives: 122 us -> none  [the longest x2 61.9 us: body(): lax.all_to_all(collide(lax.all_to_all(grouped, 'vel', split_axis=1, conca...]
    ppermute x8 -> x24, waiting for transfers between devices: 85.6 us -> 17.5 us  [the longest x8 9.39 us: shift(): lax.ppermute(array, 'space', [(i, (i + step) % count) for i in range(coun...]
    pallas_call x0 -> x16, Pallas kernels: none -> 55.5 us  [the longest x4 17.4 us: transport(): pl.pallas_call(functools.partial(advect_kernel, planes, cells, 16, scaled...]
    add x12 -> x0, other arithmetic: 41.9 us -> none  [the longest x4 12.1 us: change(): upward * (left_value + 0.5 * (1.0 - speeds) * left_slope)]
    unnamed x29 -> x33, local copies, waits for them, and re-layouts: 43.7 us -> 10.6 us
    convert_element_type x2 -> x0, local copies, waits for them, and re-layouts: 22.1 us -> none  [update(): gained.astype(jnp.float32) - rate * rounded.astype(jnp.float32)]
    dot_general x4 -> x0, matrix products: 15.7 us -> none  [the longest x2 8.24 us: collide(): jnp.dot(gain_matrix, columns, preferred_element_type=jnp.float32)]
    ppermute x8 -> x24, starting transfers between devices: 16.7 us -> 31.3 us  [the longest x8 15.9 us: shift(): lax.ppermute(array, 'space', [(i, (i + step) % count) for i in range(coun...]
  transfers between devices with their start and end apart: 8 -> 24, of which waited for: 8 -> 5; matrix products, arithmetic and copies ran while one was open for 0% -> 28% of each run, Pallas kernels for 0% -> 33%
where the time goes in v1:
time: 155 us; the launch traced here: 153 us
  Pallas kernels  55.5 us (36%)
  starting transfers between devices  31.3 us (20%)
  local copies, waits for them, and re-layouts  28.5 us (18%)
  other arithmetic  19.7 us (13%)
  waiting for transfers between devices  17.5 us (11%)
    pallas_call x4, Pallas kernels, transport(): pl.pallas_call(functools.partial(advect_kernel, planes, cells, 16, scaled...  17.4 us
    ppermute x8, starting transfers between devices, shift(): lax.ppermute(array, 'space', [(i, (i + step) % count) for i in range(coun...  15.9 us
    ppermute x16, starting transfers between devices, exchange(): return lax.ppermute(array, 'vel', [(i, i ^ mask) for i in range(count)])  15.4 us
    pallas_call x4, Pallas kernels, final(): pl.pallas_call(functools.partial(final_kernel, blocks), grid=(blocks,), i...  15.1 us
    unnamed x33, local copies, waits for them, and re-layouts  10.6 us
    ppermute x8, waiting for transfers between devices, shift(): lax.ppermute(array, 'space', [(i, (i + step) % count) for i in range(coun...  9.39 us
    convert_element_type x16, other arithmetic, half(): return array.astype(jnp.float16)  8.47 us
    ppermute x16, waiting for transfers between devices, exchange(): return lax.ppermute(array, 'vel', [(i, i ^ mask) for i in range(count)])  8.09 us
  transfers between devices with their start and end apart: 24, of which 5 were waited for; matrix products, arithmetic and copies ran while one was open for 28% of the time, Pallas kernels for 33%

profile of v1, /device:TPU:0, one launch (start us, length us, event | category | flops | bytes accessed | tf_op | source)
XLA Modules:
  0.0 153.2 jit_solution(685065755995296433)
XLA Ops:
  0.0 3.0 %pack.2 = (f32[1032,128]{1,0:T(8,128)S(1)}, f32[1032,128]{1,0:T(8,128)S(1)}, f32[1032,128]{1,0:T(8,128)S(1)}, f32[1032,128]{1,0:T(8,128)S(1)}) custom-call(s32[1]{0:T(128)} %bitcast.chip_ref, f32[128,16,512]{2,1,0:T(8,128)} %d_ref.3), custom_call_target="tpu_custom_call" | custom-call | flops 1000000 | bytes 4194304 | tf_op jit(solution)/shard_map/pack/pallas_call | solution.py:154
  3.7 3.9 %collective-permute-start.2 = (f16[1032,128]{1,0:T(8,128)(2,1)}, f16[1032,128]{1,0:T(8,128)(2,1)}, u32[]{:S(2)}, u32[]{:S(2)}) collective-permute-start(f16[1032,128]{1,0:T(8,128)(2,1)} %convert_element_type.110), channel_id=1, source_target_pairs={{0,24},{4,28},{8,16},{12,20},{16,8},{20,12},{24,0},{28,4},{1,25},{... | collective-permute-start | bytes 792584 | tf_op jit(solution)/shard_map/ppermute | solution.py:438
  9.7 3.0 %pack.3 = (f32[1032,128]{1,0:T(8,128)S(1)}, f32[1032,128]{1,0:T(8,128)S(1)}, f32[1032,128]{1,0:T(8,128)S(1)}, f32[1032,128]{1,0:T(8,128)S(1)}) custom-call(s32[1]{0:T(128)} %bitcast.chip_ref, f32[128,16,512]{2,1,0:T(8,128)} %d_ref.3), custom_call_target="tpu_custom_call" | custom-call | flops 1000000 | bytes 4194304 | tf_op jit(solution)/shard_map/pack/pallas_call | solution.py:154
  14.1 2.9 %collective-permute-start.14 = (f16[1032,128]{1,0:T(8,128)(2,1)}, f16[1032,128]{1,0:T(8,128)(2,1)S(1)}, u32[]{:S(2)}, u32[]{:S(2)}) collective-permute-start(f16[1032,128]{1,0:T(8,128)(2,1)} %convert_element_type.128), channel_id=1, source_target_pairs={{0,24},{4,28},{8,16},{12,20},{16,8},{20,12},{24,0},{28,4},{1,25},{... | collective-permute-start | bytes 792584 | tf_op jit(solution)/shard_map/ppermute | solution.py:438
  45.1 4.6 %transport.4 = (f32[1024,512]{1,0:T(8,128)S(1)}, bf16[1024,512]{1,0:T(8,128)(2,1)S(1)}) custom-call(f32[8,512]{1,0:T(8,128)S(1)} %broadcast_in_dim.20.c_ref, f32[264,512]{1,0:T(8,128)S(1)} %convert_element_type.112.low_ref, f32[264,512]{1,0:T(8,128)S(1)} %convert_element_type.113.high_ref, f32[1032,512]{1,0:T(8,128)} %pad_maximum_fusion.refs_0_), custom_call_target="tpu_custom_call" | custom-call | flops 20971520 | bytes 6291456 | tf_op jit(solution)/shard_map/transport/pallas_call | solution.py:228
  60.0 3.1 %collective-permute-start.16 = (f16[264,512]{1,0:T(8,128)(2,1)S(1)}, f16[264,512]{1,0:T(8,128)(2,1)S(1)}, u32[]{:S(2)}, u32[]{:S(2)}) collective-permute-start(f16[264,512]{1,0:T(8,128)(2,1)S(1)} %maximum_maximum_fusion.1), channel_id=1, source_target_pairs={{0,3},{1,0},{2,1},{3,2},{4,7},{5,4},{6,5},{7,6},{8,11},{9,8},{10,9... | collective-permute-start | bytes 811016 | tf_op jit(solution)/shard_map/ppermute | solution.py:443
  66.7 5.0 %collective-permute-done.16 = f16[264,512]{1,0:T(8,128)(2,1)S(1)} collective-permute-done((f16[264,512]{1,0:T(8,128)(2,1)S(1)}, f16[264,512]{1,0:T(8,128)(2,1)S(1)}, u32[]{:S(2)}, u32[]{:S(2)}) %collective-permute-start.16) | collective-permute-done | bytes 270368 | tf_op jit(solution)/shard_map/ppermute | solution.py:443
  71.7 4.6 %transport.6 = (f32[1024,512]{1,0:T(8,128)S(1)}, bf16[1024,512]{1,0:T(8,128)(2,1)S(1)}) custom-call(f32[8,512]{1,0:T(8,128)S(1)} %broadcast_in_dim.20.c_ref, f32[264,512]{1,0:T(8,128)S(1)} %convert_element_type.130.low_ref, f32[264,512]{1,0:T(8,128)S(1)} %convert_element_type.131.high_ref, f32[1032,512]{1,0:T(8,128)} %pad_maximum_fusion.1.refs_0_), custom_call_target="tpu_custom_call" | custom-call | flops 20971520 | bytes 6291456 | tf_op jit(solution)/shard_map/transport/pallas_call | solution.py:228
  81.7 3.6 %faces.2 = (f32[2,256,512]{2,1,0:T(8,128)S(1)}, f32[2,264,512]{2,1,0:T(8,128)}) custom-call(bf16[1024,512]{1,0:T(8,128)(2,1)S(1)} %get-tuple-element.37.own_ref, bf16[1024,512]{1,0:T(8,128)(2,1)} %collective-permute-done.5.other_ref, f32[1024,512]{1,0:T(8,128)} %copy-done, f32[1024,128]{1,0:T(8,128)S(1)} %broadcast_in_dim.22.rate_ref, ...), custom_call_target="tpu_custom_call" | custom-call | flops 1073741824 | bytes 3932160 | tf_op jit(solution)/shard_map/faces/pallas_call | solution.py:282
  87.5 3.2 %collective-permute-start.7 = (f16[264,512]{1,0:T(8,128)(2,1)S(1)}, f16[264,512]{1,0:T(8,128)(2,1)S(1)}, u32[]{:S(2)}, u32[]{:S(2)}) collective-permute-start(f16[264,512]{1,0:T(8,128)(2,1)S(1)} %get-tuple-element.75), channel_id=1, source_target_pairs={{0,3},{1,0},{2,1},{3,2},{4,7},{5,4},{6,5},{7,6},{8,11},{9,8},{10,9... | collective-permute-start | bytes 811016 | tf_op jit(solution)/shard_map/ppermute | solution.py:443
  91.0 3.6 %faces.3 = (f32[2,256,512]{2,1,0:T(8,128)S(1)}, f32[2,264,512]{2,1,0:T(8,128)}) custom-call(bf16[1024,512]{1,0:T(8,128)(2,1)S(1)} %get-tuple-element.51.own_ref, bf16[1024,512]{1,0:T(8,128)(2,1)S(1)} %collective-permute-done.17.other_ref, f32[1024,512]{1,0:T(8,128)} %copy-done.1, f32[1024,128]{1,0:T(8,128)S(1)} %broadcast_in_dim.24.rate_ref, ...), custom_call_target="tpu_custom_call" | custom-call | flops 1073741824 | bytes 3932160 | tf_op jit(solution)/shard_map/faces/pallas_call | solution.py:282
  96.1 3.8 %collective-permute-start.19 = (f16[264,512]{1,0:T(8,128)(2,1)S(1)}, f16[264,512]{1,0:T(8,128)(2,1)S(1)}, u32[]{:S(2)}, u32[]{:S(2)}) collective-permute-start(f16[264,512]{1,0:T(8,128)(2,1)S(1)} %get-tuple-element.73), channel_id=1, source_target_pairs={{0,3},{1,0},{2,1},{3,2},{4,7},{5,4},{6,5},{7,6},{8,11},{9,8},{10,9... | collective-permute-start | bytes 811016 | tf_op jit(solution)/shard_map/ppermute | solution.py:443
  100.0 2.7 %inside.2.refs_1_ = f32[512,512]{1,0:T(8,128)S(1)} custom-call(bf16[1024,512]{1,0:T(8,128)(2,1)S(1)} %get-tuple-element.37.own_ref, bf16[1024,512]{1,0:T(8,128)(2,1)} %collective-permute-done.5.other_ref, f32[1024,512]{1,0:T(8,128)} %copy-done, f32[1024,128]{1,0:T(8,128)S(1)} %broadcast_in_dim.22.rate_ref, ...), custom_call_target="tpu_custom_call" | custom-call | flops 1073741824 | bytes 5242880 | tf_op jit(solution)/shard_map/inside/pallas_call | solution.py:316
  102.8 4.1 %transport.5 = (f32[1024,512]{1,0:T(8,128)}, bf16[1024,512]{1,0:T(8,128)(2,1)S(1)}) custom-call(f32[8,512]{1,0:T(8,128)S(1)} %broadcast_in_dim.20.c_ref, f32[264,512]{1,0:T(8,128)S(1)} %convert_element_type.118.low_ref, f32[264,512]{1,0:T(8,128)S(1)} %convert_element_type.119.high_ref, f32[256,512]{1,0:T(8,128)S(1)} %get-tuple-element.72.refs_0_, ...), custom_call_target="tpu_custom_call" | custom-call | flops 20971520 | bytes 6291456 | tf_op jit(solution)/shard_map/transport/pallas_call | solution.py:228
  106.9 2.6 %inside.3.refs_1_ = f32[512,512]{1,0:T(8,128)S(1)} custom-call(bf16[1024,512]{1,0:T(8,128)(2,1)S(1)} %get-tuple-element.51.own_ref, bf16[1024,512]{1,0:T(8,128)(2,1)S(1)} %collective-permute-done.17.other_ref, f32[1024,512]{1,0:T(8,128)} %copy-done.1, f32[1024,128]{1,0:T(8,128)S(1)} %broadcast_in_dim.24.rate_ref, ...), custom_call_target="tpu_custom_call" | custom-call | flops 1073741824 | bytes 5242880 | tf_op jit(solution)/shard_map/inside/pallas_call | solution.py:316
  109.7 3.7 %collective-permute-done.19 = f16[264,512]{1,0:T(8,128)(2,1)S(1)} collective-permute-done((f16[264,512]{1,0:T(8,128)(2,1)S(1)}, f16[264,512]{1,0:T(8,128)(2,1)S(1)}, u32[]{:S(2)}, u32[]{:S(2)}) %collective-permute-start.19) | collective-permute-done | bytes 270368 | tf_op jit(solution)/shard_map/ppermute | solution.py:443
  113.5 4.1 %transport.7 = (f32[1024,512]{1,0:T(8,128)}, bf16[1024,512]{1,0:T(8,128)(2,1)S(1)}) custom-call(f32[8,512]{1,0:T(8,128)S(1)} %broadcast_in_dim.20.c_ref, f32[264,512]{1,0:T(8,128)S(1)} %convert_element_type.136.low_ref, f32[264,512]{1,0:T(8,128)S(1)} %convert_element_type.137.high_ref, f32[256,512]{1,0:T(8,128)S(1)} %get-tuple-element.70.refs_0_, ...), custom_call_target="tpu_custom_call" | custom-call | flops 20971520 | bytes 6291456 | tf_op jit(solution)/shard_map/transport/pallas_call | solution.py:228
  117.6 3.8 %final.4 = (f32[1032,128]{1,0:T(8,128)S(1)}, f32[1032,128]{1,0:T(8,128)S(1)}) custom-call(bf16[1024,512]{1,0:T(8,128)(2,1)S(1)} %get-tuple-element.41.own_ref.rounded_ref, bf16[1024,512]{1,0:T(8,128)(2,1)S(1)} %collective-permute-done.8.other_ref, bf16[1024,512]{1,0:T(8,128)(2,1)S(1)} %get-tuple-element.41.own_ref.rounded_ref, ...), custom_call_target="tpu_custom_call" | custom-call | flops 1073741824 | bytes 5242880 | tf_op jit(solution)/shard_map/final/pallas_call | solution.py:369
  124.6 3.8 %final.6 = (f32[1032,128]{1,0:T(8,128)S(1)}, f32[1032,128]{1,0:T(8,128)S(1)}) custom-call(bf16[1024,512]{1,0:T(8,128)(2,1)S(1)} %get-tuple-element.55.own_ref.rounded_ref, bf16[1024,512]{1,0:T(8,128)(2,1)S(1)} %collective-permute-done.20.other_ref, bf16[1024,512]{1,0:T(8,128)(2,1)S(1)} %get-tuple-element.55.own_ref.rounded_ref, ...), custom_call_target="tpu_custom_call" | custom-call | flops 1073741824 | bytes 5242880 | tf_op jit(solution)/shard_map/final/pallas_call | solution.py:369
  129.7 3.8 %final.7 = (f32[1032,128]{1,0:T(8,128)S(1)}, f32[1032,128]{1,0:T(8,128)S(1)}) custom-call(bf16[1024,512]{1,0:T(8,128)(2,1)S(1)} %get-tuple-element.55.own_ref.rounded_ref, bf16[1024,512]{1,0:T(8,128)(2,1)S(1)} %collective-permute-done.20.other_ref, bf16[1024,512]{1,0:T(8,128)(2,1)S(1)} %get-tuple-element.55.own_ref.rounded_ref, ...), custom_call_target="tpu_custom_call" | custom-call | flops 1073741824 | bytes 5242880 | tf_op jit(solution)/shard_map/final/pallas_call | solution.py:369
  133.5 2.5 %collective-permute-start.23 = (f16[1032,128]{1,0:T(8,128)(2,1)S(1)}, f16[1032,128]{1,0:T(8,128)(2,1)S(1)}, u32[]{:S(2)}, u32[]{:S(2)}) collective-permute-start(f16[1032,128]{1,0:T(8,128)(2,1)S(1)} %convert_element_type.142), channel_id=1, source_target_pairs={{0,24},{4,28},{8,16},{12,20},{16,8},{20,12},{24,0},{28,4},{1,25},{... | collective-permute-start | bytes 792584 | tf_op jit(solution)/shard_map/ppermute | solution.py:438
  136.0 3.8 %final.5 = (f32[1032,128]{1,0:T(8,128)S(1)}, f32[1032,128]{1,0:T(8,128)S(1)}) custom-call(bf16[1024,512]{1,0:T(8,128)(2,1)S(1)} %get-tuple-element.41.own_ref.rounded_ref, bf16[1024,512]{1,0:T(8,128)(2,1)S(1)} %collective-permute-done.8.other_ref, bf16[1024,512]{1,0:T(8,128)(2,1)S(1)} %get-tuple-element.41.own_ref.rounded_ref, ...), custom_call_target="tpu_custom_call" | custom-call | flops 1073741824 | bytes 5242880 | tf_op jit(solution)/shard_map/final/pallas_call | solution.py:369
  140.5 8.0 %collective-permute-done.22 = f16[1032,128]{1,0:T(8,128)(2,1)S(1)} collective-permute-done((f16[1032,128]{1,0:T(8,128)(2,1)S(1)}, f16[1032,128]{1,0:T(8,128)(2,1)S(1)}, u32[]{:S(2)}, u32[]{:S(2)}) %collective-permute-start.22) | collective-permute-done | bytes 264224 | tf_op jit(solution)/shard_map/ppermute | solution.py:438
  151.0 2.3 %unpack.3 = f32[128,16,512]{2,1,0:T(8,128)} custom-call(s32[1]{0:T(128)} %bitcast.chip_ref, f32[1032,128]{1,0:T(8,128)S(1)} %convert_element_type.121.refs_0_, f32[1032,128]{1,0:T(8,128)S(1)} %convert_element_type.123.refs_1_, f32[1032,128]{1,0:T(8,128)S(1)} %convert_element_type.125.refs_2_, ...), custom_call_target="tpu_custom_call", output_to_operand_aliasing={{}: (5, {})} | custom-call | flops 1000000 | bytes 4194304 | tf_op jit(solution)/shard_map/unpack/pallas_call | solution.py:419
  (157 shorter events, 63.1 us)
Async XLA Ops:
  3.7 23.7 %collective-permute-start.2 = (f16[1032,128]{1,0:T(8,128)(2,1)}, f16[1032,128]{1,0:T(8,128)(2,1)}, u32[]{:S(2)}, u32[]{:S(2)}) collective-permute-start(f16[1032,128]{1,0:T(8,128)(2,1)} %convert_element_type.110), channel_id=1, source_target_pairs={{0,24},{4,28},{8,16},{12,20},{16,8},{20,12},{24,0},{28,4},{1,25},{... | collective-permute-start | bytes 792584 | tf_op jit(solution)/shard_map/ppermute | solution.py:438
  8.3 20.1 %collective-permute-start.1 = (f16[1032,128]{1,0:T(8,128)(2,1)}, f16[1032,128]{1,0:T(8,128)(2,1)}, u32[]{:S(2)}, u32[]{:S(2)}) collective-permute-start(f16[1032,128]{1,0:T(8,128)(2,1)} %convert_element_type.109), channel_id=1, source_target_pairs={{0,16},{4,20},{8,24},{12,28},{16,0},{20,4},{24,8},{28,12},{1,17},{... | collective-permute-start | bytes 792584 | tf_op jit(solution)/shard_map/ppermute | solution.py:438
  9.6 19.7 %collective-permute-start = (f16[1032,128]{1,0:T(8,128)(2,1)}, f16[1032,128]{1,0:T(8,128)(2,1)}, u32[]{:S(2)}, u32[]{:S(2)}) collective-permute-start(f16[1032,128]{1,0:T(8,128)(2,1)} %convert_element_type.108), channel_id=1, source_target_pairs={{0,8},{4,12},{8,0},{12,4},{16,24},{20,28},{24,16},{28,20},{1,9},{5... | collective-permute-start | bytes 792584 | tf_op jit(solution)/shard_map/ppermute | solution.py:438
  14.1 38.9 %collective-permute-start.14 = (f16[1032,128]{1,0:T(8,128)(2,1)}, f16[1032,128]{1,0:T(8,128)(2,1)S(1)}, u32[]{:S(2)}, u32[]{:S(2)}) collective-permute-start(f16[1032,128]{1,0:T(8,128)(2,1)} %convert_element_type.128), channel_id=1, source_target_pairs={{0,24},{4,28},{8,16},{12,20},{16,8},{20,12},{24,0},{28,4},{1,25},{... | collective-permute-start | bytes 792584 | tf_op jit(solution)/shard_map/ppermute | solution.py:438
  17.8 35.3 %collective-permute-start.13 = (f16[1032,128]{1,0:T(8,128)(2,1)}, f16[1032,128]{1,0:T(8,128)(2,1)}, u32[]{:S(2)}, u32[]{:S(2)}) collective-permute-start(f16[1032,128]{1,0:T(8,128)(2,1)} %convert_element_type.127), channel_id=1, source_target_pairs={{0,16},{4,20},{8,24},{12,28},{16,0},{20,4},{24,8},{28,12},{1,17},{... | collective-permute-start | bytes 792584 | tf_op jit(solution)/shard_map/ppermute | solution.py:438
  27.4 26.7 %collective-permute-start.12 = (f16[1032,128]{1,0:T(8,128)(2,1)}, f16[1032,128]{1,0:T(8,128)(2,1)}, u32[]{:S(2)}, u32[]{:S(2)}) collective-permute-start(f16[1032,128]{1,0:T(8,128)(2,1)} %convert_element_type.126), channel_id=1, source_target_pairs={{0,8},{4,12},{8,0},{12,4},{16,24},{20,28},{24,16},{28,20},{1,9},{5... | collective-permute-start | bytes 792584 | tf_op jit(solution)/shard_map/ppermute | solution.py:438
  30.3 14.0 %collective-permute-start.3 = (f16[264,512]{1,0:T(8,128)(2,1)S(1)}, f16[264,512]{1,0:T(8,128)(2,1)S(1)}, u32[]{:S(2)}, u32[]{:S(2)}) collective-permute-start(f16[264,512]{1,0:T(8,128)(2,1)S(1)} %pad_maximum_fusion.4), channel_id=1, source_target_pairs={{0,1},{1,2},{2,3},{3,0},{4,5},{5,6},{6,7},{7,4},{8,9},{9,10},{10,1... | collective-permute-start | bytes 811016 | tf_op jit(solution)/shard_map/ppermute | solution.py:443
  37.8 7.3 %collective-permute-start.4 = (f16[264,512]{1,0:T(8,128)(2,1)S(1)}, f16[264,512]{1,0:T(8,128)(2,1)S(1)}, u32[]{:S(2)}, u32[]{:S(2)}) collective-permute-start(f16[264,512]{1,0:T(8,128)(2,1)S(1)} %maximum_maximum_fusion), channel_id=1, source_target_pairs={{0,3},{1,0},{2,1},{3,2},{4,7},{5,4},{6,5},{7,6},{8,11},{9,8},{10,9... | collective-permute-start | bytes 811016 | tf_op jit(solution)/shard_map/ppermute | solution.py:443
  51.1 30.4 %collective-permute-start.5 = (bf16[1024,512]{1,0:T(8,128)(2,1)S(1)}, bf16[1024,512]{1,0:T(8,128)(2,1)}, u32[]{:S(2)}, u32[]{:S(2)}) collective-permute-start(bf16[1024,512]{1,0:T(8,128)(2,1)S(1)} %get-tuple-element.37.own_ref), channel_id=1, source_target_pairs={{0,4},{4,0},{8,12},{12,8},{16,20},{20,16},{24,28},{28,24},{1,5},{5... | collective-permute-start | bytes 3145736 | tf_op jit(solution)/shard_map/ppermute | solution.py:438
  55.1 11.5 %collective-permute-start.15 = (f16[264,512]{1,0:T(8,128)(2,1)S(1)}, f16[264,512]{1,0:T(8,128)(2,1)S(1)}, u32[]{:S(2)}, u32[]{:S(2)}) collective-permute-start(f16[264,512]{1,0:T(8,128)(2,1)S(1)} %pad_maximum_fusion.5), channel_id=1, source_target_pairs={{0,1},{1,2},{2,3},{3,0},{4,5},{5,6},{6,7},{7,4},{8,9},{9,10},{10,1... | collective-permute-start | bytes 811016 | tf_op jit(solution)/shard_map/ppermute | solution.py:443
  60.0 11.6 %collective-permute-start.16 = (f16[264,512]{1,0:T(8,128)(2,1)S(1)}, f16[264,512]{1,0:T(8,128)(2,1)S(1)}, u32[]{:S(2)}, u32[]{:S(2)}) collective-permute-start(f16[264,512]{1,0:T(8,128)(2,1)S(1)} %maximum_maximum_fusion.1), channel_id=1, source_target_pairs={{0,3},{1,0},{2,1},{3,2},{4,7},{5,4},{6,5},{7,6},{8,11},{9,8},{10,9... | collective-permute-start | bytes 811016 | tf_op jit(solution)/shard_map/ppermute | solution.py:443
  77.7 13.1 %collective-permute-start.17 = (bf16[1024,512]{1,0:T(8,128)(2,1)S(1)}, bf16[1024,512]{1,0:T(8,128)(2,1)S(1)}, u32[]{:S(2)}, u32[]{:S(2)}) collective-permute-start(bf16[1024,512]{1,0:T(8,128)(2,1)S(1)} %get-tuple-element.51.own_ref), channel_id=1, source_target_pairs={{0,4},{4,0},{8,12},{12,8},{16,20},{20,16},{24,28},{28,24},{1,5},{5... | collective-permute-start | bytes 3145736 | tf_op jit(solution)/shard_map/ppermute | solution.py:438
  86.8 15.8 %collective-permute-start.6 = (f16[264,512]{1,0:T(8,128)(2,1)S(1)}, f16[264,512]{1,0:T(8,128)(2,1)S(1)}, u32[]{:S(2)}, u32[]{:S(2)}) collective-permute-start(f16[264,512]{1,0:T(8,128)(2,1)S(1)} %get-tuple-element.76), channel_id=1, source_target_pairs={{0,1},{1,2},{2,3},{3,0},{4,5},{5,6},{6,7},{7,4},{8,9},{9,10},{10,1... | collective-permute-start | bytes 811016 | tf_op jit(solution)/shard_map/ppermute | solution.py:443
  87.5 15.3 %collective-permute-start.7 = (f16[264,512]{1,0:T(8,128)(2,1)S(1)}, f16[264,512]{1,0:T(8,128)(2,1)S(1)}, u32[]{:S(2)}, u32[]{:S(2)}) collective-permute-start(f16[264,512]{1,0:T(8,128)(2,1)S(1)} %get-tuple-element.75), channel_id=1, source_target_pairs={{0,3},{1,0},{2,1},{3,2},{4,7},{5,4},{6,5},{7,6},{8,11},{9,8},{10,9... | collective-permute-start | bytes 811016 | tf_op jit(solution)/shard_map/ppermute | solution.py:443
  96.0 13.6 %collective-permute-start.18 = (f16[264,512]{1,0:T(8,128)(2,1)S(1)}, f16[264,512]{1,0:T(8,128)(2,1)S(1)}, u32[]{:S(2)}, u32[]{:S(2)}) collective-permute-start(f16[264,512]{1,0:T(8,128)(2,1)S(1)} %get-tuple-element.74), channel_id=1, source_target_pairs={{0,1},{1,2},{2,3},{3,0},{4,5},{5,6},{6,7},{7,4},{8,9},{9,10},{10,1... | collective-permute-start | bytes 811016 | tf_op jit(solution)/shard_map/ppermute | solution.py:443
  96.1 17.3 %collective-permute-start.19 = (f16[264,512]{1,0:T(8,128)(2,1)S(1)}, f16[264,512]{1,0:T(8,128)(2,1)S(1)}, u32[]{:S(2)}, u32[]{:S(2)}) collective-permute-start(f16[264,512]{1,0:T(8,128)(2,1)S(1)} %get-tuple-element.73), channel_id=1, source_target_pairs={{0,3},{1,0},{2,1},{3,2},{4,7},{5,4},{6,5},{7,6},{8,11},{9,8},{10,9... | collective-permute-start | bytes 811016 | tf_op jit(solution)/shard_map/ppermute | solution.py:443
  106.9 10.7 %collective-permute-start.8 = (bf16[1024,512]{1,0:T(8,128)(2,1)S(1)}, bf16[1024,512]{1,0:T(8,128)(2,1)S(1)}, u32[]{:S(2)}, u32[]{:S(2)}) collective-permute-start(bf16[1024,512]{1,0:T(8,128)(2,1)S(1)} %get-tuple-element.41.own_ref.rounded_ref), channel_id=1, source_target_pairs={{0,4},{4,0},{8,12},{12,8},{16,20},{20,16},{24,28},{28,24},{1,5},{5... | collective-permute-start | bytes 3145736 | tf_op jit(solution)/shard_map/ppermute | solution.py:438
  117.6 7.0 %collective-permute-start.20 = (bf16[1024,512]{1,0:T(8,128)(2,1)S(1)}, bf16[1024,512]{1,0:T(8,128)(2,1)S(1)}, u32[]{:S(2)}, u32[]{:S(2)}) collective-permute-start(bf16[1024,512]{1,0:T(8,128)(2,1)S(1)} %get-tuple-element.55.own_ref.rounded_ref), channel_id=1, source_target_pairs={{0,4},{4,0},{8,12},{12,8},{16,20},{20,16},{24,28},{28,24},{1,5},{5... | collective-permute-start | bytes 3145736 | tf_op jit(solution)/shard_map/ppermute | solution.py:438
  121.4 18.4 %collective-permute-start.9 = (f16[1032,128]{1,0:T(8,128)(2,1)S(1)}, f16[1032,128]{1,0:T(8,128)(2,1)S(1)}, u32[]{:S(2)}, u32[]{:S(2)}) collective-permute-start(f16[1032,128]{1,0:T(8,128)(2,1)S(1)} %convert_element_type.120), channel_id=1, source_target_pairs={{0,8},{4,12},{8,0},{12,4},{16,24},{20,28},{24,16},{28,20},{1,9},{5... | collective-permute-start | bytes 792584 | tf_op jit(solution)/shard_map/ppermute | solution.py:438
  123.0 17.4 %collective-permute-start.10 = (f16[1032,128]{1,0:T(8,128)(2,1)S(1)}, f16[1032,128]{1,0:T(8,128)(2,1)S(1)}, u32[]{:S(2)}, u32[]{:S(2)}) collective-permute-start(f16[1032,128]{1,0:T(8,128)(2,1)S(1)} %convert_element_type.122), channel_id=1, source_target_pairs={{0,16},{4,20},{8,24},{12,28},{16,0},{20,4},{24,8},{28,12},{1,17},{... | collective-permute-start | bytes 792584 | tf_op jit(solution)/shard_map/ppermute | solution.py:438
  128.4 12.0 %collective-permute-start.21 = (f16[1032,128]{1,0:T(8,128)(2,1)S(1)}, f16[1032,128]{1,0:T(8,128)(2,1)S(1)}, u32[]{:S(2)}, u32[]{:S(2)}) collective-permute-start(f16[1032,128]{1,0:T(8,128)(2,1)S(1)} %convert_element_type.138), channel_id=1, source_target_pairs={{0,8},{4,12},{8,0},{12,4},{16,24},{20,28},{24,16},{28,20},{1,9},{5... | collective-permute-start | bytes 792584 | tf_op jit(solution)/shard_map/ppermute | solution.py:438
  129.1 19.5 %collective-permute-start.22 = (f16[1032,128]{1,0:T(8,128)(2,1)S(1)}, f16[1032,128]{1,0:T(8,128)(2,1)S(1)}, u32[]{:S(2)}, u32[]{:S(2)}) collective-permute-start(f16[1032,128]{1,0:T(8,128)(2,1)S(1)} %convert_element_type.140), channel_id=1, source_target_pairs={{0,16},{4,20},{8,24},{12,28},{16,0},{20,4},{24,8},{28,12},{1,17},{... | collective-permute-start | bytes 792584 | tf_op jit(solution)/shard_map/ppermute | solution.py:438
  133.5 15.1 %collective-permute-start.23 = (f16[1032,128]{1,0:T(8,128)(2,1)S(1)}, f16[1032,128]{1,0:T(8,128)(2,1)S(1)}, u32[]{:S(2)}, u32[]{:S(2)}) collective-permute-start(f16[1032,128]{1,0:T(8,128)(2,1)S(1)} %convert_element_type.142), channel_id=1, source_target_pairs={{0,24},{4,28},{8,16},{12,20},{16,8},{20,12},{24,0},{28,4},{1,25},{... | collective-permute-start | bytes 792584 | tf_op jit(solution)/shard_map/ppermute | solution.py:438
  139.8 11.1 %collective-permute-start.11 = (f16[1032,128]{1,0:T(8,128)(2,1)S(1)}, f16[1032,128]{1,0:T(8,128)(2,1)S(1)}, u32[]{:S(2)}, u32[]{:S(2)}) collective-permute-start(f16[1032,128]{1,0:T(8,128)(2,1)S(1)} %convert_element_type.124), channel_id=1, source_target_pairs={{0,24},{4,28},{8,16},{12,20},{16,8},{20,12},{24,0},{28,4},{1,25},{... | collective-permute-start | bytes 792584 | tf_op jit(solution)/shard_map/ppermute | solution.py:438
  (10 other events, 37.1 us)

commit v2 on v1

--- a/solution.py
+++ b/solution.py
@@ -9,10 +9,10 @@
 
 STEPS = 2
 HALO = 4
-HEAD = 8
+HEAD = 16
 CHUNKS = 2
 LANES = 128
-VMEM = 48 * 1024 * 1024
+VMEM = 16 * 1024 * 1024
 
 time_step = 0.2
 
@@ -100,9 +100,9 @@
     return field
 
 
-def params(count=1):
+def params(fusable=None):
     return pltpu.CompilerParams(
-        dimension_semantics=("arbitrary",) * count, vmem_limit_bytes=VMEM
+        dimension_semantics=("arbitrary",), vmem_limit_bytes=VMEM, allow_input_fusion=fusable
     )
 
 
@@ -137,13 +137,21 @@
             scale = jnp.exp2(power)
 
             def write(x, carry):
-                out[pl.ds(pl.multiple_of(x * cells, cells), cells), :] = (
+                start = place_of(x, planes, cells)
+                out[pl.ds(pl.multiple_of(start, 16), cells), :] = (
                     scratch[x, pl.ds(first, cells), :] * scale
                 )
                 return carry
 
             lax.fori_loop(0, planes, write, 0)
-            out[planes * cells :, :] = jnp.broadcast_to(power, (HEAD, LANES))
+            out[HALO * cells : HALO * cells + HEAD, :] = jnp.broadcast_to(power, (HEAD, LANES))
+
+
+def place_of(x, planes, cells):
+    first = planes - HALO
+    if isinstance(x, int):
+        return (x - first) * cells if x >= first else HALO * cells + HEAD + x * cells
+    return jnp.where(x >= first, (x - first) * cells, HALO * cells + HEAD + x * cells)
 
 
 def pack(distribution, chip, order, chunk, cells):
@@ -169,6 +177,100 @@
     )(chip, distribution)
 
 
+def message_kernel(cells, *refs):
+    pieces, up_ref, down_ref = refs[:-2], refs[-2], refs[-1]
+    rows = HALO * cells
+    for index, piece in enumerate(pieces):
+        columns = slice(index * LANES, (index + 1) * LANES)
+        up_ref[:, columns] = piece[: rows + HEAD, :]
+        down_ref[:, columns] = piece[rows : 2 * rows + HEAD, :]
+
+
+def messages_of(pieces, cells):
+    rows = 2 * HALO * cells + HEAD
+    shape = (HALO * cells + HEAD, LANES * len(pieces))
+    return pl.pallas_call(
+        functools.partial(message_kernel, cells),
+        grid=(1,),
+        in_specs=[pl.BlockSpec(p.shape, lambda i: (0, 0)) for p in pieces],
+        out_specs=[pl.BlockSpec(shape, lambda i: (0, 0))] * 2,
+        out_shape=[jax.ShapeDtypeStruct(shape, jnp.float32)] * 2,
+        compiler_params=params([True] * len(pieces)),
+        cost_estimate=cost(1e5, 8 * rows * LANES * len(pieces)),
+        name="messages",
+    )(*pieces)
+
+
+def spread_kernel(planes, cells, *refs):
+    pieces, out = refs[:-1], refs[-1]
+    rows = HALO * cells
+    for index, piece in enumerate(pieces):
+        columns = slice(index * LANES, (index + 1) * LANES)
+        scale = jnp.exp2(-piece[rows : rows + 1, :])
+        for x in range(planes):
+            start = place_of(x, planes, cells)
+            out[x * cells : (x + 1) * cells, columns] = piece[start : start + cells, :] * scale
+
+
+def spread(pieces, planes, cells):
+    shape = (planes * cells, LANES * len(pieces))
+    return pl.pallas_call(
+        functools.partial(spread_kernel, planes, cells),
+        grid=(1,),
+        in_specs=[pl.BlockSpec(p.shape, lambda i: (0, 0)) for p in pieces],
+        out_specs=pl.BlockSpec(shape, lambda i: (0, 0)),
+        out_shape=jax.ShapeDtypeStruct(shape, jnp.float32),
+        compiler_params=params([True] * len(pieces)),
+        cost_estimate=cost(1e6, 8 * shape[0] * shape[1]),
+        name="spread",
+    )(*pieces)
+
+
+def arrange_kernel(order, word_ref, c_ref, g_ref, p_ref, speeds_ref, gain_ref, product_ref):
+    chip, core = word_ref[0], word_ref[1]
+    count = len(order)
+    for row, mask in enumerate(order):
+        own = 2 * (chip ^ mask) + core
+        lines = slice(row * LANES, (row + 1) * LANES)
+        speeds_ref[:, lines] = jnp.broadcast_to(c_ref[pl.ds(own, 1), :], (8, LANES))
+        source = pl.ds(pl.multiple_of(own * LANES, LANES), LANES)
+        for column in range(2 * count):
+            other = order[column % count]
+            block = 2 * (chip ^ other) + (core if column < count else 1 - core)
+            lanes = pl.ds(pl.multiple_of(block * LANES, LANES), LANES)
+            target = slice(column * LANES, (column + 1) * LANES)
+            gain_ref[lines, target] = g_ref[source, lanes]
+            product_ref[lines, target] = p_ref[source, lanes]
+
+
+def arrange(courant, gain_matrix, product_matrix, word, order):
+    count = len(order)
+    whole = pl.BlockSpec(gain_matrix.shape, lambda i, s: (0, 0))
+    half = (count * LANES, 2 * count * LANES)
+    table = courant.reshape(-1, LANES)
+    return pl.pallas_call(
+        functools.partial(arrange_kernel, order),
+        grid_spec=pltpu.PrefetchScalarGridSpec(
+            num_scalar_prefetch=1,
+            grid=(1,),
+            in_specs=[pl.BlockSpec(table.shape, lambda i, s: (0, 0)), whole, whole],
+            out_specs=[
+                pl.BlockSpec((8, count * LANES), lambda i, s: (0, 0)),
+                pl.BlockSpec(half, lambda i, s: (0, 0)),
+                pl.BlockSpec(half, lambda i, s: (0, 0)),
+            ],
+        ),
+        out_shape=[
+            jax.ShapeDtypeStruct((8, count * LANES), jnp.float32),
+            jax.ShapeDtypeStruct(half, jnp.bfloat16),
+            jax.ShapeDtypeStruct(half, jnp.bfloat16),
+        ],
+        compiler_params=params(),
+        cost_estimate=cost(1e5, 12 * half[0] * half[1]),
+        name="arrange",
+    )(word, table, gain_matrix, product_matrix)
+
+
 def stage(values, speed, bend, positive):
     differ = [b - a for a, b in zip(values[:-1], values[1:])]
     slopes = [
@@ -180,53 +282,60 @@
     return [u - (b - a) for u, a, b in zip(values[2:-2], faces[:-1], faces[1:])]
 
 
-def advect_kernel(planes, cells, tile, scaled, c_ref, low_ref, high_ref, *refs):
+def advect_kernel(planes, cells, tile, c_ref, low_ref, high_ref, *refs):
     bodies, smoothed_ref, rounded_ref = refs[:-2], refs[-2], refs[-1]
+    rows = HALO * cells
     speed = c_ref[0:1, :]
     size = jnp.abs(speed)
     bend = 0.5 * size * (1.0 - size)
     positive = jnp.broadcast_to(speed, (tile, LANES)) > 0.0
-
-    def back(ref):
-        return jnp.exp2(-ref[HALO * cells : HALO * cells + 1, :])
-
-    back_low, back_high = back(low_ref), back(high_ref)
-    if scaled:
-        back_body = jnp.exp2(-bodies[0][planes * cells : planes * cells + 1, :])
-
-    def at(ref, x, t):
-        return ref[pl.ds(pl.multiple_of(x * cells + t * tile, tile), tile), :]
-
-    def body(t, carry):
-        values = [at(low_ref, x, t) * back_low for x in range(HALO)]
-        if scaled:
-            values += [at(bodies[0], x, t) * back_body for x in range(planes)]
-        else:
-            low, middle, high = bodies
-            values += [at(low, x, t) for x in range(HALO)]
-            values += [at(middle, x, t) for x in range(planes - 2 * HALO)]
-            values += [at(high, x, t) for x in range(HALO)]
-        values += [at(high_ref, x, t) * back_high for x in range(HALO)]
-        section = stage(values, speed, bend, positive)
-        moved = stage(section, speed, bend, positive)
-        for x in range(planes):
-            result = 0.5 * values[x + HALO] + 0.5 * moved[x]
-            where = pl.ds(pl.multiple_of(x * cells + t * tile, tile), tile)
-            smoothed_ref[where, :] = result
-            rounded_ref[where, :] = result.astype(jnp.bfloat16)
-        return carry
-
-    lax.fori_loop(0, cells // tile, body, 0)
-
-
-def transport(speeds, low, high, bodies, planes, cells, scaled):
+    back_low = jnp.exp2(-low_ref[rows : rows + 1, :])
+    back_high = jnp.exp2(-high_ref[0:1, :])
+
+    def run(read):
+        def body(t, carry):
+            def at(ref, start):
+                return ref[pl.ds(pl.multiple_of(start + t * tile, 16), tile), :]
+
+            values = [at(low_ref, x * cells) * back_low for x in range(HALO)]
+            values += [read(x, at) for x in range(planes)]
+            values += [at(high_ref, HEAD + x * cells) * back_high for x in range(HALO)]
+            section = stage(values, speed, bend, positive)
+            moved = stage(section, speed, bend, positive)
+            for x in range(planes):
+                result = 0.5 * values[x + HALO] + 0.5 * moved[x]
+                where = pl.ds(pl.multiple_of(x * cells + t * tile, tile), tile)
+                smoothed_ref[where, :] = result
+                rounded_ref[where, :] = result.astype(jnp.bfloat16)
+            return carry
+
+        lax.fori_loop(0, cells // tile, body, 0)
+
+    if len(bodies) == 1:
+        run(lambda x, at: at(bodies[0], x * cells))
+    else:
+        ends, middle = bodies
+
+        def read(x, at):
+            if x < HALO:
+                return at(ends.at[0], x * cells)
+            if x >= planes - HALO:
+                return at(ends.at[1], (x - planes + HALO) * cells)
+            return at(middle, (x - HALO) * cells)
+
+        run(read)
+
+
+def transport(speeds, low, high, bodies, planes, cells):
     rows, width = planes * cells, low.shape[1]
 
     def spec(a):
+        if a.ndim == 3:
+            return pl.BlockSpec((2, a.shape[1], LANES), lambda j: (0, 0, j))
         return pl.BlockSpec((a.shape[0], LANES), lambda j: (0, j))
 
     return pl.pallas_call(
-        functools.partial(advect_kernel, planes, cells, 16, scaled),
+        functools.partial(advect_kernel, planes, cells, 16),
         grid=(width // LANES,),
         in_specs=[spec(a) for a in (speeds, low, high, *bodies)],
         out_specs=[pl.BlockSpec((rows, LANES), lambda j: (0, j))] * 2,
@@ -259,9 +368,10 @@
     return smoothed + time_step * (gained - rate * rounded.astype(jnp.float32))
 
 
-def faces_kernel(own_ref, other_ref, smoothed_ref, rate_ref, gain_ref, product_ref, state_ref, message_ref):
+def faces_kernel(own_ref, other_ref, smoothed_ref, rate_ref, gain_ref, product_ref, state_ref, down_ref, up_ref):
     rows, width = own_ref.shape
     group = 2 * LANES
+    step = pl.program_id(0)
     for start in range(0, width, group):
         columns = slice(start, start + group)
         state = collided(
@@ -270,8 +380,18 @@
         )
         state_ref[0, :, columns] = state
         power = exponent_of(jnp.max(jnp.abs(state), axis=0, keepdims=True))
-        message_ref[0, :rows, columns] = state * jnp.exp2(power)
-        message_ref[0, rows:, columns] = jnp.broadcast_to(power, (HEAD, group))
+        scaled = state * jnp.exp2(power)
+        head = jnp.broadcast_to(power, (HEAD, group))
+
+        @pl.when(step == 0)
+        def _():
+            down_ref[:HEAD, columns] = head
+            down_ref[HEAD:, columns] = scaled
+
+        @pl.when(step == 1)
+        def _():
+            up_ref[:rows, columns] = scaled
+            up_ref[rows:, columns] = head
 
 
 def faces(own, other, smoothed, rate, gain, product, planes, cells):
@@ -279,17 +399,20 @@
     last = planes // HALO - 1
     block = pl.BlockSpec((rows, width), lambda i: (i * last, 0))
     whole = pl.BlockSpec(gain.shape, lambda i: (0, 0))
+    message = (rows + HEAD, width)
     return pl.pallas_call(
         faces_kernel,
         grid=(2,),
         in_specs=[block, block, block, pl.BlockSpec((rows, LANES), lambda i: (i * last, 0)), whole, whole],
         out_specs=[
             pl.BlockSpec((1, rows, width), lambda i: (i, 0, 0)),
-            pl.BlockSpec((1, rows + HEAD, width), lambda i: (i, 0, 0)),
+            pl.BlockSpec(message, lambda i: (0, 0)),
+            pl.BlockSpec(message, lambda i: (0, 0)),
         ],
         out_shape=[
             jax.ShapeDtypeStruct((2, rows, width), jnp.float32),
-            jax.ShapeDtypeStruct((2, rows + HEAD, width), jnp.float32),
+            jax.ShapeDtypeStruct(message, jnp.float32),
+            jax.ShapeDtypeStruct(message, jnp.float32),
         ],
         compiler_params=params(),
         cost_estimate=cost(16 * rows * width * width, 30 * rows * width),
@@ -392,13 +515,8 @@
             first = pl.multiple_of((chip ^ mask) * cells, cells)
             scale = jnp.exp2(-piece[planes * cells : planes * cells + 1, :])
 
-            def place(x, carry):
-                scratch[x, pl.ds(first, cells), :] = (
-                    piece[pl.ds(pl.multiple_of(x * cells, cells), cells), :] * scale
-                )
-                return carry
-
-            lax.fori_loop(0, planes, place, 0)
+            for x in range(planes):
+                scratch[x, pl.ds(first, cells), :] = piece[x * cells : (x + 1) * cells, :] * scale
 
     for x in range(planes):
         part = scratch[x, pl.ds(pl.multiple_of(step * LANES, LANES), LANES), :]
@@ -411,6 +529,7 @@
     shape = (LANES, planes, width * CHUNKS)
     specs = [pl.BlockSpec(p.shape, lambda i, s: (0, 0)) for p in pieces]
     operands = list(pieces)
+    count = len(pieces)
     aliases = {}
     if target is not None:
         specs.append(pl.BlockSpec(memory_space=pl.ANY))
@@ -427,7 +546,7 @@
         ),
         out_shape=jax.ShapeDtypeStruct(shape, jnp.float32),
         input_output_aliases=aliases,
-        compiler_params=params(),
+        compiler_params=params([False] + [True] * count + [False] * (len(operands) - count)),
         cost_estimate=cost(1e6, 8 * LANES * planes * width),
         name="unpack",
     )(chip, *operands)
@@ -451,51 +570,23 @@
     return array.astype(jnp.float32)
 
 
-def first_faces(pieces, cells, planes):
-    body = HALO * cells
-    top = planes * cells
-
-    def message(start):
-        return jnp.concatenate(
-            [jnp.concatenate([p[start : start + body], p[top:]], axis=0) for p in pieces], axis=1
-        )
-
-    return message(top - body), message(0)
-
-
 def body(distribution, courant, gain_matrix, product_matrix, collision_rate):
     planes, plane = distribution.shape[1:]
     chips = lax.axis_size("vel") // 2
-    member = lax.axis_index("vel")
-    chip, core = member // 2, member % 2
+    member = lax.axis_index("vel").astype(jnp.int32)
+    chip, core = lax.shift_right_logical(member, 1), member & 1
     order = list(range(1, chips)) + [0]
     cells = plane // (chips * CHUNKS)
     span = cells * chips
-    chip_word = chip.astype(jnp.int32).reshape(1)
-
-    pieces = [pack(distribution, chip_word, order, k, cells) for k in range(CHUNKS)]
-    sent = [
-        [half(a) if mask == 0 else exchange(half(a), 2 * mask) for a, mask in zip(pieces[k], order)]
-        for k in range(CHUNKS)
-    ]
-
-    own_blocks = [2 * (chip ^ mask) + core for mask in order]
-    other_blocks = [2 * (chip ^ mask) + 1 - core for mask in order]
-
-    def arranged(matrix):
-        lines = jnp.concatenate(
-            [lax.dynamic_slice_in_dim(matrix, b * LANES, LANES, 0) for b in own_blocks], axis=0
+    word = jnp.stack([chip, core])
+
+    sent = []
+    for k in range(CHUNKS):
+        pieces = pack(distribution, word, order, k, cells)
+        sent.append(
+            [a if m == 0 else full(exchange(half(a), 2 * m)) for a, m in zip(pieces, order)]
         )
-        return jnp.concatenate(
-            [lax.dynamic_slice_in_dim(lines, b * LANES, LANES, 1) for b in own_blocks + other_blocks],
-            axis=1,
-        )
-
-    gain, product = arranged(gain_matrix), arranged(product_matrix)
-    speeds = jnp.concatenate(
-        [lax.dynamic_slice_in_dim(courant, b * LANES, LANES, 0) for b in own_blocks]
-    )
-    speeds = jnp.broadcast_to(speeds[None], (8, speeds.shape[0]))
+    speeds, gain, product = arrange(courant, gain_matrix, product_matrix, word, order)
     rates = []
     for k in range(CHUNKS):
         own = lax.dynamic_slice_in_dim(collision_rate, k * span + chip * cells, cells, 1)
@@ -504,29 +595,23 @@
     result = None
     states = []
     for k in range(CHUNKS):
-        up, down = first_faces(sent[k], cells, planes)
-        low, high = full(shift(up, 1)), full(shift(down, -1))
-        local = jnp.concatenate(
-            [a if mask == 0 else full(b) for a, b, mask in zip(pieces[k], sent[k], order)], axis=1
-        )
-        smoothed, rounded = transport(speeds, low, high, [local], planes, cells, True)
+        up, down = messages_of(sent[k], cells)
+        low, high = full(shift(half(up), 1)), full(shift(half(down), -1))
+        smoothed, rounded = transport(speeds, low, high, [spread(sent[k], planes, cells)], planes, cells)
         other = exchange(rounded, 1)
-        ends, messages = faces(rounded, other, smoothed, rates[k], gain, product, planes, cells)
-        messages = half(messages)
-        low, high = full(shift(messages[1], 1)), full(shift(messages[0], -1))
+        ends, down, up = faces(rounded, other, smoothed, rates[k], gain, product, planes, cells)
+        low, high = full(shift(half(up), 1)), full(shift(half(down), -1))
         middle = inside(rounded, other, smoothed, rates[k], gain, product, planes, cells)
-        states.append((low, high, [ends[0], middle, ends[1]]))
+        states.append((low, high, [ends, middle]))
     for k in range(CHUNKS):
         low, high, parts = states[k]
-        smoothed, rounded = transport(speeds, low, high, parts, planes, cells, False)
+        smoothed, rounded = transport(speeds, low, high, parts, planes, cells)
         other = exchange(rounded, 1)
         ready = []
         for part in range(chips // 2):
             ready += final(rounded, other, smoothed, rates[k], gain, product, planes, cells, part)
-        back = [
-            a if mask == 0 else full(exchange(half(a), 2 * mask)) for a, mask in zip(ready, order)
-        ]
-        result = unpack(back, result, chip_word, order, k, planes, cells)
+        back = [a if m == 0 else full(exchange(half(a), 2 * m)) for a, m in zip(ready, order)]
+        result = unpack(back, result, word, order, k, planes, cells)
     return result
 
 

time: 155 us -> 129 us (0.83)
  local copies, waits for them, and re-layouts: 28.5 us -> 11.5 us
  other arithmetic: 19.7 us -> 4.64 us
  waiting for transfers between devices: 17.5 us -> 30 us
  Pallas kernels: 55.5 us -> 48.2 us
  starting transfers between devices: 31.3 us -> 33.7 us
    ppermute x16, waiting for transfers between devices: 8.09 us -> 22.8 us  [exchange(): return lax.ppermute(array, 'vel', [(i, i ^ mask) for i in range(count)])]
    slice x16 -> x0, local copies, waits for them, and re-layouts: 8.9 us -> none  [the longest x8 4.95 us: message(): p[start:start + body]]
    convert_element_type x16 -> x20, other arithmetic: 8.47 us -> 1.52 us  [half(): return array.astype(jnp.float16)]
    concatenate x10 -> x0, local copies, waits for them, and re-layouts: 6.51 us -> none  [the longest x8 4.61 us: message(): jnp.concatenate([p[start:start + body], p[top:]], axis=0)]
    concatenate x9 -> x0, other arithmetic: 5.62 us -> none  [the longest x2 2.99 us: body(): jnp.concatenate([a if mask == 0 else full(b) for a, b, mask in zip(pieces...]
    pallas_call x4, Pallas kernels: 15.1 us -> 9.68 us  [final(): pl.pallas_call(functools.partial(final_kernel, blocks), grid=(blocks,), i...]
    convert_element_type x20, other arithmetic: 5.64 us -> 3.05 us  [full(): return array.astype(jnp.float32)]
    ppermute x16, starting transfers between devices: 15.4 us -> 17.9 us  [exchange(): return lax.ppermute(array, 'vel', [(i, i ^ mask) for i in range(count)])]
  transfers between devices with their start and end apart: 24 -> 24, of which waited for: 5 -> 7; matrix products, arithmetic and copies ran while one was open for 28% -> 4% of each run, Pallas kernels for 33% -> 33%
where the time goes in v2:
time: 129 us
  Pallas kernels  48.2 us (37%)
  starting transfers between devices  33.7 us (26%)
  waiting for transfers between devices  30 us (23%)
  local copies, waits for them, and re-layouts  11.5 us (9%)
  other arithmetic  4.64 us (4%)
    ppermute x16, waiting for transfers between devices, exchange(): return lax.ppermute(array, 'vel', [(i, i ^ mask) for i in range(count)])  22.8 us
    ppermute x16, starting transfers between devices, exchange(): return lax.ppermute(array, 'vel', [(i, i ^ mask) for i in range(count)])  17.9 us
    ppermute x8, starting transfers between devices, shift(): lax.ppermute(array, 'space', [(i, (i + step) % count) for i in range(coun...  15.8 us
    pallas_call x4, Pallas kernels, transport(): pl.pallas_call(functools.partial(advect_kernel, planes, cells, 16), grid=...  14.8 us
    unnamed x32, local copies, waits for them, and re-layouts  10.9 us
    pallas_call x4, Pallas kernels, final(): pl.pallas_call(functools.partial(final_kernel, blocks), grid=(blocks,), i...  9.68 us
    ppermute x8, waiting for transfers between devices, shift(): lax.ppermute(array, 'space', [(i, (i + step) % count) for i in range(coun...  7.16 us
    pallas_call x2, Pallas kernels, faces(): pl.pallas_call(faces_kernel, grid=(2,), in_specs=[block, block, block, pl...  6.43 us
  transfers between devices with their start and end apart: 24, of which 7 were waited for; matrix products, arithmetic and copies ran while one was open for 4% of the time, Pallas kernels for 33%

profile of v2, /device:TPU:0, one launch (start us, length us, event | category | flops | bytes accessed | tf_op | source)
XLA Modules:
  0.0 128.7 jit_solution(5555520186604922383)
XLA Ops:
  2.3 2.6 %pack.2 = (f32[1040,128]{1,0:T(8,128)S(1)}, f32[1040,128]{1,0:T(8,128)S(1)}, f32[1040,128]{1,0:T(8,128)S(1)}, f32[1040,128]{1,0:T(8,128)S(1)}) custom-call(s32[2]{0:T(128)S(1)} %pad_add_fusion.word_ref.chip_ref, f32[128,16,512]{2,1,0:T(8,128)S(1)} %copy-done), custom_call_target="tpu_custom_call" | custom-call | flops 1000000 | bytes 4194304 | tf_op jit(solution)/shard_map/pack/pallas_call | solution.py:162
  5.0 3.0 %collective-permute-start = (f16[1040,128]{1,0:T(8,128)(2,1)S(1)}, f16[1040,128]{1,0:T(8,128)(2,1)S(1)}, u32[]{:S(2)}, u32[]{:S(2)}) collective-permute-start(f16[1040,128]{1,0:T(8,128)(2,1)S(1)} %convert_element_type.120), channel_id=1, source_target_pairs={{0,8},{4,12},{8,0},{12,4},{16,24},{20,28},{24,16},{28,20},{1,9},{5... | collective-permute-start | bytes 798728 | tf_op jit(solution)/shard_map/ppermute | solution.py:557
  9.7 2.7 %pack.3 = (f32[1040,128]{1,0:T(8,128)S(1)}, f32[1040,128]{1,0:T(8,128)S(1)}, f32[1040,128]{1,0:T(8,128)S(1)}, f32[1040,128]{1,0:T(8,128)S(1)}) custom-call(s32[2]{0:T(128)S(1)} %pad_add_fusion.word_ref.chip_ref, f32[128,16,512]{2,1,0:T(8,128)S(1)} %copy-done), custom_call_target="tpu_custom_call" | custom-call | flops 1000000 | bytes 4194304 | tf_op jit(solution)/shard_map/pack/pallas_call | solution.py:162
  18.2 4.0 %collective-permute-done.1 = f16[1040,128]{1,0:T(8,128)(2,1)S(1)} collective-permute-done((f16[1040,128]{1,0:T(8,128)(2,1)S(1)}, f16[1040,128]{1,0:T(8,128)(2,1)S(1)}, u32[]{:S(2)}, u32[]{:S(2)}) %collective-permute-start.1) | collective-permute-done | bytes 266272 | tf_op jit(solution)/shard_map/ppermute | solution.py:557
  26.7 6.3 %collective-permute-done.13 = f16[1040,128]{1,0:T(8,128)(2,1)S(1)} collective-permute-done((f16[1040,128]{1,0:T(8,128)(2,1)S(1)}, f16[1040,128]{1,0:T(8,128)(2,1)S(1)}, u32[]{:S(2)}, u32[]{:S(2)}) %collective-permute-start.13) | collective-permute-done | bytes 266272 | tf_op jit(solution)/shard_map/ppermute | solution.py:557
  38.9 3.5 %transport.4 = (f32[1024,512]{1,0:T(8,128)S(1)}, bf16[1024,512]{1,0:T(8,128)(2,1)S(1)}) custom-call(f32[8,512]{1,0:T(8,128)S(1)} %get-tuple-element.42.c_ref, f32[272,512]{1,0:T(8,128)S(1)} %convert_element_type.127.low_ref, f32[272,512]{1,0:T(8,128)S(1)} %convert_element_type.129.high_ref, f32[1024,512]{1,0:T(8,128)S(1)} %spread.2.refs_0_), custom_call_target="tpu_custom_call" | custom-call | flops 20971520 | bytes 6291456 | tf_op jit(solution)/shard_map/transport/pallas_call | solution.py:337
  44.9 3.5 %collective-permute-done.16 = f16[272,512]{1,0:T(8,128)(2,1)S(1)} collective-permute-done((f16[272,512]{1,0:T(8,128)(2,1)S(1)}, f16[272,512]{1,0:T(8,128)(2,1)S(1)}, u32[]{:S(2)}, u32[]{:S(2)}) %collective-permute-start.16) | collective-permute-done | bytes 278560 | tf_op jit(solution)/shard_map/ppermute | solution.py:562
  48.5 4.1 %transport.6 = (f32[1024,512]{1,0:T(8,128)S(1)}, bf16[1024,512]{1,0:T(8,128)(2,1)}) custom-call(f32[8,512]{1,0:T(8,128)S(1)} %get-tuple-element.42.c_ref, f32[272,512]{1,0:T(8,128)S(1)} %convert_element_type.147.low_ref, f32[272,512]{1,0:T(8,128)S(1)} %convert_element_type.149.high_ref, f32[1024,512]{1,0:T(8,128)S(1)} %spread.3.refs_0_), custom_call_target="tpu_custom_call" | custom-call | flops 20971520 | bytes 6291456 | tf_op jit(solution)/shard_map/transport/pallas_call | solution.py:337
  57.1 3.1 %faces.2 = (f32[2,256,512]{2,1,0:T(8,128)S(1)}, f32[272,512]{1,0:T(8,128)S(1)}, f32[272,512]{1,0:T(8,128)S(1)}) custom-call(bf16[1024,512]{1,0:T(8,128)(2,1)S(1)} %copy-done.8, bf16[1024,512]{1,0:T(8,128)(2,1)} %collective-permute-done.5.other_ref, f32[1024,512]{1,0:T(8,128)S(1)} %copy-done.5, f32[1024,128]{1,0:T(8,128)S(1)} %broadcast_in_dim.15.rate_ref, ...), custom_call_target="tpu_custom_call" | custom-call | flops 1073741824 | bytes 3932160 | tf_op jit(solution)/shard_map/faces/pallas_call | solution.py:403
  63.1 2.8 %collective-permute-start.7 = (f16[272,512]{1,0:T(8,128)(2,1)}, f16[272,512]{1,0:T(8,128)(2,1)}, u32[]{:S(2)}, u32[]{:S(2)}) collective-permute-start(f16[272,512]{1,0:T(8,128)(2,1)} %convert_element_type.132), channel_id=1, source_target_pairs={{0,3},{1,0},{2,1},{3,2},{4,7},{5,4},{6,5},{7,6},{8,11},{9,8},{10,9... | collective-permute-start | bytes 835592 | tf_op jit(solution)/shard_map/ppermute | solution.py:562
  67.7 3.3 %faces.3 = (f32[2,256,512]{2,1,0:T(8,128)S(1)}, f32[272,512]{1,0:T(8,128)S(1)}, f32[272,512]{1,0:T(8,128)S(1)}) custom-call(bf16[1024,512]{1,0:T(8,128)(2,1)} %get-tuple-element.68.own_ref, bf16[1024,512]{1,0:T(8,128)(2,1)} %collective-permute-done.17.other_ref, f32[1024,512]{1,0:T(8,128)S(1)} %copy-done.2, f32[1024,128]{1,0:T(8,128)S(1)} %broadcast_in_dim.17.rate_ref, ...), custom_call_target="tpu_custom_call" | custom-call | flops 1073741824 | bytes 3932160 | tf_op jit(solution)/shard_map/faces/pallas_call | solution.py:403
  71.3 4.0 %collective-permute-start.19 = (f16[272,512]{1,0:T(8,128)(2,1)S(1)}, f16[272,512]{1,0:T(8,128)(2,1)S(1)}, u32[]{:S(2)}, u32[]{:S(2)}) collective-permute-start(f16[272,512]{1,0:T(8,128)(2,1)S(1)} %convert_element_type.152), channel_id=1, source_target_pairs={{0,3},{1,0},{2,1},{3,2},{4,7},{5,4},{6,5},{7,6},{8,11},{9,8},{10,9... | collective-permute-start | bytes 835592 | tf_op jit(solution)/shard_map/ppermute | solution.py:562
  75.3 2.5 %inside.2.refs_1_ = f32[512,512]{1,0:T(8,128)S(1)} custom-call(bf16[1024,512]{1,0:T(8,128)(2,1)S(1)} %copy-done.9, bf16[1024,512]{1,0:T(8,128)(2,1)} %collective-permute-done.5.other_ref, f32[1024,512]{1,0:T(8,128)S(1)} %copy-done.6, f32[1024,128]{1,0:T(8,128)S(1)} %broadcast_in_dim.15.rate_ref, bf16[512,1024]{1,0:T(8,128)(2,1)S(1)} %get-tuple-element.51.gain_ref, ...), custom_call_target="tpu_custom_call" | custom-call | flops 1073741824 | bytes 5242880 | tf_op jit(solution)/shard_map/inside/pallas_call | solution.py:439
  80.1 3.6 %transport.5 = (f32[1024,512]{1,0:T(8,128)S(1)}, bf16[1024,512]{1,0:T(8,128)(2,1)S(1)}) custom-call(f32[8,512]{1,0:T(8,128)S(1)} %get-tuple-element.42.c_ref, f32[272,512]{1,0:T(8,128)S(1)} %convert_element_type.131.low_ref, f32[272,512]{1,0:T(8,128)S(1)} %convert_element_type.133.high_ref, f32[2,256,512]{2,1,0:T(8,128)S(1)} %copy-done.13, ...), custom_call_target="tpu_custom_call" | custom-call | flops 20971520 | bytes 6291456 | tf_op jit(solution)/shard_map/transport/pallas_call | solution.py:337
  83.8 2.6 %inside.3.refs_1_ = f32[512,512]{1,0:T(8,128)S(1)} custom-call(bf16[1024,512]{1,0:T(8,128)(2,1)} %get-tuple-element.68.own_ref, bf16[1024,512]{1,0:T(8,128)(2,1)} %collective-permute-done.17.other_ref, f32[1024,512]{1,0:T(8,128)S(1)} %copy-done.3, f32[1024,128]{1,0:T(8,128)S(1)} %broadcast_in_dim.17.rate_ref, ...), custom_call_target="tpu_custom_call" | custom-call | flops 1073741824 | bytes 5242880 | tf_op jit(solution)/shard_map/inside/pallas_call | solution.py:439
  86.5 3.5 %collective-permute-done.19 = f16[272,512]{1,0:T(8,128)(2,1)S(1)} collective-permute-done((f16[272,512]{1,0:T(8,128)(2,1)S(1)}, f16[272,512]{1,0:T(8,128)(2,1)S(1)}, u32[]{:S(2)}, u32[]{:S(2)}) %collective-permute-start.19) | collective-permute-done | bytes 278560 | tf_op jit(solution)/shard_map/ppermute | solution.py:562
  90.1 3.6 %transport.7 = (f32[1024,512]{1,0:T(8,128)S(1)}, bf16[1024,512]{1,0:T(8,128)(2,1)S(1)}) custom-call(f32[8,512]{1,0:T(8,128)S(1)} %get-tuple-element.42.c_ref, f32[272,512]{1,0:T(8,128)S(1)} %convert_element_type.151.low_ref, f32[272,512]{1,0:T(8,128)S(1)} %convert_element_type.153.high_ref, f32[2,256,512]{2,1,0:T(8,128)S(1)} %get-tuple-element.72.refs_0_, ...), custom_call_target="tpu_custom_call" | custom-call | flops 20971520 | bytes 6291456 | tf_op jit(solution)/shard_map/transport/pallas_call | solution.py:337
  93.7 2.4 %final.4 = (f32[1040,128]{1,0:T(8,128)S(1)}, f32[1040,128]{1,0:T(8,128)S(1)}) custom-call(bf16[1024,512]{1,0:T(8,128)(2,1)S(1)} %get-tuple-element.56.own_ref.rounded_ref, bf16[1024,512]{1,0:T(8,128)(2,1)S(1)} %collective-permute-done.8.other_ref, bf16[1024,512]{1,0:T(8,128)(2,1)S(1)} %get-tuple-element.56.own_ref.rounded_ref, ...), custom_call_target="tpu_custom_call" | custom-call | flops 1073741824 | bytes 5242880 | tf_op jit(solution)/shard_map/final/pallas_call | solution.py:492
  98.4 2.4 %final.6 = (f32[1040,128]{1,0:T(8,128)S(1)}, f32[1040,128]{1,0:T(8,128)S(1)}) custom-call(bf16[1024,512]{1,0:T(8,128)(2,1)S(1)} %get-tuple-element.73.own_ref.rounded_ref, bf16[1024,512]{1,0:T(8,128)(2,1)S(1)} %collective-permute-done.20.other_ref, bf16[1024,512]{1,0:T(8,128)(2,1)S(1)} %get-tuple-element.73.own_ref.rounded_ref, ...), custom_call_target="tpu_custom_call" | custom-call | flops 1073741824 | bytes 5242880 | tf_op jit(solution)/shard_map/final/pallas_call | solution.py:492
  103.1 2.4 %final.7 = (f32[1040,128]{1,0:T(8,128)S(1)}, f32[1040,128]{1,0:T(8,128)S(1)}) custom-call(bf16[1024,512]{1,0:T(8,128)(2,1)S(1)} %get-tuple-element.73.own_ref.rounded_ref, bf16[1024,512]{1,0:T(8,128)(2,1)S(1)} %collective-permute-done.20.other_ref, bf16[1024,512]{1,0:T(8,128)(2,1)S(1)} %get-tuple-element.73.own_ref.rounded_ref, ...), custom_call_target="tpu_custom_call" | custom-call | flops 1073741824 | bytes 5242880 | tf_op jit(solution)/shard_map/final/pallas_call | solution.py:492
  107.0 2.4 %final.5 = (f32[1040,128]{1,0:T(8,128)S(1)}, f32[1040,128]{1,0:T(8,128)S(1)}) custom-call(bf16[1024,512]{1,0:T(8,128)(2,1)S(1)} %get-tuple-element.56.own_ref.rounded_ref, bf16[1024,512]{1,0:T(8,128)(2,1)S(1)} %collective-permute-done.8.other_ref, bf16[1024,512]{1,0:T(8,128)(2,1)S(1)} %get-tuple-element.56.own_ref.rounded_ref, ...), custom_call_target="tpu_custom_call" | custom-call | flops 1073741824 | bytes 5242880 | tf_op jit(solution)/shard_map/final/pallas_call | solution.py:492
  111.2 12.3 %collective-permute-done.22 = f16[1040,128]{1,0:T(8,128)(2,1)S(1)} collective-permute-done((f16[1040,128]{1,0:T(8,128)(2,1)S(1)}, f16[1040,128]{1,0:T(8,128)(2,1)S(1)}, u32[]{:S(2)}, u32[]{:S(2)}) %collective-permute-start.22) | collective-permute-done | bytes 266272 | tf_op jit(solution)/shard_map/ppermute | solution.py:557
  123.6 2.5 %unpack.2.refs_4_ = f32[128,16,512]{2,1,0:T(8,128)} custom-call(s32[2]{0:T(128)S(1)} %pad_add_fusion.word_ref.chip_ref, f32[1040,128]{1,0:T(8,128)S(1)} %convert_element_type.155.refs_0_, f32[1040,128]{1,0:T(8,128)S(1)} %convert_element_type.157.refs_1_, f32[1040,128]{1,0:T(8,128)S(1)} %convert_element_type.159.refs_2_, ...), custom_call_target="tpu_custom_call" | custom-call | flops 1000000 | bytes 4194304 | tf_op jit(solution)/shard_map/unpack/pallas_call | solution.py:538
  126.2 2.5 %unpack.3 = f32[128,16,512]{2,1,0:T(8,128)} custom-call(s32[2]{0:T(128)S(1)} %pad_add_fusion.word_ref.chip_ref, f32[1040,128]{1,0:T(8,128)S(1)} %convert_element_type.135.refs_0_, f32[1040,128]{1,0:T(8,128)S(1)} %convert_element_type.137.refs_1_, f32[1040,128]{1,0:T(8,128)S(1)} %convert_element_type.139.refs_2_, ...), custom_call_target="tpu_custom_call", output_to_operand_aliasing={{}: (5, {})} | custom-call | flops 1000000 | bytes 4194304 | tf_op jit(solution)/shard_map/unpack/pallas_call | solution.py:538
  (123 shorter events, 42.2 us)
Async XLA Ops:
  5.0 11.1 %collective-permute-start = (f16[1040,128]{1,0:T(8,128)(2,1)S(1)}, f16[1040,128]{1,0:T(8,128)(2,1)S(1)}, u32[]{:S(2)}, u32[]{:S(2)}) collective-permute-start(f16[1040,128]{1,0:T(8,128)(2,1)S(1)} %convert_element_type.120), channel_id=1, source_target_pairs={{0,8},{4,12},{8,0},{12,4},{16,24},{20,28},{24,16},{28,20},{1,9},{5... | collective-permute-start | bytes 798728 | tf_op jit(solution)/shard_map/ppermute | solution.py:557
  8.0 14.2 %collective-permute-start.1 = (f16[1040,128]{1,0:T(8,128)(2,1)S(1)}, f16[1040,128]{1,0:T(8,128)(2,1)S(1)}, u32[]{:S(2)}, u32[]{:S(2)}) collective-permute-start(f16[1040,128]{1,0:T(8,128)(2,1)S(1)} %convert_element_type.122), channel_id=1, source_target_pairs={{0,16},{4,20},{8,24},{12,28},{16,0},{20,4},{24,8},{28,12},{1,17},{... | collective-permute-start | bytes 798728 | tf_op jit(solution)/shard_map/ppermute | solution.py:557
  9.6 12.8 %collective-permute-start.2 = (f16[1040,128]{1,0:T(8,128)(2,1)S(1)}, f16[1040,128]{1,0:T(8,128)(2,1)S(1)}, u32[]{:S(2)}, u32[]{:S(2)}) collective-permute-start(f16[1040,128]{1,0:T(8,128)(2,1)S(1)} %convert_element_type.124), channel_id=1, source_target_pairs={{0,24},{4,28},{8,16},{12,20},{16,8},{20,12},{24,0},{28,4},{1,25},{... | collective-permute-start | bytes 798728 | tf_op jit(solution)/shard_map/ppermute | solution.py:557
  12.4 14.3 %collective-permute-start.12 = (f16[1040,128]{1,0:T(8,128)(2,1)S(1)}, f16[1040,128]{1,0:T(8,128)(2,1)S(1)}, u32[]{:S(2)}, u32[]{:S(2)}) collective-permute-start(f16[1040,128]{1,0:T(8,128)(2,1)S(1)} %convert_element_type.140), channel_id=1, source_target_pairs={{0,8},{4,12},{8,0},{12,4},{16,24},{20,28},{24,16},{28,20},{1,9},{5... | collective-permute-start | bytes 798728 | tf_op jit(solution)/shard_map/ppermute | solution.py:557
  14.5 18.6 %collective-permute-start.13 = (f16[1040,128]{1,0:T(8,128)(2,1)S(1)}, f16[1040,128]{1,0:T(8,128)(2,1)S(1)}, u32[]{:S(2)}, u32[]{:S(2)}) collective-permute-start(f16[1040,128]{1,0:T(8,128)(2,1)S(1)} %convert_element_type.142), channel_id=1, source_target_pairs={{0,16},{4,20},{8,24},{12,28},{16,0},{20,4},{24,8},{28,12},{1,17},{... | collective-permute-start | bytes 798728 | tf_op jit(solution)/shard_map/ppermute | solution.py:557
  16.1 17.0 %collective-permute-start.14 = (f16[1040,128]{1,0:T(8,128)(2,1)S(1)}, f16[1040,128]{1,0:T(8,128)(2,1)S(1)}, u32[]{:S(2)}, u32[]{:S(2)}) collective-permute-start(f16[1040,128]{1,0:T(8,128)(2,1)S(1)} %convert_element_type.144), channel_id=1, source_target_pairs={{0,24},{4,28},{8,16},{12,20},{16,8},{20,12},{24,0},{28,4},{1,25},{... | collective-permute-start | bytes 798728 | tf_op jit(solution)/shard_map/ppermute | solution.py:557
  22.7 16.0 %collective-permute-start.3 = (f16[272,512]{1,0:T(8,128)(2,1)S(1)}, f16[272,512]{1,0:T(8,128)(2,1)S(1)}, u32[]{:S(2)}, u32[]{:S(2)}) collective-permute-start(f16[272,512]{1,0:T(8,128)(2,1)S(1)} %convert_element_type.126), channel_id=1, source_target_pairs={{0,1},{1,2},{2,3},{3,0},{4,5},{5,6},{6,7},{7,4},{8,9},{9,10},{10,1... | collective-permute-start | bytes 835592 | tf_op jit(solution)/shard_map/ppermute | solution.py:562
  24.4 14.4 %collective-permute-start.4 = (f16[272,512]{1,0:T(8,128)(2,1)S(1)}, f16[272,512]{1,0:T(8,128)(2,1)S(1)}, u32[]{:S(2)}, u32[]{:S(2)}) collective-permute-start(f16[272,512]{1,0:T(8,128)(2,1)S(1)} %convert_element_type.128), channel_id=1, source_target_pairs={{0,3},{1,0},{2,1},{3,2},{4,7},{5,4},{6,5},{7,6},{8,11},{9,8},{10,9... | collective-permute-start | bytes 835592 | tf_op jit(solution)/shard_map/ppermute | solution.py:562
  33.4 11.5 %collective-permute-start.15 = (f16[272,512]{1,0:T(8,128)(2,1)S(1)}, f16[272,512]{1,0:T(8,128)(2,1)S(1)}, u32[]{:S(2)}, u32[]{:S(2)}) collective-permute-start(f16[272,512]{1,0:T(8,128)(2,1)S(1)} %convert_element_type.146), channel_id=1, source_target_pairs={{0,1},{1,2},{2,3},{3,0},{4,5},{5,6},{6,7},{7,4},{8,9},{9,10},{10,1... | collective-permute-start | bytes 835592 | tf_op jit(solution)/shard_map/ppermute | solution.py:562
  35.0 13.4 %collective-permute-start.16 = (f16[272,512]{1,0:T(8,128)(2,1)S(1)}, f16[272,512]{1,0:T(8,128)(2,1)S(1)}, u32[]{:S(2)}, u32[]{:S(2)}) collective-permute-start(f16[272,512]{1,0:T(8,128)(2,1)S(1)} %convert_element_type.148), channel_id=1, source_target_pairs={{0,3},{1,0},{2,1},{3,2},{4,7},{5,4},{6,5},{7,6},{8,11},{9,8},{10,9... | collective-permute-start | bytes 835592 | tf_op jit(solution)/shard_map/ppermute | solution.py:562
  43.8 10.3 %collective-permute-start.5 = (bf16[1024,512]{1,0:T(8,128)(2,1)S(1)}, bf16[1024,512]{1,0:T(8,128)(2,1)}, u32[]{:S(2)}, u32[]{:S(2)}) collective-permute-start(bf16[1024,512]{1,0:T(8,128)(2,1)S(1)} %get-tuple-element.49.own_ref), channel_id=1, source_target_pairs={{0,4},{4,0},{8,12},{12,8},{16,20},{20,16},{24,28},{28,24},{1,5},{5... | collective-permute-start | bytes 3145736 | tf_op jit(solution)/shard_map/ppermute | solution.py:557
  53.9 12.0 %collective-permute-start.17 = (bf16[1024,512]{1,0:T(8,128)(2,1)}, bf16[1024,512]{1,0:T(8,128)(2,1)}, u32[]{:S(2)}, u32[]{:S(2)}) collective-permute-start(bf16[1024,512]{1,0:T(8,128)(2,1)} %get-tuple-element.68.own_ref), channel_id=1, source_target_pairs={{0,4},{4,0},{8,12},{12,8},{16,20},{20,16},{24,28},{28,24},{1,5},{5... | collective-permute-start | bytes 3145736 | tf_op jit(solution)/shard_map/ppermute | solution.py:557
  61.2 16.6 %collective-permute-start.6 = (f16[272,512]{1,0:T(8,128)(2,1)S(1)}, f16[272,512]{1,0:T(8,128)(2,1)}, u32[]{:S(2)}, u32[]{:S(2)}) collective-permute-start(f16[272,512]{1,0:T(8,128)(2,1)S(1)} %convert_element_type.130), channel_id=1, source_target_pairs={{0,1},{1,2},{2,3},{3,0},{4,5},{5,6},{6,7},{7,4},{8,9},{9,10},{10,1... | collective-permute-start | bytes 835592 | tf_op jit(solution)/shard_map/ppermute | solution.py:562
  63.1 15.9 %collective-permute-start.7 = (f16[272,512]{1,0:T(8,128)(2,1)}, f16[272,512]{1,0:T(8,128)(2,1)}, u32[]{:S(2)}, u32[]{:S(2)}) collective-permute-start(f16[272,512]{1,0:T(8,128)(2,1)} %convert_element_type.132), channel_id=1, source_target_pairs={{0,3},{1,0},{2,1},{3,2},{4,7},{5,4},{6,5},{7,6},{8,11},{9,8},{10,9... | collective-permute-start | bytes 835592 | tf_op jit(solution)/shard_map/ppermute | solution.py:562
  71.1 15.2 %collective-permute-start.18 = (f16[272,512]{1,0:T(8,128)(2,1)S(1)}, f16[272,512]{1,0:T(8,128)(2,1)S(1)}, u32[]{:S(2)}, u32[]{:S(2)}) collective-permute-start(f16[272,512]{1,0:T(8,128)(2,1)S(1)} %convert_element_type.150), channel_id=1, source_target_pairs={{0,1},{1,2},{2,3},{3,0},{4,5},{5,6},{6,7},{7,4},{8,9},{9,10},{10,1... | collective-permute-start | bytes 835592 | tf_op jit(solution)/shard_map/ppermute | solution.py:562
  71.3 18.7 %collective-permute-start.19 = (f16[272,512]{1,0:T(8,128)(2,1)S(1)}, f16[272,512]{1,0:T(8,128)(2,1)S(1)}, u32[]{:S(2)}, u32[]{:S(2)}) collective-permute-start(f16[272,512]{1,0:T(8,128)(2,1)S(1)} %convert_element_type.152), channel_id=1, source_target_pairs={{0,3},{1,0},{2,1},{3,2},{4,7},{5,4},{6,5},{7,6},{8,11},{9,8},{10,9... | collective-permute-start | bytes 835592 | tf_op jit(solution)/shard_map/ppermute | solution.py:562
  83.7 10.0 %collective-permute-start.8 = (bf16[1024,512]{1,0:T(8,128)(2,1)S(1)}, bf16[1024,512]{1,0:T(8,128)(2,1)S(1)}, u32[]{:S(2)}, u32[]{:S(2)}) collective-permute-start(bf16[1024,512]{1,0:T(8,128)(2,1)S(1)} %get-tuple-element.56.own_ref.rounded_ref), channel_id=1, source_target_pairs={{0,4},{4,0},{8,12},{12,8},{16,20},{20,16},{24,28},{28,24},{1,5},{5... | collective-permute-start | bytes 3145736 | tf_op jit(solution)/shard_map/ppermute | solution.py:557
  93.6 4.7 %collective-permute-start.20 = (bf16[1024,512]{1,0:T(8,128)(2,1)S(1)}, bf16[1024,512]{1,0:T(8,128)(2,1)S(1)}, u32[]{:S(2)}, u32[]{:S(2)}) collective-permute-start(bf16[1024,512]{1,0:T(8,128)(2,1)S(1)} %get-tuple-element.73.own_ref.rounded_ref), channel_id=1, source_target_pairs={{0,4},{4,0},{8,12},{12,8},{16,20},{20,16},{24,28},{28,24},{1,5},{5... | collective-permute-start | bytes 3145736 | tf_op jit(solution)/shard_map/ppermute | solution.py:557
  96.2 13.3 %collective-permute-start.9 = (f16[1040,128]{1,0:T(8,128)(2,1)S(1)}, f16[1040,128]{1,0:T(8,128)(2,1)S(1)}, u32[]{:S(2)}, u32[]{:S(2)}) collective-permute-start(f16[1040,128]{1,0:T(8,128)(2,1)S(1)} %convert_element_type.134), channel_id=1, source_target_pairs={{0,8},{4,12},{8,0},{12,4},{16,24},{20,28},{24,16},{28,20},{1,9},{5... | collective-permute-start | bytes 798728 | tf_op jit(solution)/shard_map/ppermute | solution.py:557
  97.8 13.3 %collective-permute-start.10 = (f16[1040,128]{1,0:T(8,128)(2,1)S(1)}, f16[1040,128]{1,0:T(8,128)(2,1)S(1)}, u32[]{:S(2)}, u32[]{:S(2)}) collective-permute-start(f16[1040,128]{1,0:T(8,128)(2,1)S(1)} %convert_element_type.136), channel_id=1, source_target_pairs={{0,16},{4,20},{8,24},{12,28},{16,0},{20,4},{24,8},{28,12},{1,17},{... | collective-permute-start | bytes 798728 | tf_op jit(solution)/shard_map/ppermute | solution.py:557
  100.8 10.3 %collective-permute-start.21 = (f16[1040,128]{1,0:T(8,128)(2,1)S(1)}, f16[1040,128]{1,0:T(8,128)(2,1)S(1)}, u32[]{:S(2)}, u32[]{:S(2)}) collective-permute-start(f16[1040,128]{1,0:T(8,128)(2,1)S(1)} %convert_element_type.154), channel_id=1, source_target_pairs={{0,8},{4,12},{8,0},{12,4},{16,24},{20,28},{24,16},{28,20},{1,9},{5... | collective-permute-start | bytes 798728 | tf_op jit(solution)/shard_map/ppermute | solution.py:557
  102.3 21.2 %collective-permute-start.22 = (f16[1040,128]{1,0:T(8,128)(2,1)S(1)}, f16[1040,128]{1,0:T(8,128)(2,1)S(1)}, u32[]{:S(2)}, u32[]{:S(2)}) collective-permute-start(f16[1040,128]{1,0:T(8,128)(2,1)S(1)} %convert_element_type.156), channel_id=1, source_target_pairs={{0,16},{4,20},{8,24},{12,28},{16,0},{20,4},{24,8},{28,12},{1,17},{... | collective-permute-start | bytes 798728 | tf_op jit(solution)/shard_map/ppermute | solution.py:557
  105.5 18.0 %collective-permute-start.23 = (f16[1040,128]{1,0:T(8,128)(2,1)S(1)}, f16[1040,128]{1,0:T(8,128)(2,1)S(1)}, u32[]{:S(2)}, u32[]{:S(2)}) collective-permute-start(f16[1040,128]{1,0:T(8,128)(2,1)S(1)} %convert_element_type.158), channel_id=1, source_target_pairs={{0,24},{4,28},{8,16},{12,20},{16,8},{20,12},{24,0},{28,4},{1,25},{... | collective-permute-start | bytes 798728 | tf_op jit(solution)/shard_map/ppermute | solution.py:557
  109.5 16.6 %collective-permute-start.11 = (f16[1040,128]{1,0:T(8,128)(2,1)S(1)}, f16[1040,128]{1,0:T(8,128)(2,1)S(1)}, u32[]{:S(2)}, u32[]{:S(2)}) collective-permute-start(f16[1040,128]{1,0:T(8,128)(2,1)S(1)} %convert_element_type.138), channel_id=1, source_target_pairs={{0,24},{4,28},{8,16},{12,20},{16,8},{20,12},{24,0},{28,4},{1,25},{... | collective-permute-start | bytes 798728 | tf_op jit(solution)/shard_map/ppermute | solution.py:557
  (16 other events, 51.8 us)

commit v3 on v2

--- a/solution.py
+++ b/solution.py
@@ -12,7 +12,7 @@
 HEAD = 16
 CHUNKS = 2
 LANES = 128
-VMEM = 16 * 1024 * 1024
+VMEM = 12 * 1024 * 1024
 
 time_step = 0.2
 
@@ -100,10 +100,20 @@
     return field
 
 
-def params(fusable=None):
+def params(fusable=None, grid=True):
     return pltpu.CompilerParams(
-        dimension_semantics=("arbitrary",), vmem_limit_bytes=VMEM, allow_input_fusion=fusable
+        dimension_semantics=("arbitrary",) if grid else None,
+        vmem_limit_bytes=VMEM,
+        allow_input_fusion=fusable,
     )
+
+
+def resident():
+    return pl.BlockSpec(memory_space=pltpu.VMEM)
+
+
+def anywhere():
+    return pl.BlockSpec(memory_space=pl.ANY)
 
 
 def cost(flops, moved):
@@ -167,18 +177,18 @@
             in_specs=[
                 pl.BlockSpec((LANES, planes, LANES), lambda i, s: (0, 0, chunk * steps + i))
             ],
-            out_specs=[pl.BlockSpec(shape, lambda i, s: (0, 0)) for _ in order],
+            out_specs=[resident() for _ in order],
             scratch_shapes=[pltpu.VMEM((planes, width, LANES), jnp.float32)],
         ),
         out_shape=[jax.ShapeDtypeStruct(shape, jnp.float32) for _ in order],
         compiler_params=params(),
         cost_estimate=cost(1e6, 8 * LANES * planes * width),
         name="pack",
-    )(chip, distribution)
+    )(chip, pltpu.with_memory_space_constraint(distribution, pltpu.HBM))
 
 
 def message_kernel(cells, *refs):
-    pieces, up_ref, down_ref = refs[:-2], refs[-2], refs[-1]
+    pieces, up_ref, down_ref = refs[:-3], refs[-2], refs[-1]
     rows = HALO * cells
     for index, piece in enumerate(pieces):
         columns = slice(index * LANES, (index + 1) * LANES)
@@ -186,19 +196,19 @@
         down_ref[:, columns] = piece[rows : 2 * rows + HEAD, :]
 
 
-def messages_of(pieces, cells):
+def messages_of(pieces, cells, after):
     rows = 2 * HALO * cells + HEAD
     shape = (HALO * cells + HEAD, LANES * len(pieces))
     return pl.pallas_call(
         functools.partial(message_kernel, cells),
         grid=(1,),
-        in_specs=[pl.BlockSpec(p.shape, lambda i: (0, 0)) for p in pieces],
-        out_specs=[pl.BlockSpec(shape, lambda i: (0, 0))] * 2,
+        in_specs=[pl.BlockSpec(p.shape, lambda i: (0, 0)) for p in pieces] + [anywhere()],
+        out_specs=[resident()] * 2,
         out_shape=[jax.ShapeDtypeStruct(shape, jnp.float32)] * 2,
-        compiler_params=params([True] * len(pieces)),
+        compiler_params=params([True] * len(pieces) + [False]),
         cost_estimate=cost(1e5, 8 * rows * LANES * len(pieces)),
         name="messages",
-    )(*pieces)
+    )(*pieces, after)
 
 
 def spread_kernel(planes, cells, *refs):
@@ -218,7 +228,7 @@
         functools.partial(spread_kernel, planes, cells),
         grid=(1,),
         in_specs=[pl.BlockSpec(p.shape, lambda i: (0, 0)) for p in pieces],
-        out_specs=pl.BlockSpec(shape, lambda i: (0, 0)),
+        out_specs=resident(),
         out_shape=jax.ShapeDtypeStruct(shape, jnp.float32),
         compiler_params=params([True] * len(pieces)),
         cost_estimate=cost(1e6, 8 * shape[0] * shape[1]),
@@ -245,30 +255,20 @@
 
 def arrange(courant, gain_matrix, product_matrix, word, order):
     count = len(order)
-    whole = pl.BlockSpec(gain_matrix.shape, lambda i, s: (0, 0))
-    half = (count * LANES, 2 * count * LANES)
-    table = courant.reshape(-1, LANES)
+    shape = (count * LANES, 2 * count * LANES)
     return pl.pallas_call(
         functools.partial(arrange_kernel, order),
-        grid_spec=pltpu.PrefetchScalarGridSpec(
-            num_scalar_prefetch=1,
-            grid=(1,),
-            in_specs=[pl.BlockSpec(table.shape, lambda i, s: (0, 0)), whole, whole],
-            out_specs=[
-                pl.BlockSpec((8, count * LANES), lambda i, s: (0, 0)),
-                pl.BlockSpec(half, lambda i, s: (0, 0)),
-                pl.BlockSpec(half, lambda i, s: (0, 0)),
-            ],
-        ),
+        in_specs=[pl.BlockSpec(memory_space=pltpu.SMEM)] + [resident()] * 3,
+        out_specs=[resident()] * 3,
         out_shape=[
             jax.ShapeDtypeStruct((8, count * LANES), jnp.float32),
-            jax.ShapeDtypeStruct(half, jnp.bfloat16),
-            jax.ShapeDtypeStruct(half, jnp.bfloat16),
+            jax.ShapeDtypeStruct(shape, jnp.bfloat16),
+            jax.ShapeDtypeStruct(shape, jnp.bfloat16),
         ],
-        compiler_params=params(),
-        cost_estimate=cost(1e5, 12 * half[0] * half[1]),
+        compiler_params=params(grid=False),
+        cost_estimate=cost(1e5, 12 * shape[0] * shape[1]),
         name="arrange",
-    )(word, table, gain_matrix, product_matrix)
+    )(word, courant.reshape(-1, LANES), gain_matrix, product_matrix)
 
 
 def stage(values, speed, bend, positive):
@@ -282,224 +282,194 @@
     return [u - (b - a) for u, a, b in zip(values[2:-2], faces[:-1], faces[1:])]
 
 
-def advect_kernel(planes, cells, tile, c_ref, low_ref, high_ref, *refs):
-    bodies, smoothed_ref, rounded_ref = refs[:-2], refs[-2], refs[-1]
+def advect_kernel(planes, cells, tile, count, c_ref, low_ref, high_ref, *refs):
+    bodies, smoothed_ref, rounded_ref = refs[: count], refs[-2], refs[-1]
     rows = HALO * cells
-    speed = c_ref[0:1, :]
-    size = jnp.abs(speed)
-    bend = 0.5 * size * (1.0 - size)
-    positive = jnp.broadcast_to(speed, (tile, LANES)) > 0.0
-    back_low = jnp.exp2(-low_ref[rows : rows + 1, :])
-    back_high = jnp.exp2(-high_ref[0:1, :])
-
-    def run(read):
+
+    def read(x, start, lanes):
+        if count == 1:
+            ref, first = bodies[0], x * cells
+        elif x < HALO:
+            ref, first = bodies[0].at[0], x * cells
+        elif x >= planes - HALO:
+            ref, first = bodies[0].at[1], (x - planes + HALO) * cells
+        else:
+            ref, first = bodies[1], (x - HALO) * cells
+        return ref[pl.ds(pl.multiple_of(first + start, tile), tile), lanes]
+
+    def column(j, outer):
+        lanes = pl.ds(pl.multiple_of(j * LANES, LANES), LANES)
+        speed = c_ref[0:1, lanes]
+        size = jnp.abs(speed)
+        bend = 0.5 * size * (1.0 - size)
+        positive = jnp.broadcast_to(speed, (tile, LANES)) > 0.0
+        back_low = jnp.exp2(-low_ref[rows : rows + 1, lanes])
+        back_high = jnp.exp2(-high_ref[0:1, lanes])
+
         def body(t, carry):
-            def at(ref, start):
-                return ref[pl.ds(pl.multiple_of(start + t * tile, 16), tile), :]
-
-            values = [at(low_ref, x * cells) * back_low for x in range(HALO)]
-            values += [read(x, at) for x in range(planes)]
-            values += [at(high_ref, HEAD + x * cells) * back_high for x in range(HALO)]
+            start = t * tile
+
+            def halo(ref, first):
+                return ref[pl.ds(pl.multiple_of(first + start, tile), tile), lanes]
+
+            values = [halo(low_ref, x * cells) * back_low for x in range(HALO)]
+            values += [read(x, start, lanes) for x in range(planes)]
+            values += [halo(high_ref, HEAD + x * cells) * back_high for x in range(HALO)]
             section = stage(values, speed, bend, positive)
             moved = stage(section, speed, bend, positive)
             for x in range(planes):
-                result = 0.5 * values[x + HALO] + 0.5 * moved[x]
-                where = pl.ds(pl.multiple_of(x * cells + t * tile, tile), tile)
-                smoothed_ref[where, :] = result
-                rounded_ref[where, :] = result.astype(jnp.bfloat16)
+                result = 0.5 * read(x, start, lanes) + 0.5 * moved[x]
+                where = pl.ds(pl.multiple_of(x * cells + start, tile), tile)
+                smoothed_ref[where, lanes] = result
+                rounded_ref[where, lanes] = result.astype(jnp.bfloat16)
             return carry
 
-        lax.fori_loop(0, cells // tile, body, 0)
-
-    if len(bodies) == 1:
-        run(lambda x, at: at(bodies[0], x * cells))
-    else:
-        ends, middle = bodies
-
-        def read(x, at):
-            if x < HALO:
-                return at(ends.at[0], x * cells)
-            if x >= planes - HALO:
-                return at(ends.at[1], (x - planes + HALO) * cells)
-            return at(middle, (x - HALO) * cells)
-
-        run(read)
-
-
-def transport(speeds, low, high, bodies, planes, cells):
+        return lax.fori_loop(0, cells // tile, body, outer)
+
+    lax.fori_loop(0, low_ref.shape[1] // LANES, column, 0)
+
+
+def transport(speeds, low, high, bodies, planes, cells, after):
     rows, width = planes * cells, low.shape[1]
-
-    def spec(a):
-        if a.ndim == 3:
-            return pl.BlockSpec((2, a.shape[1], LANES), lambda j: (0, 0, j))
-        return pl.BlockSpec((a.shape[0], LANES), lambda j: (0, j))
-
-    return pl.pallas_call(
-        functools.partial(advect_kernel, planes, cells, 16),
-        grid=(width // LANES,),
-        in_specs=[spec(a) for a in (speeds, low, high, *bodies)],
-        out_specs=[pl.BlockSpec((rows, LANES), lambda j: (0, j))] * 2,
+    return pl.pallas_call(
+        functools.partial(advect_kernel, planes, cells, 16, len(bodies)),
+        in_specs=[resident()] * (3 + len(bodies)) + [anywhere()],
+        out_specs=[resident()] * 2,
         out_shape=[
             jax.ShapeDtypeStruct((rows, width), jnp.float32),
             jax.ShapeDtypeStruct((rows, width), jnp.bfloat16),
         ],
-        compiler_params=params(),
+        compiler_params=params(grid=False),
         cost_estimate=cost(40 * rows * width, 12 * rows * width),
         name="transport",
-    )(speeds, low, high, *bodies)
-
-
-def gains(own, other, matrix_ref, columns):
-    half = own.shape[1]
+    )(speeds, low, high, *bodies, after)
+
+
+def collided(lhs, smoothed, rounded, rate, gain_ref, product_ref, columns):
     dims = (((1,), (1,)), ((), ()))
-    return lax.dot_general(
-        own, matrix_ref[columns, :half], dims, preferred_element_type=jnp.float32
-    ) + lax.dot_general(
-        other, matrix_ref[columns, half:], dims, preferred_element_type=jnp.float32
-    )
-
-
-def collided(own_ref, other_ref, smoothed, rounded, rate_ref, gain_ref, product_ref, columns):
-    own, other = own_ref[...], other_ref[...]
-    gained = gains(own, other, gain_ref, columns) * gains(own, other, product_ref, columns)
-    gained = gained.astype(jnp.bfloat16).astype(jnp.float32)
-    rate = rate_ref[...]
+
+    def term(ref):
+        return lax.dot_general(lhs, ref[columns, :], dims, preferred_element_type=jnp.float32)
+
+    gained = (term(gain_ref) * term(product_ref)).astype(jnp.bfloat16).astype(jnp.float32)
     rate = jnp.concatenate([rate] * (rounded.shape[1] // LANES), axis=1)
     return smoothed + time_step * (gained - rate * rounded.astype(jnp.float32))
 
 
-def faces_kernel(own_ref, other_ref, smoothed_ref, rate_ref, gain_ref, product_ref, state_ref, down_ref, up_ref):
-    rows, width = own_ref.shape
-    group = 2 * LANES
-    step = pl.program_id(0)
-    for start in range(0, width, group):
+def joined(own_ref, other_ref, rows):
+    return jnp.concatenate([own_ref[rows, :], other_ref[rows, :]], axis=1)
+
+
+def faces_kernel(planes, cells, own_ref, other_ref, smoothed_ref, rate_ref, gain_ref, product_ref, state_ref, down_ref, up_ref):
+    rows, group = HALO * cells, 2 * LANES
+    first, last = slice(0, rows), slice((planes - HALO) * cells, planes * cells)
+    lhs = jnp.concatenate(
+        [joined(own_ref, other_ref, first), joined(own_ref, other_ref, last)], axis=0
+    )
+    rate = jnp.concatenate([rate_ref[first, :], rate_ref[last, :]], axis=0)
+    for start in range(0, own_ref.shape[1], group):
         columns = slice(start, start + group)
-        state = collided(
-            own_ref, other_ref, smoothed_ref[:, columns], own_ref[:, columns], rate_ref,
-            gain_ref, product_ref, columns,
-        )
-        state_ref[0, :, columns] = state
-        power = exponent_of(jnp.max(jnp.abs(state), axis=0, keepdims=True))
-        scaled = state * jnp.exp2(power)
-        head = jnp.broadcast_to(power, (HEAD, group))
-
-        @pl.when(step == 0)
-        def _():
-            down_ref[:HEAD, columns] = head
-            down_ref[HEAD:, columns] = scaled
-
-        @pl.when(step == 1)
-        def _():
-            up_ref[:rows, columns] = scaled
-            up_ref[rows:, columns] = head
+        smoothed = jnp.concatenate([smoothed_ref[first, columns], smoothed_ref[last, columns]], axis=0)
+        rounded = jnp.concatenate([own_ref[first, columns], own_ref[last, columns]], axis=0)
+        state = collided(lhs, smoothed, rounded, rate, gain_ref, product_ref, columns)
+        for index, part in enumerate((state[:rows], state[rows:])):
+            state_ref[index, :, columns] = part
+            power = exponent_of(jnp.max(jnp.abs(part), axis=0, keepdims=True))
+            scaled = part * jnp.exp2(power)
+            head = jnp.broadcast_to(power, (HEAD, group))
+            if index == 0:
+                down_ref[:HEAD, columns] = head
+                down_ref[HEAD:, columns] = scaled
+            else:
+                up_ref[:rows, columns] = scaled
+                up_ref[rows:, columns] = head
 
 
 def faces(own, other, smoothed, rate, gain, product, planes, cells):
     rows, width = HALO * cells, own.shape[1]
-    last = planes // HALO - 1
-    block = pl.BlockSpec((rows, width), lambda i: (i * last, 0))
-    whole = pl.BlockSpec(gain.shape, lambda i: (0, 0))
-    message = (rows + HEAD, width)
-    return pl.pallas_call(
-        faces_kernel,
-        grid=(2,),
-        in_specs=[block, block, block, pl.BlockSpec((rows, LANES), lambda i: (i * last, 0)), whole, whole],
-        out_specs=[
-            pl.BlockSpec((1, rows, width), lambda i: (i, 0, 0)),
-            pl.BlockSpec(message, lambda i: (0, 0)),
-            pl.BlockSpec(message, lambda i: (0, 0)),
-        ],
-        out_shape=[
-            jax.ShapeDtypeStruct((2, rows, width), jnp.float32),
-            jax.ShapeDtypeStruct(message, jnp.float32),
-            jax.ShapeDtypeStruct(message, jnp.float32),
-        ],
-        compiler_params=params(),
+    message = jax.ShapeDtypeStruct((rows + HEAD, width), jnp.float32)
+    return pl.pallas_call(
+        functools.partial(faces_kernel, planes, cells),
+        in_specs=[resident()] * 6,
+        out_specs=[resident()] * 3,
+        out_shape=[jax.ShapeDtypeStruct((2, rows, width), jnp.float32), message, message],
+        compiler_params=params(grid=False),
         cost_estimate=cost(16 * rows * width * width, 30 * rows * width),
         name="faces",
     )(own, other, smoothed, rate, gain, product)
 
 
-def inside_kernel(own_ref, other_ref, smoothed_ref, rate_ref, gain_ref, product_ref, state_ref):
-    width = own_ref.shape[1]
+def inside_kernel(planes, cells, own_ref, other_ref, smoothed_ref, rate_ref, gain_ref, product_ref, after_ref, state_ref):
     group = 2 * LANES
-    for start in range(0, width, group):
+    rows = slice(HALO * cells, (planes - HALO) * cells)
+    lhs = joined(own_ref, other_ref, rows)
+    for start in range(0, own_ref.shape[1], group):
         columns = slice(start, start + group)
         state_ref[:, columns] = collided(
-            own_ref, other_ref, smoothed_ref[:, columns], own_ref[:, columns], rate_ref,
+            lhs, smoothed_ref[rows, columns], own_ref[rows, columns], rate_ref[rows, :],
             gain_ref, product_ref, columns,
         )
 
 
-def inside(own, other, smoothed, rate, gain, product, planes, cells):
-    rows, width = HALO * cells, own.shape[1]
-    count = planes // HALO - 2
-    block = pl.BlockSpec((rows, width), lambda i: (i + 1, 0))
-    whole = pl.BlockSpec(gain.shape, lambda i: (0, 0))
-    return pl.pallas_call(
-        inside_kernel,
-        grid=(count,),
-        in_specs=[block, block, block, pl.BlockSpec((rows, LANES), lambda i: (i + 1, 0)), whole, whole],
-        out_specs=pl.BlockSpec((rows, width), lambda i: (i, 0)),
-        out_shape=jax.ShapeDtypeStruct((count * rows, width), jnp.float32),
-        compiler_params=params(),
-        cost_estimate=cost(8 * count * rows * width * width, 20 * count * rows * width),
+def inside(own, other, smoothed, rate, gain, product, planes, cells, after):
+    rows, width = (planes - 2 * HALO) * cells, own.shape[1]
+    return pl.pallas_call(
+        functools.partial(inside_kernel, planes, cells),
+        in_specs=[resident()] * 6 + [anywhere()],
+        out_specs=resident(),
+        out_shape=jax.ShapeDtypeStruct((rows, width), jnp.float32),
+        compiler_params=params(grid=False),
+        cost_estimate=cost(8 * rows * width * width, 20 * rows * width),
         name="inside",
-    )(own, other, smoothed, rate, gain, product)
-
-
-def final_kernel(blocks, own_ref, other_ref, rounded_ref, smoothed_ref, rate_ref, gain_ref, product_ref, *refs):
-    outs, scratch = refs[:-1], refs[-1]
-    step = pl.program_id(0)
-    rows, group = smoothed_ref.shape
-    state = collided(
-        own_ref, other_ref, smoothed_ref[...], rounded_ref[...], rate_ref,
-        gain_ref, product_ref, slice(0, group),
-    )
-    scratch[pl.ds(pl.multiple_of(step * rows, rows), rows), :] = state
-
-    @pl.when(step == blocks - 1)
-    def _():
-        for index, out in enumerate(outs):
-            columns = slice(index * LANES, (index + 1) * LANES)
-
-            def peak(i, carry):
-                return jnp.maximum(
-                    carry, jnp.abs(scratch[pl.ds(pl.multiple_of(i * LANES, LANES), LANES), columns])
-                )
-
-            top = lax.fori_loop(0, blocks * rows // LANES, peak, jnp.zeros((LANES, LANES), jnp.float32))
-            power = exponent_of(jnp.max(top, axis=0, keepdims=True))
-            scale = jnp.exp2(power)
-
-            def write(i, carry):
-                where = pl.ds(pl.multiple_of(i * LANES, LANES), LANES)
-                out[where, :] = scratch[where, columns] * scale
-                return carry
-
-            lax.fori_loop(0, blocks * rows // LANES, write, 0)
-            out[blocks * rows :, :] = jnp.broadcast_to(power, (HEAD, LANES))
-
-
-def final(own, other, smoothed, rate, gain, product, planes, cells, part):
-    rows, width = HALO * cells, own.shape[1]
-    blocks = planes // HALO
+    )(own, other, smoothed, rate, gain, product, after)
+
+
+def final_kernel(part, own_ref, other_ref, smoothed_ref, rate_ref, gain_ref, product_ref, *refs):
+    outs, scratch = refs[1:-1], refs[-1]
+    rows, group = scratch.shape
+    columns = slice(part * group, (part + 1) * group)
+    size = 512 if rows % 512 == 0 else rows
+    for start in range(0, rows, size):
+        lines = slice(start, start + size)
+        scratch[lines, :] = collided(
+            joined(own_ref, other_ref, lines), smoothed_ref[lines, columns], own_ref[lines, columns],
+            rate_ref[lines, :], gain_ref, product_ref, columns,
+        )
+    for index, out in enumerate(outs):
+        lanes = slice(index * LANES, (index + 1) * LANES)
+
+        def block(i):
+            return pl.ds(pl.multiple_of(i * LANES, LANES), LANES)
+
+        def peak(i, carry):
+            return jnp.maximum(carry, jnp.abs(scratch[block(i), lanes]))
+
+        top = lax.fori_loop(0, rows // LANES, peak, jnp.zeros((LANES, LANES), jnp.float32))
+        power = exponent_of(jnp.max(top, axis=0, keepdims=True))
+        scale = jnp.exp2(power)
+
+        def write(i, carry):
+            out[block(i), :] = scratch[block(i), lanes] * scale
+            return carry
+
+        lax.fori_loop(0, rows // LANES, write, 0)
+        out[rows:, :] = jnp.broadcast_to(power, (HEAD, LANES))
+
+
+def final(own, other, smoothed, rate, gain, product, part, after):
+    rows, width = own.shape
     group = 2 * LANES
-    block = pl.BlockSpec((rows, width), lambda i: (i, 0))
-    narrow = pl.BlockSpec((rows, group), lambda i: (i, part))
-    matrix = pl.BlockSpec((group, gain.shape[1]), lambda i: (part, 0))
-    shape = (blocks * rows + HEAD, LANES)
-    return pl.pallas_call(
-        functools.partial(final_kernel, blocks),
-        grid=(blocks,),
-        in_specs=[block, block, narrow, narrow, pl.BlockSpec((rows, LANES), lambda i: (i, 0)), matrix, matrix],
-        out_specs=[pl.BlockSpec(shape, lambda i: (0, 0))] * 2,
-        out_shape=[jax.ShapeDtypeStruct(shape, jnp.float32)] * 2,
-        scratch_shapes=[pltpu.VMEM((blocks * rows, group), jnp.float32)],
-        compiler_params=params(),
-        cost_estimate=cost(8 * blocks * rows * width * group, 20 * blocks * rows * group),
+    shape = jax.ShapeDtypeStruct((rows + HEAD, LANES), jnp.float32)
+    return pl.pallas_call(
+        functools.partial(final_kernel, part),
+        in_specs=[resident()] * 6 + [anywhere()],
+        out_specs=[resident()] * 2,
+        out_shape=[shape] * 2,
+        scratch_shapes=[pltpu.VMEM((rows, group), jnp.float32)],
+        compiler_params=params(grid=False),
+        cost_estimate=cost(8 * rows * width * group, 20 * rows * group),
         name="final",
-    )(own, other, own, smoothed, rate, gain, product)
+    )(own, other, smoothed, rate, gain, product, after)
 
 
 def unpack_kernel(order, planes, cells, chip_ref, *refs):
@@ -594,22 +564,26 @@
 
     result = None
     states = []
+    after = product
     for k in range(CHUNKS):
-        up, down = messages_of(sent[k], cells)
+        up, down = messages_of(sent[k], cells, product)
         low, high = full(shift(half(up), 1)), full(shift(half(down), -1))
-        smoothed, rounded = transport(speeds, low, high, [spread(sent[k], planes, cells)], planes, cells)
+        local = [spread(sent[k], planes, cells)]
+        smoothed, rounded = transport(speeds, low, high, local, planes, cells, after)
         other = exchange(rounded, 1)
         ends, down, up = faces(rounded, other, smoothed, rates[k], gain, product, planes, cells)
         low, high = full(shift(half(up), 1)), full(shift(half(down), -1))
-        middle = inside(rounded, other, smoothed, rates[k], gain, product, planes, cells)
+        middle = inside(rounded, other, smoothed, rates[k], gain, product, planes, cells, ends)
         states.append((low, high, [ends, middle]))
+        after = middle
     for k in range(CHUNKS):
         low, high, parts = states[k]
-        smoothed, rounded = transport(speeds, low, high, parts, planes, cells)
+        smoothed, rounded = transport(speeds, low, high, parts, planes, cells, after)
         other = exchange(rounded, 1)
         ready = []
         for part in range(chips // 2):
-            ready += final(rounded, other, smoothed, rates[k], gain, product, planes, cells, part)
+            ready += final(rounded, other, smoothed, rates[k], gain, product, part, (ready or [gain])[0])
+        after = ready[-1]
         back = [a if m == 0 else full(exchange(half(a), 2 * m)) for a, m in zip(ready, order)]
         result = unpack(back, result, word, order, k, planes, cells)
     return result

time: 129 us -> 170 us (1.32)
  waiting for transfers between devices: 30 us -> 84.7 us
  local copies, waits for them, and re-layouts: 11.5 us -> 5.06 us
  starting transfers between devices: 33.7 us -> 27.7 us
  Pallas kernels: 48.2 us -> 45.4 us
    ppermute x8, waiting for transfers between devices: 7.16 us -> 47.7 us  [shift(): lax.ppermute(array, 'space', [(i, (i + step) % count) for i in range(coun...]
    ppermute x16, waiting for transfers between devices: 22.8 us -> 37 us  [exchange(): return lax.ppermute(array, 'vel', [(i, i ^ mask) for i in range(count)])]
    unnamed x32, local copies, waits for them, and re-layouts: 10.9 us -> 4.46 us
    pallas_call x13, Pallas kernels: 37 us -> 32.1 us  [the longest x4 12.7 us: transport(): pl.pallas_call(functools.partial(advect_kernel, planes, cells, 16, len(bo...]
    ppermute x8, starting transfers between devices: 15.8 us -> 11.9 us  [shift(): lax.ppermute(array, 'space', [(i, (i + step) % count) for i in range(coun...]
    pallas_call x2, Pallas kernels: 5.3 us -> 7.43 us  [pack(): pl.pallas_call(functools.partial(pack_kernel, order, planes, cells), grid...]
    ppermute x16, starting transfers between devices: 17.9 us -> 15.8 us  [exchange(): return lax.ppermute(array, 'vel', [(i, i ^ mask) for i in range(count)])]
  transfers between devices with their start and end apart: 24 -> 24, of which waited for: 7 -> 18; matrix products, arithmetic and copies ran while one was open for 4% -> 4% of each run, Pallas kernels for 33% -> 7%
where the time goes in v3:
time: 170 us; the launch traced here: 169 us
  waiting for transfers between devices  84.7 us (50%)
  Pallas kernels  45.4 us (27%)
  starting transfers between devices  27.7 us (16%)
  other arithmetic  6.01 us (4%)
  local copies, waits for them, and re-layouts  5.06 us (3%)
    ppermute x8, waiting for transfers between devices, shift(): lax.ppermute(array, 'space', [(i, (i + step) % count) for i in range(coun...  47.7 us
    ppermute x16, waiting for transfers between devices, exchange(): return lax.ppermute(array, 'vel', [(i, i ^ mask) for i in range(count)])  37 us
    ppermute x16, starting transfers between devices, exchange(): return lax.ppermute(array, 'vel', [(i, i ^ mask) for i in range(count)])  15.8 us
    pallas_call x4, Pallas kernels, transport(): pl.pallas_call(functools.partial(advect_kernel, planes, cells, 16, len(bo...  12.7 us
    ppermute x8, starting transfers between devices, shift(): lax.ppermute(array, 'space', [(i, (i + step) % count) for i in range(coun...  11.9 us
    pallas_call x2, Pallas kernels, pack(): pl.pallas_call(functools.partial(pack_kernel, order, planes, cells), grid...  7.43 us
    pallas_call x4, Pallas kernels, final(): pl.pallas_call(functools.partial(final_kernel, part), in_specs=[resident(...  6.48 us
    pallas_call x2, Pallas kernels, faces(): pl.pallas_call(functools.partial(faces_kernel, planes, cells), in_specs=[...  5.97 us
  transfers between devices with their start and end apart: 24, of which 18 were waited for; matrix products, arithmetic and copies ran while one was open for 4% of the time, Pallas kernels for 7%

profile of v3, /device:TPU:0, one launch (start us, length us, event | category | flops | bytes accessed | tf_op | source)
XLA Modules:
  0.0 169.5 jit_solution(16754204664659581942)
XLA Ops:
  0.1 3.7 %pack.3 = (f32[1040,128]{1,0:T(8,128)S(1)}, f32[1040,128]{1,0:T(8,128)S(1)}, f32[1040,128]{1,0:T(8,128)S(1)}, f32[1040,128]{1,0:T(8,128)S(1)}) custom-call(s32[2]{0:T(128)S(1)} %pad_add_fusion.word_ref.chip_ref, f32[128,16,512]{2,1,0:T(8,128)} %d_ref.3), custom_call_target="tpu_custom_call" | custom-call | flops 1000000 | bytes 4194304 | tf_op jit(solution)/shard_map/pack/pallas_call | solution.py:172
  3.8 4.0 %collective-permute-start.7 = (f16[1040,128]{1,0:T(8,128)(2,1)S(1)}, f16[1040,128]{1,0:T(8,128)(2,1)S(1)}, u32[]{:S(2)}, u32[]{:S(2)}) collective-permute-start(f16[1040,128]{1,0:T(8,128)(2,1)S(1)} %convert_element_type.134), channel_id=1, source_target_pairs={{0,24},{4,28},{8,16},{12,20},{16,8},{20,12},{24,0},{28,4},{1,25},{... | collective-permute-start | bytes 798728 | tf_op jit(solution)/shard_map/ppermute | solution.py:527
  9.7 5.4 %collective-permute-done.7 = f16[1040,128]{1,0:T(8,128)(2,1)S(1)} collective-permute-done((f16[1040,128]{1,0:T(8,128)(2,1)S(1)}, f16[1040,128]{1,0:T(8,128)(2,1)S(1)}, u32[]{:S(2)}, u32[]{:S(2)}) %collective-permute-start.7) | collective-permute-done | bytes 266272 | tf_op jit(solution)/shard_map/ppermute | solution.py:527
  15.1 4.8 %collective-permute-done.6 = f16[1040,128]{1,0:T(8,128)(2,1)S(1)} collective-permute-done((f16[1040,128]{1,0:T(8,128)(2,1)S(1)}, f16[1040,128]{1,0:T(8,128)(2,1)S(1)}, u32[]{:S(2)}, u32[]{:S(2)}) %collective-permute-start.6) | collective-permute-done | bytes 266272 | tf_op jit(solution)/shard_map/ppermute | solution.py:527
  20.4 3.7 %collective-permute-start.9 = (f16[272,512]{1,0:T(8,128)(2,1)S(1)}, f16[272,512]{1,0:T(8,128)(2,1)S(1)}, u32[]{:S(2)}, u32[]{:S(2)}) collective-permute-start(f16[272,512]{1,0:T(8,128)(2,1)S(1)} %convert_element_type.138), channel_id=1, source_target_pairs={{0,3},{1,0},{2,1},{3,2},{4,7},{5,4},{6,5},{7,6},{8,11},{9,8},{10,9... | collective-permute-start | bytes 835592 | tf_op jit(solution)/shard_map/ppermute | solution.py:532
  24.5 6.7 %collective-permute-done.9 = f16[272,512]{1,0:T(8,128)(2,1)S(1)} collective-permute-done((f16[272,512]{1,0:T(8,128)(2,1)S(1)}, f16[272,512]{1,0:T(8,128)(2,1)S(1)}, u32[]{:S(2)}, u32[]{:S(2)}) %collective-permute-start.9) | collective-permute-done | bytes 278560 | tf_op jit(solution)/shard_map/ppermute | solution.py:532
  31.2 5.8 %collective-permute-done.8 = f16[272,512]{1,0:T(8,128)(2,1)S(1)} collective-permute-done((f16[272,512]{1,0:T(8,128)(2,1)S(1)}, f16[272,512]{1,0:T(8,128)(2,1)S(1)}, u32[]{:S(2)}, u32[]{:S(2)}) %collective-permute-start.8) | collective-permute-done | bytes 278560 | tf_op jit(solution)/shard_map/ppermute | solution.py:532
  37.1 3.6 %transport.4 = (f32[1024,512]{1,0:T(8,128)S(1)}, bf16[1024,512]{1,0:T(8,128)(2,1)}) custom-call(f32[8,512]{1,0:T(8,128)S(1)} %get-tuple-element.42.c_ref, f32[272,512]{1,0:T(8,128)S(1)} %convert_element_type.137.low_ref, f32[272,512]{1,0:T(8,128)S(1)} %convert_element_type.139.high_ref, f32[1024,512]{1,0:T(8,128)S(1)} %spread.3.refs_0_, ...), custom_call_target="tpu_custom_call" | custom-call | flops 20971520 | bytes 6291456 | tf_op jit(solution)/shard_map/transport/pallas_call | solution.py:334
  40.7 3.8 %pack.2 = (f32[1040,128]{1,0:T(8,128)S(1)}, f32[1040,128]{1,0:T(8,128)S(1)}, f32[1040,128]{1,0:T(8,128)S(1)}, f32[1040,128]{1,0:T(8,128)S(1)}) custom-call(s32[2]{0:T(128)S(1)} %pad_add_fusion.word_ref.chip_ref, f32[128,16,512]{2,1,0:T(8,128)} %d_ref.3), custom_call_target="tpu_custom_call" | custom-call | flops 1000000 | bytes 4194304 | tf_op jit(solution)/shard_map/pack/pallas_call | solution.py:172
  48.3 6.5 %collective-permute-done.2 = f16[1040,128]{1,0:T(8,128)(2,1)S(1)} collective-permute-done((f16[1040,128]{1,0:T(8,128)(2,1)S(1)}, f16[1040,128]{1,0:T(8,128)(2,1)S(1)}, u32[]{:S(2)}, u32[]{:S(2)}) %collective-permute-start.2) | collective-permute-done | bytes 266272 | tf_op jit(solution)/shard_map/ppermute | solution.py:527
  54.8 5.0 %collective-permute-done.1 = f16[1040,128]{1,0:T(8,128)(2,1)S(1)} collective-permute-done((f16[1040,128]{1,0:T(8,128)(2,1)S(1)}, f16[1040,128]{1,0:T(8,128)(2,1)S(1)}, u32[]{:S(2)}, u32[]{:S(2)}) %collective-permute-start.1) | collective-permute-done | bytes 266272 | tf_op jit(solution)/shard_map/ppermute | solution.py:527
  65.6 4.0 %collective-permute-done.4 = f16[272,512]{1,0:T(8,128)(2,1)} collective-permute-done((f16[272,512]{1,0:T(8,128)(2,1)S(1)}, f16[272,512]{1,0:T(8,128)(2,1)}, u32[]{:S(2)}, u32[]{:S(2)}) %collective-permute-start.4) | collective-permute-done | bytes 278560 | tf_op jit(solution)/shard_map/ppermute | solution.py:532
  70.6 4.6 %collective-permute-done.3 = f16[272,512]{1,0:T(8,128)(2,1)} collective-permute-done((f16[272,512]{1,0:T(8,128)(2,1)}, f16[272,512]{1,0:T(8,128)(2,1)}, u32[]{:S(2)}, u32[]{:S(2)}) %collective-permute-start.3) | collective-permute-done | bytes 278560 | tf_op jit(solution)/shard_map/ppermute | solution.py:532
  76.5 3.0 %faces.2 = (f32[2,256,512]{2,1,0:T(8,128)S(1)}, f32[272,512]{1,0:T(8,128)S(1)}, f32[272,512]{1,0:T(8,128)S(1)}) custom-call(bf16[1024,512]{1,0:T(8,128)(2,1)} %get-tuple-element.56.own_ref, bf16[1024,512]{1,0:T(8,128)(2,1)} %collective-permute-done.10.other_ref, f32[1024,512]{1,0:T(8,128)S(1)} %copy-done.3, f32[1024,128]{1,0:T(8,128)S(1)} %broadcast_in_dim.15.rate_ref, ...), custom_call_target="tpu_custom_call" | custom-call | flops 1073741824 | bytes 3932160 | tf_op jit(solution)/shard_map/faces/pallas_call | solution.py:391
  83.3 3.6 %transport.5 = (f32[1024,512]{1,0:T(8,128)S(1)}, bf16[1024,512]{1,0:T(8,128)(2,1)}) custom-call(f32[8,512]{1,0:T(8,128)S(1)} %get-tuple-element.42.c_ref, f32[272,512]{1,0:T(8,128)S(1)} %convert_element_type.127.low_ref, f32[272,512]{1,0:T(8,128)S(1)} %convert_element_type.129.high_ref, f32[1024,512]{1,0:T(8,128)S(1)} %spread.2.refs_0_, ...), custom_call_target="tpu_custom_call" | custom-call | flops 20971520 | bytes 6291456 | tf_op jit(solution)/shard_map/transport/pallas_call | solution.py:334
  88.3 3.2 %collective-permute-start.15 = (f16[272,512]{1,0:T(8,128)(2,1)S(1)}, f16[272,512]{1,0:T(8,128)(2,1)S(1)}, u32[]{:S(2)}, u32[]{:S(2)}) collective-permute-start(f16[272,512]{1,0:T(8,128)(2,1)S(1)} %convert_element_type.146), channel_id=1, source_target_pairs={{0,3},{1,0},{2,1},{3,2},{4,7},{5,4},{6,5},{7,6},{8,11},{9,8},{10,9... | collective-permute-start | bytes 835592 | tf_op jit(solution)/shard_map/ppermute | solution.py:532
  92.3 6.2 %collective-permute-done.15 = f16[272,512]{1,0:T(8,128)(2,1)S(1)} collective-permute-done((f16[272,512]{1,0:T(8,128)(2,1)S(1)}, f16[272,512]{1,0:T(8,128)(2,1)S(1)}, u32[]{:S(2)}, u32[]{:S(2)}) %collective-permute-start.15) | collective-permute-done | bytes 278560 | tf_op jit(solution)/shard_map/ppermute | solution.py:532
  98.5 6.8 %collective-permute-done.14 = f16[272,512]{1,0:T(8,128)(2,1)} collective-permute-done((f16[272,512]{1,0:T(8,128)(2,1)}, f16[272,512]{1,0:T(8,128)(2,1)}, u32[]{:S(2)}, u32[]{:S(2)}) %collective-permute-start.14) | collective-permute-done | bytes 278560 | tf_op jit(solution)/shard_map/ppermute | solution.py:532
  106.6 3.0 %faces.3 = (f32[2,256,512]{2,1,0:T(8,128)S(1)}, f32[272,512]{1,0:T(8,128)S(1)}, f32[272,512]{1,0:T(8,128)S(1)}) custom-call(bf16[1024,512]{1,0:T(8,128)(2,1)} %get-tuple-element.60.own_ref, bf16[1024,512]{1,0:T(8,128)(2,1)} %collective-permute-done.11.other_ref, f32[1024,512]{1,0:T(8,128)S(1)} %copy-done.5, f32[1024,128]{1,0:T(8,128)S(1)} %broadcast_in_dim.17.rate_ref, ...), custom_call_target="tpu_custom_call" | custom-call | flops 1073741824 | bytes 3932160 | tf_op jit(solution)/shard_map/faces/pallas_call | solution.py:391
  109.6 3.0 %inside.3.refs_2_.refs_1_ = f32[512,512]{1,0:T(8,128)S(1)} custom-call(bf16[1024,512]{1,0:T(8,128)(2,1)} %get-tuple-element.60.own_ref, bf16[1024,512]{1,0:T(8,128)(2,1)} %collective-permute-done.11.other_ref, f32[1024,512]{1,0:T(8,128)S(1)} %copy-done.5, f32[1024,128]{1,0:T(8,128)S(1)} %broadcast_in_dim.17.rate_ref, ...), custom_call_target="tpu_custom_call" | custom-call | flops 1073741824 | bytes 5242880 | tf_op jit(solution)/shard_map/inside/pallas_call | solution.py:416
  118.5 6.7 %collective-permute-done.13 = f16[272,512]{1,0:T(8,128)(2,1)S(1)} collective-permute-done((f16[272,512]{1,0:T(8,128)(2,1)S(1)}, f16[272,512]{1,0:T(8,128)(2,1)S(1)}, u32[]{:S(2)}, u32[]{:S(2)}) %collective-permute-start.13) | collective-permute-done | bytes 278560 | tf_op jit(solution)/shard_map/ppermute | solution.py:532
  125.3 6.8 %collective-permute-done.12 = f16[272,512]{1,0:T(8,128)(2,1)S(1)} collective-permute-done((f16[272,512]{1,0:T(8,128)(2,1)S(1)}, f16[272,512]{1,0:T(8,128)(2,1)S(1)}, u32[]{:S(2)}, u32[]{:S(2)}) %collective-permute-start.12) | collective-permute-done | bytes 278560 | tf_op jit(solution)/shard_map/ppermute | solution.py:532
  149.2 5.1 %collective-permute-done.23 = f16[1040,128]{1,0:T(8,128)(2,1)S(1)} collective-permute-done((f16[1040,128]{1,0:T(8,128)(2,1)S(1)}, f16[1040,128]{1,0:T(8,128)(2,1)S(1)}, u32[]{:S(2)}, u32[]{:S(2)}) %collective-permute-start.23) | collective-permute-done | bytes 266272 | tf_op jit(solution)/shard_map/ppermute | solution.py:527
  159.1 6.3 %collective-permute-done.20 = f16[1040,128]{1,0:T(8,128)(2,1)S(1)} collective-permute-done((f16[1040,128]{1,0:T(8,128)(2,1)S(1)}, f16[1040,128]{1,0:T(8,128)(2,1)S(1)}, u32[]{:S(2)}, u32[]{:S(2)}) %collective-permute-start.20) | collective-permute-done | bytes 266272 | tf_op jit(solution)/shard_map/ppermute | solution.py:527
  (123 shorter events, 53.7 us)
Async XLA Ops:
  3.8 11.2 %collective-permute-start.7 = (f16[1040,128]{1,0:T(8,128)(2,1)S(1)}, f16[1040,128]{1,0:T(8,128)(2,1)S(1)}, u32[]{:S(2)}, u32[]{:S(2)}) collective-permute-start(f16[1040,128]{1,0:T(8,128)(2,1)S(1)} %convert_element_type.134), channel_id=1, source_target_pairs={{0,24},{4,28},{8,16},{12,20},{16,8},{20,12},{24,0},{28,4},{1,25},{... | collective-permute-start | bytes 798728 | tf_op jit(solution)/shard_map/ppermute | solution.py:527
  7.8 12.1 %collective-permute-start.6 = (f16[1040,128]{1,0:T(8,128)(2,1)S(1)}, f16[1040,128]{1,0:T(8,128)(2,1)S(1)}, u32[]{:S(2)}, u32[]{:S(2)}) collective-permute-start(f16[1040,128]{1,0:T(8,128)(2,1)S(1)} %convert_element_type.132), channel_id=1, source_target_pairs={{0,16},{4,20},{8,24},{12,28},{16,0},{20,4},{24,8},{28,12},{1,17},{... | collective-permute-start | bytes 798728 | tf_op jit(solution)/shard_map/ppermute | solution.py:527
  8.4 11.7 %collective-permute-start.5 = (f16[1040,128]{1,0:T(8,128)(2,1)S(1)}, f16[1040,128]{1,0:T(8,128)(2,1)S(1)}, u32[]{:S(2)}, u32[]{:S(2)}) collective-permute-start(f16[1040,128]{1,0:T(8,128)(2,1)S(1)} %convert_element_type.130), channel_id=1, source_target_pairs={{0,8},{4,12},{8,0},{12,4},{16,24},{20,28},{24,16},{28,20},{1,9},{5... | collective-permute-start | bytes 798728 | tf_op jit(solution)/shard_map/ppermute | solution.py:527
  20.4 10.7 %collective-permute-start.9 = (f16[272,512]{1,0:T(8,128)(2,1)S(1)}, f16[272,512]{1,0:T(8,128)(2,1)S(1)}, u32[]{:S(2)}, u32[]{:S(2)}) collective-permute-start(f16[272,512]{1,0:T(8,128)(2,1)S(1)} %convert_element_type.138), channel_id=1, source_target_pairs={{0,3},{1,0},{2,1},{3,2},{4,7},{5,4},{6,5},{7,6},{8,11},{9,8},{10,9... | collective-permute-start | bytes 835592 | tf_op jit(solution)/shard_map/ppermute | solution.py:532
  24.1 12.9 %collective-permute-start.8 = (f16[272,512]{1,0:T(8,128)(2,1)S(1)}, f16[272,512]{1,0:T(8,128)(2,1)S(1)}, u32[]{:S(2)}, u32[]{:S(2)}) collective-permute-start(f16[272,512]{1,0:T(8,128)(2,1)S(1)} %convert_element_type.136), channel_id=1, source_target_pairs={{0,1},{1,2},{2,3},{3,0},{4,5},{5,6},{6,7},{7,4},{8,9},{9,10},{10,1... | collective-permute-start | bytes 835592 | tf_op jit(solution)/shard_map/ppermute | solution.py:532
  40.7 35.6 %collective-permute-start.10 = (bf16[1024,512]{1,0:T(8,128)(2,1)}, bf16[1024,512]{1,0:T(8,128)(2,1)}, u32[]{:S(2)}, u32[]{:S(2)}) collective-permute-start(bf16[1024,512]{1,0:T(8,128)(2,1)} %get-tuple-element.56.own_ref), channel_id=1, source_target_pairs={{0,4},{4,0},{8,12},{12,8},{16,20},{20,16},{24,28},{28,24},{1,5},{5... | collective-permute-start | bytes 3145736 | tf_op jit(solution)/shard_map/ppermute | solution.py:527
  44.5 10.2 %collective-permute-start.2 = (f16[1040,128]{1,0:T(8,128)(2,1)S(1)}, f16[1040,128]{1,0:T(8,128)(2,1)S(1)}, u32[]{:S(2)}, u32[]{:S(2)}) collective-permute-start(f16[1040,128]{1,0:T(8,128)(2,1)S(1)} %convert_element_type.124), channel_id=1, source_target_pairs={{0,24},{4,28},{8,16},{12,20},{16,8},{20,12},{24,0},{28,4},{1,25},{... | collective-permute-start | bytes 798728 | tf_op jit(solution)/shard_map/ppermute | solution.py:527
  45.9 14.0 %collective-permute-start.1 = (f16[1040,128]{1,0:T(8,128)(2,1)S(1)}, f16[1040,128]{1,0:T(8,128)(2,1)S(1)}, u32[]{:S(2)}, u32[]{:S(2)}) collective-permute-start(f16[1040,128]{1,0:T(8,128)(2,1)S(1)} %convert_element_type.122), channel_id=1, source_target_pairs={{0,16},{4,20},{8,24},{12,28},{16,0},{20,4},{24,8},{28,12},{1,17},{... | collective-permute-start | bytes 798728 | tf_op jit(solution)/shard_map/ppermute | solution.py:527
  47.7 12.2 %collective-permute-start = (f16[1040,128]{1,0:T(8,128)(2,1)S(1)}, f16[1040,128]{1,0:T(8,128)(2,1)S(1)}, u32[]{:S(2)}, u32[]{:S(2)}) collective-permute-start(f16[1040,128]{1,0:T(8,128)(2,1)S(1)} %convert_element_type.120), channel_id=1, source_target_pairs={{0,8},{4,12},{8,0},{12,4},{16,24},{20,28},{24,16},{28,20},{1,9},{5... | collective-permute-start | bytes 798728 | tf_op jit(solution)/shard_map/ppermute | solution.py:527
  60.2 9.4 %collective-permute-start.4 = (f16[272,512]{1,0:T(8,128)(2,1)S(1)}, f16[272,512]{1,0:T(8,128)(2,1)}, u32[]{:S(2)}, u32[]{:S(2)}) collective-permute-start(f16[272,512]{1,0:T(8,128)(2,1)S(1)} %convert_element_type.128), channel_id=1, source_target_pairs={{0,3},{1,0},{2,1},{3,2},{4,7},{5,4},{6,5},{7,6},{8,11},{9,8},{10,9... | collective-permute-start | bytes 835592 | tf_op jit(solution)/shard_map/ppermute | solution.py:532
  62.8 12.4 %collective-permute-start.3 = (f16[272,512]{1,0:T(8,128)(2,1)}, f16[272,512]{1,0:T(8,128)(2,1)}, u32[]{:S(2)}, u32[]{:S(2)}) collective-permute-start(f16[272,512]{1,0:T(8,128)(2,1)} %convert_element_type.126), channel_id=1, source_target_pairs={{0,1},{1,2},{2,3},{3,0},{4,5},{5,6},{6,7},{7,4},{8,9},{9,10},{10,1... | collective-permute-start | bytes 835592 | tf_op jit(solution)/shard_map/ppermute | solution.py:532
  88.3 18.1 %collective-permute-start.11 = (bf16[1024,512]{1,0:T(8,128)(2,1)}, bf16[1024,512]{1,0:T(8,128)(2,1)}, u32[]{:S(2)}, u32[]{:S(2)}) collective-permute-start(bf16[1024,512]{1,0:T(8,128)(2,1)} %get-tuple-element.60.own_ref), channel_id=1, source_target_pairs={{0,4},{4,0},{8,12},{12,8},{16,20},{20,16},{24,28},{28,24},{1,5},{5... | collective-permute-start | bytes 3145736 | tf_op jit(solution)/shard_map/ppermute | solution.py:527
  88.3 10.2 %collective-permute-start.15 = (f16[272,512]{1,0:T(8,128)(2,1)S(1)}, f16[272,512]{1,0:T(8,128)(2,1)S(1)}, u32[]{:S(2)}, u32[]{:S(2)}) collective-permute-start(f16[272,512]{1,0:T(8,128)(2,1)S(1)} %convert_element_type.146), channel_id=1, source_target_pairs={{0,3},{1,0},{2,1},{3,2},{4,7},{5,4},{6,5},{7,6},{8,11},{9,8},{10,9... | collective-permute-start | bytes 835592 | tf_op jit(solution)/shard_map/ppermute | solution.py:532
  92.2 13.2 %collective-permute-start.14 = (f16[272,512]{1,0:T(8,128)(2,1)}, f16[272,512]{1,0:T(8,128)(2,1)}, u32[]{:S(2)}, u32[]{:S(2)}) collective-permute-start(f16[272,512]{1,0:T(8,128)(2,1)} %convert_element_type.144), channel_id=1, source_target_pairs={{0,1},{1,2},{2,3},{3,0},{4,5},{5,6},{6,7},{7,4},{8,9},{9,10},{10,1... | collective-permute-start | bytes 835592 | tf_op jit(solution)/shard_map/ppermute | solution.py:532
  115.3 16.9 %collective-permute-start.16 = (bf16[1024,512]{1,0:T(8,128)(2,1)S(1)}, bf16[1024,512]{1,0:T(8,128)(2,1)S(1)}, u32[]{:S(2)}, u32[]{:S(2)}) collective-permute-start(bf16[1024,512]{1,0:T(8,128)(2,1)S(1)} %get-tuple-element.67.own_ref), channel_id=1, source_target_pairs={{0,4},{4,0},{8,12},{12,8},{16,20},{20,16},{24,28},{28,24},{1,5},{5... | collective-permute-start | bytes 3145736 | tf_op jit(solution)/shard_map/ppermute | solution.py:527
  115.5 9.8 %collective-permute-start.13 = (f16[272,512]{1,0:T(8,128)(2,1)S(1)}, f16[272,512]{1,0:T(8,128)(2,1)S(1)}, u32[]{:S(2)}, u32[]{:S(2)}) collective-permute-start(f16[272,512]{1,0:T(8,128)(2,1)S(1)} %convert_element_type.142), channel_id=1, source_target_pairs={{0,3},{1,0},{2,1},{3,2},{4,7},{5,4},{6,5},{7,6},{8,11},{9,8},{10,9... | collective-permute-start | bytes 835592 | tf_op jit(solution)/shard_map/ppermute | solution.py:532
  118.3 13.9 %collective-permute-start.12 = (f16[272,512]{1,0:T(8,128)(2,1)S(1)}, f16[272,512]{1,0:T(8,128)(2,1)S(1)}, u32[]{:S(2)}, u32[]{:S(2)}) collective-permute-start(f16[272,512]{1,0:T(8,128)(2,1)S(1)} %convert_element_type.140), channel_id=1, source_target_pairs={{0,1},{1,2},{2,3},{3,0},{4,5},{5,6},{6,7},{7,4},{8,9},{9,10},{10,1... | collective-permute-start | bytes 835592 | tf_op jit(solution)/shard_map/ppermute | solution.py:532
  138.2 3.8 %collective-permute-start.17 = (bf16[1024,512]{1,0:T(8,128)(2,1)S(1)}, bf16[1024,512]{1,0:T(8,128)(2,1)S(1)}, u32[]{:S(2)}, u32[]{:S(2)}) collective-permute-start(bf16[1024,512]{1,0:T(8,128)(2,1)S(1)} %get-tuple-element.71.own_ref), channel_id=1, source_target_pairs={{0,4},{4,0},{8,12},{12,8},{16,20},{20,16},{24,28},{28,24},{1,5},{5... | collective-permute-start | bytes 3145736 | tf_op jit(solution)/shard_map/ppermute | solution.py:527
  138.3 10.2 %collective-permute-start.21 = (f16[1040,128]{1,0:T(8,128)(2,1)S(1)}, f16[1040,128]{1,0:T(8,128)(2,1)S(1)}, u32[]{:S(2)}, u32[]{:S(2)}) collective-permute-start(f16[1040,128]{1,0:T(8,128)(2,1)S(1)} %convert_element_type.154), channel_id=1, source_target_pairs={{0,8},{4,12},{8,0},{12,4},{16,24},{20,28},{24,16},{28,20},{1,9},{5... | collective-permute-start | bytes 798728 | tf_op jit(solution)/shard_map/ppermute | solution.py:527
  140.0 14.3 %collective-permute-start.23 = (f16[1040,128]{1,0:T(8,128)(2,1)S(1)}, f16[1040,128]{1,0:T(8,128)(2,1)S(1)}, u32[]{:S(2)}, u32[]{:S(2)}) collective-permute-start(f16[1040,128]{1,0:T(8,128)(2,1)S(1)} %convert_element_type.158), channel_id=1, source_target_pairs={{0,24},{4,28},{8,16},{12,20},{16,8},{20,12},{24,0},{28,4},{1,25},{... | collective-permute-start | bytes 798728 | tf_op jit(solution)/shard_map/ppermute | solution.py:527
  141.5 15.0 %collective-permute-start.22 = (f16[1040,128]{1,0:T(8,128)(2,1)S(1)}, f16[1040,128]{1,0:T(8,128)(2,1)S(1)}, u32[]{:S(2)}, u32[]{:S(2)}) collective-permute-start(f16[1040,128]{1,0:T(8,128)(2,1)S(1)} %convert_element_type.156), channel_id=1, source_target_pairs={{0,16},{4,20},{8,24},{12,28},{16,0},{20,4},{24,8},{28,12},{1,17},{... | collective-permute-start | bytes 798728 | tf_op jit(solution)/shard_map/ppermute | solution.py:527
  143.8 15.3 %collective-permute-start.18 = (f16[1040,128]{1,0:T(8,128)(2,1)S(1)}, f16[1040,128]{1,0:T(8,128)(2,1)S(1)}, u32[]{:S(2)}, u32[]{:S(2)}) collective-permute-start(f16[1040,128]{1,0:T(8,128)(2,1)S(1)} %convert_element_type.148), channel_id=1, source_target_pairs={{0,8},{4,12},{8,0},{12,4},{16,24},{20,28},{24,16},{28,20},{1,9},{5... | collective-permute-start | bytes 798728 | tf_op jit(solution)/shard_map/ppermute | solution.py:527
  147.0 18.4 %collective-permute-start.20 = (f16[1040,128]{1,0:T(8,128)(2,1)S(1)}, f16[1040,128]{1,0:T(8,128)(2,1)S(1)}, u32[]{:S(2)}, u32[]{:S(2)}) collective-permute-start(f16[1040,128]{1,0:T(8,128)(2,1)S(1)} %convert_element_type.152), channel_id=1, source_target_pairs={{0,24},{4,28},{8,16},{12,20},{16,8},{20,12},{24,0},{28,4},{1,25},{... | collective-permute-start | bytes 798728 | tf_op jit(solution)/shard_map/ppermute | solution.py:527
  148.6 18.3 %collective-permute-start.19 = (f16[1040,128]{1,0:T(8,128)(2,1)S(1)}, f16[1040,128]{1,0:T(8,128)(2,1)S(1)}, u32[]{:S(2)}, u32[]{:S(2)}) collective-permute-start(f16[1040,128]{1,0:T(8,128)(2,1)S(1)} %convert_element_type.150), channel_id=1, source_target_pairs={{0,16},{4,20},{8,24},{12,28},{16,0},{20,4},{24,8},{28,12},{1,17},{... | collective-permute-start | bytes 798728 | tf_op jit(solution)/shard_map/ppermute | solution.py:527
  (16 other events, 82.6 us)

commit v4 on v3

v4 whole, which is shorter than its diff:
```python
import functools

import jax
import jax.numpy as jnp
from jax import lax
from jax.experimental import pallas as pl
from jax.experimental.pallas import tpu as pltpu
from jax.sharding import PartitionSpec as P

STEPS = 2
HALO = 4
WIDE = 2 * HALO
HEAD = 16
CHUNKS = 2
LANES = 128
QUARTERS = 4
VMEM = 12 * 1024 * 1024

time_step = 0.2


def with_halo(block, sides, width):
    for axis, dim in sides:
        count = lax.axis_size(axis)
        forward = [(i, i + 1) for i in range(count - 1)]
        forward.append((count - 1, 0))
        backward = [(target, source) for source, target in forward]
        low = lax.ppermute(
            lax.slice_in_dim(block, block.shape[dim] - width, None, axis=dim), axis, forward
        )
        high = lax.ppermute(lax.slice_in_dim(block, 0, width, axis=dim), axis, backward)
        block = jnp.concatenate([low, block, high], axis=dim)
    return block


def minmod(first, second):
    return jnp.maximum(jnp.minimum(first, second), 0.0) + jnp.minimum(
        jnp.maximum(first, second), 0.0
    )


def change(widened, speeds):
    differ = widened[:, 1:] - widened[:, :-1]
    slopes = minmod(differ[:, 1:], differ[:, :-1])
    inner = widened.shape[1] - 4
    left_value = widened[:, 1 : inner + 2]
    right_value = widened[:, 2 : inner + 3]
    left_slope = slopes[:, 0 : inner + 1]
    right_slope = slopes[:, 1 : inner + 2]
    upward = jnp.maximum(speeds, 0.0)
    downward = jnp.minimum(speeds, 0.0)
    fluxes = upward * (left_value + 0.5 * (1.0 - speeds) * left_slope) + downward * (
        right_value - 0.5 * (1.0 + speeds) * right_slope
    )
    return -(fluxes[:, 1:] - fluxes[:, :-1])


def extend(field):
    return with_halo(field, (("space", 1),), 2)


def advect(field, speeds):
    section = field + change(extend(field), speeds)
    return 0.5 * field + 0.5 * (section + change(extend(section), speeds))


def collide(pieces, gain_matrix, product_matrix):
    columns = pieces.reshape(pieces.shape[0], -1)
    first_term = jnp.dot(gain_matrix, columns, preferred_element_type=jnp.float32)
    second_term = jnp.dot(product_matrix, columns, preferred_element_type=jnp.float32)
    return (first_term * second_term).astype(jnp.bfloat16).reshape(pieces.shape)


def update(smoothed, rounded, gained, rate):
    return smoothed + time_step * (gained.astype(jnp.float32) - rate * rounded.astype(jnp.float32))


def general_body(distribution, courant, gain_matrix, product_matrix, collision_rate):
    local_count = distribution.shape[0]
    groups = lax.axis_size("vel")
    member = lax.axis_index("vel")
    own_speeds = lax.dynamic_slice_in_dim(courant, member * local_count, local_count, 0)[
        :, None, None
    ]
    field = distribution
    for step_index in range(STEPS):
        smoothed = advect(field, own_speeds)
        rounded = smoothed.astype(jnp.bfloat16)
        grouped = rounded.reshape(local_count, groups, -1)
        gained = lax.all_to_all(
            collide(
                lax.all_to_all(grouped, "vel", split_axis=1, concat_axis=0, tiled=True),
                gain_matrix,
                product_matrix,
            ),
            "vel",
            split_axis=0,
            concat_axis=1,
            tiled=True,
        )
        field = update(smoothed, rounded, gained.reshape(rounded.shape), collision_rate[None])
    return field


def params(fusable=None, grid=True):
    return pltpu.CompilerParams(
        dimension_semantics=("arbitrary",) if grid else None,
        vmem_limit_bytes=VMEM,
        allow_input_fusion=fusable,
    )


def resident():
    return pl.BlockSpec(memory_space=pltpu.VMEM)


def anywhere():
    return pl.BlockSpec(memory_space=pl.ANY)


def cost(flops, moved):
    return pl.CostEstimate(flops=1000, bytes_accessed=1000, transcendentals=0)


def exponent_of(largest):
    power = jnp.floor(14.0 - jnp.log2(jnp.maximum(largest, 1e-36)))
    return jnp.clip(power, -115.0, 120.0)


def pack_kernel(order, planes, cells, chip_ref, d_ref, after_ref, *refs):
    outs, scratch = refs[:-1], refs[-1]
    chip = chip_ref[0]
    step = pl.program_id(0)
    rows = d_ref.reshape(LANES * planes, LANES)
    for x in range(planes):
        part = rows[pl.ds(x, LANES, stride=planes), :]
        scratch[x, pl.ds(pl.multiple_of(step * LANES, LANES), LANES), :] = part.T

    @pl.when(step == pl.num_programs(0) - 1)
    def _():
        for mask, out in zip(order, outs):
            first = pl.multiple_of((chip ^ mask) * cells, cells)

            def peak(x, carry):
                return jnp.maximum(carry, jnp.abs(scratch[x, pl.ds(first, cells), :]))

            top = lax.fori_loop(0, planes, peak, jnp.zeros((cells, LANES), jnp.float32))
            power = exponent_of(jnp.max(top, axis=0, keepdims=True))
            scale = jnp.exp2(power)

            def write(x, carry):
                start = place_of(x, cells)
                out[pl.ds(pl.multiple_of(start, 16), cells), :] = (
                    scratch[x, pl.ds(first, cells), :] * scale
                )
                return carry

            lax.fori_loop(0, planes, write, 0)
            out[WIDE * cells : WIDE * cells + HEAD, :] = jnp.broadcast_to(power, (HEAD, LANES))


def place_of(x, cells):
    if isinstance(x, int):
        return x * cells + (HEAD if x >= WIDE else 0)
    return x * cells + jnp.where(x >= WIDE, HEAD, 0)


def pack(distribution, chip, order, chunk, cells, after):
    planes = distribution.shape[1]
    width = cells * len(order)
    steps = width // LANES
    shape = (planes * cells + HEAD, LANES)
    return pl.pallas_call(
        functools.partial(pack_kernel, order, planes, cells),
        grid_spec=pltpu.PrefetchScalarGridSpec(
            num_scalar_prefetch=1,
            grid=(steps,),
            in_specs=[
                pl.BlockSpec((LANES, planes, LANES), lambda i, s: (0, 0, chunk * steps + i)),
                anywhere(),
            ],
            out_specs=[resident() for _ in order],
            scratch_shapes=[pltpu.VMEM((planes, width, LANES), jnp.float32)],
        ),
        out_shape=[jax.ShapeDtypeStruct(shape, jnp.float32) for _ in order],
        compiler_params=params(),
        cost_estimate=cost(1e6, 8 * LANES * planes * width),
        name="pack",
    )(chip, pltpu.with_memory_space_constraint(distribution, pltpu.HBM), after)


def message_kernel(cells, *refs):
    pieces, out = refs[:-2], refs[-1]
    for index, piece in enumerate(pieces):
        out[:, index * LANES : (index + 1) * LANES] = piece[: WIDE * cells + HEAD, :]


def message_of(pieces, cells, after):
    shape = (WIDE * cells + HEAD, LANES * len(pieces))
    return pl.pallas_call(
        functools.partial(message_kernel, cells),
        grid=(1,),
        in_specs=[pl.BlockSpec(p.shape, lambda i: (0, 0)) for p in pieces] + [anywhere()],
        out_specs=resident(),
        out_shape=jax.ShapeDtypeStruct(shape, jnp.float32),
        compiler_params=params([True] * len(pieces) + [False]),
        cost_estimate=cost(1e5, 8 * shape[0] * shape[1]),
        name="message",
    )(*pieces, after)


def spread_kernel(planes, cells, *refs):
    pieces, out = refs[:-2], refs[-1]
    rows = WIDE * cells
    for index, piece in enumerate(pieces):
        columns = slice(index * LANES, (index + 1) * LANES)
        scale = jnp.exp2(-piece[rows : rows + 1, :])
        for x in range(planes):
            start = place_of(x, cells)
            out[x * cells : (x + 1) * cells, columns] = piece[start : start + cells, :] * scale


def spread(pieces, planes, cells, after):
    shape = (planes * cells, LANES * len(pieces))
    return pl.pallas_call(
        functools.partial(spread_kernel, planes, cells),
        grid=(1,),
        in_specs=[pl.BlockSpec(p.shape, lambda i: (0, 0)) for p in pieces] + [anywhere()],
        out_specs=resident(),
        out_shape=jax.ShapeDtypeStruct(shape, jnp.float32),
        compiler_params=params([True] * len(pieces) + [False]),
        cost_estimate=cost(1e6, 8 * shape[0] * shape[1]),
        name="spread",
    )(*pieces, after)


def arrange_kernel(order, planes, cells, word_ref, c_ref, rate_ref, next_ref, g_ref, p_ref, after_ref, speeds_ref, gain_ref, product_ref, *refs):
    rates, scratch = refs[:-1], refs[-1]
    chip, core = word_ref[0], word_ref[1]
    count = len(order)
    for row, mask in enumerate(order):
        own = 2 * (chip ^ mask) + core
        lines = slice(row * LANES, (row + 1) * LANES)
        speeds_ref[:, lines] = jnp.broadcast_to(c_ref[pl.ds(own, 1), :], (8, LANES))
        source = pl.ds(pl.multiple_of(own * LANES, LANES), LANES)
        for column in range(2 * count):
            other = order[column % count]
            block = 2 * (chip ^ other) + (core if column < count else 1 - core)
            lanes = pl.ds(pl.multiple_of(block * LANES, LANES), LANES)
            target = slice(column * LANES, (column + 1) * LANES)
            gain_ref[lines, target] = g_ref[source, lanes]
            product_ref[lines, target] = p_ref[source, lanes]
    tall = jnp.concatenate([rate_ref[...], next_ref[...]], axis=0)
    tall = jnp.concatenate([tall, jnp.zeros((LANES - tall.shape[0], tall.shape[1]), jnp.float32)], axis=0)
    for lane in range(0, tall.shape[1], LANES):
        scratch[lane : lane + LANES, :] = tall[:, lane : lane + LANES].T
    for k in range(len(rates) // 2):
        first = pl.multiple_of((k * count + chip) * cells, cells)
        part = scratch[pl.ds(first, cells), :]
        for x in range(planes + HALO):
            wide = jnp.broadcast_to(part[:, x : x + 1], (cells, LANES))
            if x >= HALO:
                rates[2 * k][(x - HALO) * cells : (x - HALO + 1) * cells, :] = wide
            if x < planes:
                rates[2 * k + 1][x * cells : (x + 1) * cells, :] = wide


def arrange(courant, collision_rate, next_rate, gain_matrix, product_matrix, word, order, cells, after):
    count = len(order)
    planes, plane = collision_rate.shape
    shape = (count * LANES, 2 * count * LANES)
    rate = jax.ShapeDtypeStruct((planes * cells, LANES), jnp.float32)
    results = pl.pallas_call(
        functools.partial(arrange_kernel, order, planes, cells),
        in_specs=[pl.BlockSpec(memory_space=pltpu.SMEM)] + [resident()] * 5 + [anywhere()],
        out_specs=[resident()] * (3 + 2 * CHUNKS),
        out_shape=[
            jax.ShapeDtypeStruct((8, count * LANES), jnp.float32),
            jax.ShapeDtypeStruct(shape, jnp.bfloat16),
            jax.ShapeDtypeStruct(shape, jnp.bfloat16),
        ]
        + [rate] * (2 * CHUNKS),
        scratch_shapes=[pltpu.VMEM((plane, LANES), jnp.float32)],
        compiler_params=params(grid=False),
        cost_estimate=cost(1e5, 12 * shape[0] * shape[1]),
        name="arrange",
    )(word, courant.reshape(-1, LANES), collision_rate, next_rate, gain_matrix, product_matrix, after)
    return results[0], results[1], results[2], results[3::2], results[4::2]


def stage(values, speed, bend, positive):
    differ = [b - a for a, b in zip(values[:-1], values[1:])]
    slopes = [
        jnp.maximum(jnp.minimum(a, b), jnp.minimum(jnp.maximum(a, b), 0.0))
        for a, b in zip(differ[:-1], differ[1:])
    ]
    inner = [speed * u + bend * s for u, s in zip(values[1:-1], slopes)]
    faces = [jnp.where(positive, a, b) for a, b in zip(inner[:-1], inner[1:])]
    return [u - (b - a) for u, a, b in zip(values[2:-2], faces[:-1], faces[1:])]


def advect_kernel(cells, tile, before, c_ref, extra_ref, *refs):
    bodies, smoothed_ref, pieces = refs[: -2 - QUARTERS], refs[-1 - QUARTERS], refs[-QUARTERS:]
    rows = WIDE * cells
    sources = [(extra_ref, x * cells) for x in range(WIDE)] if before else []
    for ref in bodies:
        sources += [(ref, x * cells) for x in range(ref.shape[0] // cells)]
    if not before:
        sources += [(extra_ref, x * cells) for x in range(WIDE)]
    planes = len(sources) - WIDE
    share = planes // QUARTERS

    def column(j, outer):
        lanes = pl.ds(pl.multiple_of(j * LANES, LANES), LANES)
        speed = c_ref[0:1, lanes]
        size = jnp.abs(speed)
        bend = 0.5 * size * (1.0 - size)
        positive = jnp.broadcast_to(speed, (tile, LANES)) > 0.0
        back = jnp.exp2(-extra_ref[rows : rows + 1, lanes])

        def body(t, carry):
            start = t * tile

            def read(x):
                ref, first = sources[x]
                value = ref[pl.ds(pl.multiple_of(first + start, tile), tile), lanes]
                return value * back if ref is extra_ref else value

            section = stage([read(x) for x in range(len(sources))], speed, bend, positive)
            moved = stage(section, speed, bend, positive)
            for x in range(planes):
                result = 0.5 * read(x + HALO) + 0.5 * moved[x]
                smoothed_ref[pl.ds(pl.multiple_of(x * cells + start, tile), tile), lanes] = result
                where = pl.ds(pl.multiple_of((x % share) * cells + start, tile), tile)
                pieces[x // share][where, lanes] = result.astype(jnp.bfloat16)
            return carry

        return lax.fori_loop(0, cells // tile, body, outer)

    lax.fori_loop(0, extra_ref.shape[1] // LANES, column, 0)


def transport(speeds, extra, bodies, before, planes, cells, after):
    rows, width = planes * cells, extra.shape[1]
    results = pl.pallas_call(
        functools.partial(advect_kernel, cells, 16, before),
        in_specs=[resident()] * (2 + len(bodies)) + [anywhere()],
        out_specs=[resident()] * (1 + QUARTERS),
        out_shape=[jax.ShapeDtypeStruct((rows, width), jnp.float32)]
        + [jax.ShapeDtypeStruct((rows // QUARTERS, width), jnp.bfloat16)] * QUARTERS,
        compiler_params=params(grid=False),
        cost_estimate=cost(40 * rows * width, 12 * rows * width),
        name="transport",
    )(speeds, extra, *bodies, after)
    return results[0], results[1:]


def collided(lhs, smoothed, rounded, rate, gain_ref, product_ref, columns):
    dims = (((1,), (1,)), ((), ()))

    def term(ref):
        return lax.dot_general(lhs, ref[columns, :], dims, preferred_element_type=jnp.float32)

    gained = (term(gain_ref) * term(product_ref)).astype(jnp.bfloat16).astype(jnp.float32)
    rate = jnp.concatenate([rate] * (rounded.shape[1] // LANES), axis=1)
    return smoothed + time_step * (gained - rate * rounded.astype(jnp.float32))


def joined(own_refs, other_refs):
    return jnp.concatenate(
        [
            jnp.concatenate([own[...], other[...]], axis=1)
            for own, other in zip(own_refs, other_refs)
        ],
        axis=0,
    )


def half_kernel(count, first, sends, *refs):
    own, other = refs[:count], refs[count : 2 * count]
    smoothed_ref, rate_ref, gain_ref, product_ref, _, state_ref = refs[2 * count : 2 * count + 6]
    size, width = state_ref.shape
    group = 2 * LANES
    lines = slice(first, first + size)
    lhs = joined(own, other)
    for start in range(0, width, group):
        columns = slice(start, start + group)
        state = collided(
            lhs, smoothed_ref[lines, columns], lhs[:, columns], rate_ref[lines, :],
            gain_ref, product_ref, columns,
        )
        state_ref[:, columns] = state
        if sends:
            message_ref = refs[-1]
            power = exponent_of(jnp.max(jnp.abs(state), axis=0, keepdims=True))
            message_ref[:size, columns] = state * jnp.exp2(power)
            message_ref[size:, columns] = jnp.broadcast_to(power, (HEAD, group))


def collide_half(own, other, smoothed, rate, gain, product, first, sends, after):
    width = smoothed.shape[1]
    rows = sum(a.shape[0] for a in own)
    shapes = [jax.ShapeDtypeStruct((rows, width), jnp.float32)]
    if sends:
        shapes.append(jax.ShapeDtypeStruct((rows + HEAD, width), jnp.float32))
    return pl.pallas_call(
        functools.partial(half_kernel, len(own), first, sends),
        in_specs=[resident()] * (2 * len(own) + 4) + [anywhere()],
        out_specs=[resident()] * len(shapes),
        out_shape=shapes,
        compiler_params=params(grid=False),
        cost_estimate=cost(8 * rows * width * width, 20 * rows * width),
        name="faces" if sends else "inside",
    )(*own, *other, smoothed, rate, gain, product, after)


def final_kernel(part, *refs):
    own, other = refs[:QUARTERS], refs[QUARTERS : 2 * QUARTERS]
    smoothed_ref, rate_ref, gain_ref, product_ref = refs[2 * QUARTERS : 2 * QUARTERS + 4]
    outs, scratch = refs[2 * QUARTERS + 5 : -1], refs[-1]
    rows, group = scratch.shape
    columns = slice(part * group, (part + 1) * group)
    half = QUARTERS // 2
    size = rows // 2
    for index in range(2):
        lines = slice(index * size, (index + 1) * size)
        lhs = joined(own[index * half : (index + 1) * half], other[index * half : (index + 1) * half])
        scratch[lines, :] = collided(
            lhs, smoothed_ref[lines, columns], lhs[:, columns], rate_ref[lines, :],
            gain_ref, product_ref, columns,
        )
    for index, out in enumerate(outs):
        lanes = slice(index * LANES, (index + 1) * LANES)

        def block(i):
            return pl.ds(pl.multiple_of(i * LANES, LANES), LANES)

        def peak(i, carry):
            return jnp.maximum(carry, jnp.abs(scratch[block(i), lanes]))

        top = lax.fori_loop(0, rows // LANES, peak, jnp.zeros((LANES, LANES), jnp.float32))
        power = exponent_of(jnp.max(top, axis=0, keepdims=True))
        scale = jnp.exp2(power)

        def write(i, carry):
            out[block(i), :] = scratch[block(i), lanes] * scale
            return carry

        lax.fori_loop(0, rows // LANES, write, 0)
        out[rows:, :] = jnp.broadcast_to(power, (HEAD, LANES))


def final(own, other, smoothed, rate, gain, product, part, after):
    rows, width = smoothed.shape
    group = 2 * LANES
    shape = jax.ShapeDtypeStruct((rows + HEAD, LANES), jnp.float32)
    return pl.pallas_call(
        functools.partial(final_kernel, part),
        in_specs=[resident()] * (2 * QUARTERS + 4) + [anywhere()],
        out_specs=[resident()] * 2,
        out_shape=[shape] * 2,
        scratch_shapes=[pltpu.VMEM((rows, group), jnp.float32)],
        compiler_params=params(grid=False),
        cost_estimate=cost(8 * rows * width * group, 20 * rows * group),
        name="final",
    )(*own, *other, smoothed, rate, gain, product, after)


def unpack_kernel(order, planes, cells, chip_ref, *refs):
    count = len(order)
    pieces, out, scratch = refs[:count], refs[-2], refs[-1]
    chip = chip_ref[0]
    step = pl.program_id(0)
    flat = out.reshape(LANES * planes, LANES)

    @pl.when(step == 0)
    def _():
        for mask, piece in zip(order, pieces):
            first = pl.multiple_of((chip ^ mask) * cells, cells)
            scale = jnp.exp2(-piece[planes * cells : planes * cells + 1, :])

            for x in range(planes):
                scratch[x, pl.ds(first, cells), :] = piece[x * cells : (x + 1) * cells, :] * scale

    for x in range(planes):
        part = scratch[x, pl.ds(pl.multiple_of(step * LANES, LANES), LANES), :]
        flat[pl.ds(x, LANES, stride=planes), :] = part.T


def unpack(pieces, target, chip, order, chunk, planes, cells, after):
    width = cells * len(order)
    steps = width // LANES
    shape = (LANES, planes, width * CHUNKS)
    specs = [pl.BlockSpec(p.shape, lambda i, s: (0, 0)) for p in pieces]
    operands = list(pieces)
    count = len(pieces)
    specs.append(anywhere())
    operands.append(after)
    aliases = {}
    if target is not None:
        specs.append(pl.BlockSpec(memory_space=pl.ANY))
        operands.append(target)
        aliases = {len(operands): 0}
    return pl.pallas_call(
        functools.partial(unpack_kernel, order, planes, cells),
        grid_spec=pltpu.PrefetchScalarGridSpec(
            num_scalar_prefetch=1,
            grid=(steps,),
            in_specs=specs,
            out_specs=pl.BlockSpec((LANES, planes, LANES), lambda i, s: (0, 0, chunk * steps + i)),
            scratch_shapes=[pltpu.VMEM((planes, width, LANES), jnp.float32)],
        ),
        out_shape=jax.ShapeDtypeStruct(shape, jnp.float32),
        input_output_aliases=aliases,
        compiler_params=params([False] + [True] * count + [False] * (len(operands) - count)),
        cost_estimate=cost(1e6, 8 * LANES * planes * width),
        name="unpack",
    )(chip, *operands)


def exchange(array, mask):
    count = lax.axis_size("vel")
    return lax.ppermute(array, "vel", [(i, i ^ mask) for i in range(count)])


def shift(array, step):
    count = lax.axis_size("space")
    return lax.ppermute(array, "space", [(i, (i + step) % count) for i in range(count)])


def half(array):
    return array.astype(jnp.float16)


def full(array):
    return array.astype(jnp.float32)


def body(distribution, courant, gain_matrix, product_matrix, collision_rate):
    planes, plane = distribution.shape[1:]
    chips = lax.axis_size("vel") // 2
    member = lax.axis_index("vel").astype(jnp.int32)
    chip, core = lax.shift_right_logical(member, 1), member & 1
    order = list(range(1, chips)) + [0]
    cells = plane // (chips * CHUNKS)
    span = cells * chips
    word = jnp.stack([chip, core])

    every = range(CHUNKS)
    sent, extra, local, state = {}, {}, {}, {}
    after = distribution
    for k in every:
        pieces = pack(distribution, word, order, k, cells, after)
        after = pieces[-1]
        sent[k] = [
            a if m == 0 else full(exchange(half(a), 2 * m)) for a, m in zip(pieces, order)
        ]
    speeds, gain, product, shifted_rates, rates = arrange(
        courant, collision_rate, shift(collision_rate[:8], -1), gain_matrix, product_matrix,
        word, order, cells, after,
    )
    after = product
    for k in every:
        message = message_of(sent[k], cells, after)
        extra[k] = shift(half(message), -1)
        local[k] = after = spread(sent[k], planes, cells, message)
    middle = QUARTERS // 2
    for k in every:
        arrived, after = lax.optimization_barrier((extra[k], after))
        smoothed, own = transport(speeds, full(arrived), [local[k]], False, planes, cells, after)
        other = [exchange(a, 1) for a in own]
        upper, message = collide_half(
            own[middle:], other[middle:], smoothed, shifted_rates[k], gain, product,
            WIDE * cells, True, after,
        )
        extra[k] = shift(half(message), 1)
        (lower,) = collide_half(
            own[:middle], other[:middle], smoothed, shifted_rates[k], gain, product,
            0, False, message,
        )
        state[k] = [lower, upper]
        after = lower
    back = {}
    for k in every:
        arrived, after = lax.optimization_barrier((extra[k], after))
        smoothed, own = transport(speeds, full(arrived), state[k], True, planes, cells, after)
        other = [exchange(a, 1) for a in own]
        ready = []
        for part in range(chips // 2):
            ready += final(own, other, smoothed, rates[k], gain, product, part, after)
            after = ready[-1]
        back[k] = [a if m == 0 else full(exchange(half(a), 2 * m)) for a, m in zip(ready, order)]
    result = None
    for k in every:
        result = unpack(back[k], result, word, order, k, planes, cells, after)
    return result


def fits(mesh, shape, spaces):
    groups = mesh.shape["vel"]
    local, planes = shape[0] // groups, shape[1] // spaces
    chips = groups // 2
    return (
        groups % 4 == 0
        and chips & (chips - 1) == 0
        and local == LANES
        and planes == 2 * WIDE
        and shape[2] % (CHUNKS * LANES) == 0
        and shape[2] % (CHUNKS * chips * 16) == 0
    )


def solution(mesh):
    in_specs = (P("vel", "space", None), P(), P(), P(), P("space", None))
    out_specs = P("vel", "space", None)

    def run(distribution, courant, gain_matrix, product_matrix, collision_rate):
        special = fits(mesh, distribution.shape, mesh.shape["space"])
        return jax.shard_map(
            body if special else general_body,
            mesh=mesh, in_specs=in_specs, out_specs=out_specs, check_vma=False,
        )(distribution, courant, gain_matrix, product_matrix, collision_rate)

    return run
```

time: 170 us -> 107 us (0.63)
  waiting for transfers between devices: 84.7 us -> 33.8 us
  Pallas kernels: 45.4 us -> 37.7 us
  local copies, waits for them, and re-layouts: 5.06 us -> 0.02 us
  starting transfers between devices: 27.7 us -> 32.7 us
  other arithmetic: 6.01 us -> 1.9 us
    ppermute x8 -> x5, waiting for transfers between devices: 47.7 us -> 8.33 us  [shift(): lax.ppermute(array, 'space', [(i, (i + step) % count) for i in range(coun...]
    ppermute x16 -> x28, waiting for transfers between devices: 37 us -> 25.5 us  [exchange(): return lax.ppermute(array, 'vel', [(i, i ^ mask) for i in range(count)])]
    pallas_call x11, Pallas kernels: 25.8 us -> 18.5 us  [the longest x4 11.3 us: transport(): pl.pallas_call(functools.partial(advect_kernel, cells, 16, before), in_sp...]
    ppermute x16 -> x28, starting transfers between devices: 15.8 us -> 20.8 us  [exchange(): return lax.ppermute(array, 'vel', [(i, i ^ mask) for i in range(count)])]
    unnamed x32 -> x8, local copies, waits for them, and re-layouts: 4.46 us -> 0.02 us
    convert_element_type x20 -> x16, other arithmetic: 3.76 us -> 0.96 us  [full(): return array.astype(jnp.float32)]
    ppermute x8 -> x5, starting transfers between devices: 11.9 us -> 11.9 us  [shift(): lax.ppermute(array, 'space', [(i, (i + step) % count) for i in range(coun...]
  transfers between devices with their start and end apart: 24 -> 33, of which waited for: 18 -> 22; matrix products, arithmetic and copies ran while one was open for 4% -> 2% of each run, Pallas kernels for 7% -> 30%
where the time goes in v4:
time: 107 us
  Pallas kernels  37.7 us (35%)
  waiting for transfers between devices  33.8 us (32%)
  starting transfers between devices  32.7 us (31%)
  other arithmetic  1.9 us (2%)
    ppermute x28, waiting for transfers between devices, exchange(): return lax.ppermute(array, 'vel', [(i, i ^ mask) for i in range(count)])  25.5 us
    ppermute x28, starting transfers between devices, exchange(): return lax.ppermute(array, 'vel', [(i, i ^ mask) for i in range(count)])  20.8 us
    ppermute x5, starting transfers between devices, shift(): lax.ppermute(array, 'space', [(i, (i + step) % count) for i in range(coun...  11.9 us
    pallas_call x4, Pallas kernels, transport(): pl.pallas_call(functools.partial(advect_kernel, cells, 16, before), in_sp...  11.3 us
    ppermute x5, waiting for transfers between devices, shift(): lax.ppermute(array, 'space', [(i, (i + step) % count) for i in range(coun...  8.33 us
    pallas_call x2, Pallas kernels, pack(): pl.pallas_call(functools.partial(pack_kernel, order, planes, cells), grid...  7.04 us
    pallas_call x4, Pallas kernels, final(): pl.pallas_call(functools.partial(final_kernel, part), in_specs=[resident(...  6.52 us
    pallas_call x4, Pallas kernels, collide_half(): pl.pallas_call(functools.partial(half_kernel, len(own), first, sends), in...  5.49 us
  transfers between devices with their start and end apart: 33, of which 22 were waited for; matrix products, arithmetic and copies ran while one was open for 2% of the time, Pallas kernels for 30%

profile of v4, /device:TPU:0, one launch (start us, length us, event | category | flops | bytes accessed | tf_op | source)
XLA Modules:
  0.0 106.6 jit_solution(11561599547490969701)
XLA Ops:
  0.1 3.5 %pack.2 = (f32[1040,128]{1,0:T(8,128)S(1)}, f32[1040,128]{1,0:T(8,128)S(1)}, f32[1040,128]{1,0:T(8,128)S(1)}, f32[1040,128]{1,0:T(8,128)S(1)}) custom-call(s32[2]{0:T(128)S(1)} %pad_add_fusion.chip_ref.word_ref, f32[128,16,512]{2,1,0:T(8,128)} %d_ref.3, f32[128,16,512]{2,1,0:T(8,128)} %d_ref.3), custom_call_target="tpu_custom_call" | custom-call | flops 1000 | bytes 1000 | tf_op jit(solution)/shard_map/pack/pallas_call | solution.py:173
  3.6 4.0 %collective-permute-start.6 = (f16[1040,128]{1,0:T(8,128)(2,1)S(1)}, f16[1040,128]{1,0:T(8,128)(2,1)S(1)}, u32[]{:S(2)}, u32[]{:S(2)}) collective-permute-start(f16[1040,128]{1,0:T(8,128)(2,1)S(1)} %convert_element_type.106), channel_id=1, source_target_pairs={{0,24},{4,28},{8,16},{12,20},{16,8},{20,12},{24,0},{28,4},{1,25},{... | collective-permute-start | bytes 798728 | tf_op jit(solution)/shard_map/ppermute | solution.py:523
  8.4 4.1 %collective-permute-start = (f32[8,512]{1,0:T(8,128)S(1)}, f32[8,512]{1,0:T(8,128)S(1)}, u32[]{:S(2)}, u32[]{:S(2)}) collective-permute-start(f32[8,512]{1,0:T(8,128)S(1)} %slice.3), channel_id=1, source_target_pairs={{0,3},{1,0},{2,1},{3,2},{4,7},{5,4},{6,5},{7,6},{8,11},{9,8},{10,9... | collective-permute-start | bytes 49160 | tf_op jit(solution)/shard_map/ppermute | solution.py:528
  12.4 3.6 %pack.3 = (f32[1040,128]{1,0:T(8,128)S(1)}, f32[1040,128]{1,0:T(8,128)S(1)}, f32[1040,128]{1,0:T(8,128)S(1)}, f32[1040,128]{1,0:T(8,128)S(1)}) custom-call(s32[2]{0:T(128)S(1)} %pad_add_fusion.chip_ref.word_ref, f32[128,16,512]{2,1,0:T(8,128)} %d_ref.3, f32[1040,128]{1,0:T(8,128)S(1)} %get-tuple-element.60.after_ref.refs_3_), custom_call_target="tpu_custom_call" | custom-call | flops 1000 | bytes 1000 | tf_op jit(solution)/shard_map/pack/pallas_call | solution.py:173
  16.1 2.5 %collective-permute-start.3 = (f16[1040,128]{1,0:T(8,128)(2,1)S(1)}, f16[1040,128]{1,0:T(8,128)(2,1)S(1)}, u32[]{:S(2)}, u32[]{:S(2)}) collective-permute-start(f16[1040,128]{1,0:T(8,128)(2,1)S(1)} %convert_element_type.100), channel_id=1, source_target_pairs={{0,24},{4,28},{8,16},{12,20},{16,8},{20,12},{24,0},{28,4},{1,25},{... | collective-permute-start | bytes 798728 | tf_op jit(solution)/shard_map/ppermute | solution.py:523
  21.7 3.4 %collective-permute-start.8 = (f16[528,512]{1,0:T(8,128)(2,1)S(1)}, f16[528,512]{1,0:T(8,128)(2,1)S(1)}, u32[]{:S(2)}, u32[]{:S(2)}) collective-permute-start(f16[528,512]{1,0:T(8,128)(2,1)S(1)} %convert_element_type.109), channel_id=1, source_target_pairs={{0,3},{1,0},{2,1},{3,2},{4,7},{5,4},{6,5},{7,6},{8,11},{9,8},{10,9... | collective-permute-start | bytes 1622024 | tf_op jit(solution)/shard_map/ppermute | solution.py:528
  26.5 4.6 %collective-permute-done.2 = f16[1040,128]{1,0:T(8,128)(2,1)S(1)} collective-permute-done((f16[1040,128]{1,0:T(8,128)(2,1)S(1)}, f16[1040,128]{1,0:T(8,128)(2,1)S(1)}, u32[]{:S(2)}, u32[]{:S(2)}) %collective-permute-start.2) | collective-permute-done | bytes 266272 | tf_op jit(solution)/shard_map/ppermute | solution.py:523
  31.7 3.7 %collective-permute-start.7 = (f16[528,512]{1,0:T(8,128)(2,1)S(1)}, f16[528,512]{1,0:T(8,128)(2,1)S(1)}, u32[]{:S(2)}, u32[]{:S(2)}) collective-permute-start(f16[528,512]{1,0:T(8,128)(2,1)S(1)} %convert_element_type.108), channel_id=1, source_target_pairs={{0,3},{1,0},{2,1},{3,2},{4,7},{5,4},{6,5},{7,6},{8,11},{9,8},{10,9... | collective-permute-start | bytes 1622024 | tf_op jit(solution)/shard_map/ppermute | solution.py:528
  35.7 2.0 %collective-permute-done.8 = f16[528,512]{1,0:T(8,128)(2,1)S(1)} collective-permute-done((f16[528,512]{1,0:T(8,128)(2,1)S(1)}, f16[528,512]{1,0:T(8,128)(2,1)S(1)}, u32[]{:S(2)}, u32[]{:S(2)}) %collective-permute-start.8) | collective-permute-done | bytes 540704 | tf_op jit(solution)/shard_map/ppermute | solution.py:528
  37.8 2.8 %transport.4 = (f32[1024,512]{1,0:T(8,128)S(1)}, bf16[256,512]{1,0:T(8,128)(2,1)S(1)}, bf16[256,512]{1,0:T(8,128)(2,1)S(1)}, bf16[256,512]{1,0:T(8,128)(2,1)S(1)}, bf16[256,512]{1,0:T(8,128)(2,1)S(1)}) custom-call(f32[8,512]{1,0:T(8,128)S(1)} %get-tuple-element.62.c_ref, f32[528,512]{1,0:T(8,128)S(1)} %convert_element_type.110.extra_ref, ...), custom_call_target="tpu_custom_call" | custom-call | flops 1000 | bytes 1000 | tf_op jit(solution)/shard_map/transport/pallas_call | solution.py:345
  46.0 3.4 %collective-permute-done.7 = f16[528,512]{1,0:T(8,128)(2,1)S(1)} collective-permute-done((f16[528,512]{1,0:T(8,128)(2,1)S(1)}, f16[528,512]{1,0:T(8,128)(2,1)S(1)}, u32[]{:S(2)}, u32[]{:S(2)}) %collective-permute-start.7) | collective-permute-done | bytes 540704 | tf_op jit(solution)/shard_map/ppermute | solution.py:528
  49.5 2.8 %transport.5 = (f32[1024,512]{1,0:T(8,128)S(1)}, bf16[256,512]{1,0:T(8,128)(2,1)S(1)}, bf16[256,512]{1,0:T(8,128)(2,1)S(1)}, bf16[256,512]{1,0:T(8,128)(2,1)S(1)}, bf16[256,512]{1,0:T(8,128)(2,1)S(1)}) custom-call(f32[8,512]{1,0:T(8,128)S(1)} %get-tuple-element.62.c_ref, f32[528,512]{1,0:T(8,128)S(1)} %convert_element_type.111.extra_ref, ...), custom_call_target="tpu_custom_call" | custom-call | flops 1000 | bytes 1000 | tf_op jit(solution)/shard_map/transport/pallas_call | solution.py:345
  59.3 1.8 %collective-permute-done.16 = f16[528,512]{1,0:T(8,128)(2,1)S(1)} collective-permute-done((f16[528,512]{1,0:T(8,128)(2,1)S(1)}, f16[528,512]{1,0:T(8,128)(2,1)S(1)}, u32[]{:S(2)}, u32[]{:S(2)}) %collective-permute-start.16) | collective-permute-done | bytes 540704 | tf_op jit(solution)/shard_map/ppermute | solution.py:528
  61.2 2.9 %transport.6 = (f32[1024,512]{1,0:T(8,128)S(1)}, bf16[256,512]{1,0:T(8,128)(2,1)S(1)}, bf16[256,512]{1,0:T(8,128)(2,1)S(1)}, bf16[256,512]{1,0:T(8,128)(2,1)S(1)}, bf16[256,512]{1,0:T(8,128)(2,1)S(1)}) custom-call(f32[8,512]{1,0:T(8,128)S(1)} %get-tuple-element.62.c_ref, f32[528,512]{1,0:T(8,128)S(1)} %convert_element_type.114.extra_ref, ...), custom_call_target="tpu_custom_call" | custom-call | flops 1000 | bytes 1000 | tf_op jit(solution)/shard_map/transport/pallas_call | solution.py:345
  66.8 1.6 %final.4 = (f32[1040,128]{1,0:T(8,128)S(1)}, f32[1040,128]{1,0:T(8,128)S(1)}) custom-call(bf16[256,512]{1,0:T(8,128)(2,1)S(1)} %get-tuple-element.92.refs_0_, bf16[256,512]{1,0:T(8,128)(2,1)S(1)} %get-tuple-element.93.refs_1_, bf16[256,512]{1,0:T(8,128)(2,1)S(1)} %get-tuple-element.94.refs_2_, bf16[256,512]{1,0:T(8,128)(2,1)S(1)} %get-tuple-element.95.refs_3_, ...), custom_call_target="tpu_custom_call" | custom-call | flops 1000 | bytes 1000 | tf_op jit(solution)/shard_map/final/pallas_call | solution.py:457
  70.1 1.6 %final.5 = (f32[1040,128]{1,0:T(8,128)S(1)}, f32[1040,128]{1,0:T(8,128)S(1)}) custom-call(bf16[256,512]{1,0:T(8,128)(2,1)S(1)} %get-tuple-element.92.refs_0_, bf16[256,512]{1,0:T(8,128)(2,1)S(1)} %get-tuple-element.93.refs_1_, bf16[256,512]{1,0:T(8,128)(2,1)S(1)} %get-tuple-element.94.refs_2_, bf16[256,512]{1,0:T(8,128)(2,1)S(1)} %get-tuple-element.95.refs_3_, ...), custom_call_target="tpu_custom_call" | custom-call | flops 1000 | bytes 1000 | tf_op jit(solution)/shard_map/final/pallas_call | solution.py:457
  73.0 2.9 %transport.7 = (f32[1024,512]{1,0:T(8,128)S(1)}, bf16[256,512]{1,0:T(8,128)(2,1)S(1)}, bf16[256,512]{1,0:T(8,128)(2,1)S(1)}, bf16[256,512]{1,0:T(8,128)(2,1)S(1)}, bf16[256,512]{1,0:T(8,128)(2,1)S(1)}) custom-call(f32[8,512]{1,0:T(8,128)S(1)} %get-tuple-element.62.c_ref, f32[528,512]{1,0:T(8,128)S(1)} %convert_element_type.115.extra_ref, ...), custom_call_target="tpu_custom_call" | custom-call | flops 1000 | bytes 1000 | tf_op jit(solution)/shard_map/transport/pallas_call | solution.py:345
  80.5 1.6 %final.6 = (f32[1040,128]{1,0:T(8,128)S(1)}, f32[1040,128]{1,0:T(8,128)S(1)}) custom-call(bf16[256,512]{1,0:T(8,128)(2,1)S(1)} %get-tuple-element.103.refs_0_, bf16[256,512]{1,0:T(8,128)(2,1)S(1)} %get-tuple-element.104.refs_1_, bf16[256,512]{1,0:T(8,128)(2,1)S(1)} %get-tuple-element.105.refs_2_, bf16[256,512]{1,0:T(8,128)(2,1)S(1)} %get-tuple-element.106.refs_3_, ...), custom_call_target="tpu_custom_call" | custom-call | flops 1000 | bytes 1000 | tf_op jit(solution)/shard_map/final/pallas_call | solution.py:457
  82.8 1.6 %final.7 = (f32[1040,128]{1,0:T(8,128)S(1)}, f32[1040,128]{1,0:T(8,128)S(1)}) custom-call(bf16[256,512]{1,0:T(8,128)(2,1)S(1)} %get-tuple-element.103.refs_0_, bf16[256,512]{1,0:T(8,128)(2,1)S(1)} %get-tuple-element.104.refs_1_, bf16[256,512]{1,0:T(8,128)(2,1)S(1)} %get-tuple-element.105.refs_2_, bf16[256,512]{1,0:T(8,128)(2,1)S(1)} %get-tuple-element.106.refs_3_, ...), custom_call_target="tpu_custom_call" | custom-call | flops 1000 | bytes 1000 | tf_op jit(solution)/shard_map/final/pallas_call | solution.py:457
  87.7 5.8 %collective-permute-done.30 = f16[1040,128]{1,0:T(8,128)(2,1)S(1)} collective-permute-done((f16[1040,128]{1,0:T(8,128)(2,1)S(1)}, f16[1040,128]{1,0:T(8,128)(2,1)S(1)}, u32[]{:S(2)}, u32[]{:S(2)}) %collective-permute-start.30) | collective-permute-done | bytes 266272 | tf_op jit(solution)/shard_map/ppermute | solution.py:523
  93.5 2.5 %unpack.2.refs_5_ = f32[128,16,512]{2,1,0:T(8,128)} custom-call(s32[2]{0:T(128)S(1)} %pad_add_fusion.chip_ref.word_ref, f32[1040,128]{1,0:T(8,128)S(1)} %convert_element_type.123.refs_0_, f32[1040,128]{1,0:T(8,128)S(1)} %convert_element_type.125.refs_1_, f32[1040,128]{1,0:T(8,128)S(1)} %convert_element_type.127.refs_2_, ...), custom_call_target="tpu_custom_call" | custom-call | flops 1000 | bytes 1000 | tf_op jit(solution)/shard_map/unpack/pallas_call | solution.py:504
  96.1 3.0 %collective-permute-done.29 = f16[1040,128]{1,0:T(8,128)(2,1)S(1)} collective-permute-done((f16[1040,128]{1,0:T(8,128)(2,1)S(1)}, f16[1040,128]{1,0:T(8,128)(2,1)S(1)}, u32[]{:S(2)}, u32[]{:S(2)}) %collective-permute-start.29) | collective-permute-done | bytes 266272 | tf_op jit(solution)/shard_map/ppermute | solution.py:523
  99.1 5.0 %collective-permute-done.27 = f16[1040,128]{1,0:T(8,128)(2,1)S(1)} collective-permute-done((f16[1040,128]{1,0:T(8,128)(2,1)S(1)}, f16[1040,128]{1,0:T(8,128)(2,1)S(1)}, u32[]{:S(2)}, u32[]{:S(2)}) %collective-permute-start.27) | collective-permute-done | bytes 266272 | tf_op jit(solution)/shard_map/ppermute | solution.py:523
  104.1 2.5 %unpack.3 = f32[128,16,512]{2,1,0:T(8,128)} custom-call(s32[2]{0:T(128)S(1)} %pad_add_fusion.chip_ref.word_ref, f32[1040,128]{1,0:T(8,128)S(1)} %convert_element_type.117.refs_0_, f32[1040,128]{1,0:T(8,128)S(1)} %convert_element_type.119.refs_1_, f32[1040,128]{1,0:T(8,128)S(1)} %convert_element_type.121.refs_2_, ...), custom_call_target="tpu_custom_call", output_to_operand_aliasing={{}: (6, {})} | custom-call | flops 1000 | bytes 1000 | tf_op jit(solution)/shard_map/unpack/pallas_call | solution.py:504
  (105 shorter events, 33.2 us)
Async XLA Ops:
  3.6 15.6 %collective-permute-start.6 = (f16[1040,128]{1,0:T(8,128)(2,1)S(1)}, f16[1040,128]{1,0:T(8,128)(2,1)S(1)}, u32[]{:S(2)}, u32[]{:S(2)}) collective-permute-start(f16[1040,128]{1,0:T(8,128)(2,1)S(1)} %convert_element_type.106), channel_id=1, source_target_pairs={{0,24},{4,28},{8,16},{12,20},{16,8},{20,12},{24,0},{28,4},{1,25},{... | collective-permute-start | bytes 798728 | tf_op jit(solution)/shard_map/ppermute | solution.py:523
  7.6 13.7 %collective-permute-start.5 = (f16[1040,128]{1,0:T(8,128)(2,1)S(1)}, f16[1040,128]{1,0:T(8,128)(2,1)S(1)}, u32[]{:S(2)}, u32[]{:S(2)}) collective-permute-start(f16[1040,128]{1,0:T(8,128)(2,1)S(1)} %convert_element_type.104), channel_id=1, source_target_pairs={{0,16},{4,20},{8,24},{12,28},{16,0},{20,4},{24,8},{28,12},{1,17},{... | collective-permute-start | bytes 798728 | tf_op jit(solution)/shard_map/ppermute | solution.py:523
  8.2 13.2 %collective-permute-start.4 = (f16[1040,128]{1,0:T(8,128)(2,1)S(1)}, f16[1040,128]{1,0:T(8,128)(2,1)S(1)}, u32[]{:S(2)}, u32[]{:S(2)}) collective-permute-start(f16[1040,128]{1,0:T(8,128)(2,1)S(1)} %convert_element_type.102), channel_id=1, source_target_pairs={{0,8},{4,12},{8,0},{12,4},{16,24},{20,28},{24,16},{28,20},{1,9},{5... | collective-permute-start | bytes 798728 | tf_op jit(solution)/shard_map/ppermute | solution.py:523
  8.4 10.3 %collective-permute-start = (f32[8,512]{1,0:T(8,128)S(1)}, f32[8,512]{1,0:T(8,128)S(1)}, u32[]{:S(2)}, u32[]{:S(2)}) collective-permute-start(f32[8,512]{1,0:T(8,128)S(1)} %slice.3), channel_id=1, source_target_pairs={{0,3},{1,0},{2,1},{3,2},{4,7},{5,4},{6,5},{7,6},{8,11},{9,8},{10,9... | collective-permute-start | bytes 49160 | tf_op jit(solution)/shard_map/ppermute | solution.py:528
  16.1 10.3 %collective-permute-start.3 = (f16[1040,128]{1,0:T(8,128)(2,1)S(1)}, f16[1040,128]{1,0:T(8,128)(2,1)S(1)}, u32[]{:S(2)}, u32[]{:S(2)}) collective-permute-start(f16[1040,128]{1,0:T(8,128)(2,1)S(1)} %convert_element_type.100), channel_id=1, source_target_pairs={{0,24},{4,28},{8,16},{12,20},{16,8},{20,12},{24,0},{28,4},{1,25},{... | collective-permute-start | bytes 798728 | tf_op jit(solution)/shard_map/ppermute | solution.py:523
  18.7 12.4 %collective-permute-start.2 = (f16[1040,128]{1,0:T(8,128)(2,1)S(1)}, f16[1040,128]{1,0:T(8,128)(2,1)S(1)}, u32[]{:S(2)}, u32[]{:S(2)}) collective-permute-start(f16[1040,128]{1,0:T(8,128)(2,1)S(1)} %convert_element_type.98), channel_id=1, source_target_pairs={{0,16},{4,20},{8,24},{12,28},{16,0},{20,4},{24,8},{28,12},{1,17},{... | collective-permute-start | bytes 798728 | tf_op jit(solution)/shard_map/ppermute | solution.py:523
  19.3 12.2 %collective-permute-start.1 = (f16[1040,128]{1,0:T(8,128)(2,1)S(1)}, f16[1040,128]{1,0:T(8,128)(2,1)S(1)}, u32[]{:S(2)}, u32[]{:S(2)}) collective-permute-start(f16[1040,128]{1,0:T(8,128)(2,1)S(1)} %convert_element_type.96), channel_id=1, source_target_pairs={{0,8},{4,12},{8,0},{12,4},{16,24},{20,28},{24,16},{28,20},{1,9},{5... | collective-permute-start | bytes 798728 | tf_op jit(solution)/shard_map/ppermute | solution.py:523
  21.7 16.0 %collective-permute-start.8 = (f16[528,512]{1,0:T(8,128)(2,1)S(1)}, f16[528,512]{1,0:T(8,128)(2,1)S(1)}, u32[]{:S(2)}, u32[]{:S(2)}) collective-permute-start(f16[528,512]{1,0:T(8,128)(2,1)S(1)} %convert_element_type.109), channel_id=1, source_target_pairs={{0,3},{1,0},{2,1},{3,2},{4,7},{5,4},{6,5},{7,6},{8,11},{9,8},{10,9... | collective-permute-start | bytes 1622024 | tf_op jit(solution)/shard_map/ppermute | solution.py:528
  31.7 17.6 %collective-permute-start.7 = (f16[528,512]{1,0:T(8,128)(2,1)S(1)}, f16[528,512]{1,0:T(8,128)(2,1)S(1)}, u32[]{:S(2)}, u32[]{:S(2)}) collective-permute-start(f16[528,512]{1,0:T(8,128)(2,1)S(1)} %convert_element_type.108), channel_id=1, source_target_pairs={{0,3},{1,0},{2,1},{3,2},{4,7},{5,4},{6,5},{7,6},{8,11},{9,8},{10,9... | collective-permute-start | bytes 1622024 | tf_op jit(solution)/shard_map/ppermute | solution.py:528
  40.7 1.9 %collective-permute-start.12 = (bf16[256,512]{1,0:T(8,128)(2,1)S(1)}, bf16[256,512]{1,0:T(8,128)(2,1)S(1)}, u32[]{:S(2)}, u32[]{:S(2)}) collective-permute-start(bf16[256,512]{1,0:T(8,128)(2,1)S(1)} %get-tuple-element.78.refs_1_), channel_id=1, source_target_pairs={{0,4},{4,0},{8,12},{12,8},{16,20},{20,16},{24,28},{28,24},{1,5},{5... | collective-permute-start | bytes 786440 | tf_op jit(solution)/shard_map/ppermute | solution.py:523
  41.2 3.5 %collective-permute-start.9 = (bf16[256,512]{1,0:T(8,128)(2,1)S(1)}, bf16[256,512]{1,0:T(8,128)(2,1)S(1)}, u32[]{:S(2)}, u32[]{:S(2)}) collective-permute-start(bf16[256,512]{1,0:T(8,128)(2,1)S(1)} %get-tuple-element.72.refs_0_), channel_id=1, source_target_pairs={{0,4},{4,0},{8,12},{12,8},{16,20},{20,16},{24,28},{28,24},{1,5},{5... | collective-permute-start | bytes 786440 | tf_op jit(solution)/shard_map/ppermute | solution.py:523
  41.3 3.4 %collective-permute-start.10 = (bf16[256,512]{1,0:T(8,128)(2,1)S(1)}, bf16[256,512]{1,0:T(8,128)(2,1)S(1)}, u32[]{:S(2)}, u32[]{:S(2)}) collective-permute-start(bf16[256,512]{1,0:T(8,128)(2,1)S(1)} %get-tuple-element.73.refs_1_), channel_id=1, source_target_pairs={{0,4},{4,0},{8,12},{12,8},{16,20},{20,16},{24,28},{28,24},{1,5},{5... | collective-permute-start | bytes 786440 | tf_op jit(solution)/shard_map/ppermute | solution.py:523
  44.2 16.9 %collective-permute-start.16 = (f16[528,512]{1,0:T(8,128)(2,1)S(1)}, f16[528,512]{1,0:T(8,128)(2,1)S(1)}, u32[]{:S(2)}, u32[]{:S(2)}) collective-permute-start(f16[528,512]{1,0:T(8,128)(2,1)S(1)} %convert_element_type.113), channel_id=1, source_target_pairs={{0,1},{1,2},{2,3},{3,0},{4,5},{5,6},{6,7},{7,4},{8,9},{9,10},{10,1... | collective-permute-start | bytes 1622024 | tf_op jit(solution)/shard_map/ppermute | solution.py:528
  55.8 17.1 %collective-permute-start.15 = (f16[528,512]{1,0:T(8,128)(2,1)S(1)}, f16[528,512]{1,0:T(8,128)(2,1)S(1)}, u32[]{:S(2)}, u32[]{:S(2)}) collective-permute-start(f16[528,512]{1,0:T(8,128)(2,1)S(1)} %convert_element_type.112), channel_id=1, source_target_pairs={{0,1},{1,2},{2,3},{3,0},{4,5},{5,6},{6,7},{7,4},{8,9},{9,10},{10,1... | collective-permute-start | bytes 1622024 | tf_op jit(solution)/shard_map/ppermute | solution.py:528
  64.8 2.1 %collective-permute-start.22 = (bf16[256,512]{1,0:T(8,128)(2,1)S(1)}, bf16[256,512]{1,0:T(8,128)(2,1)S(1)}, u32[]{:S(2)}, u32[]{:S(2)}) collective-permute-start(bf16[256,512]{1,0:T(8,128)(2,1)S(1)} %get-tuple-element.95.refs_3_), channel_id=1, source_target_pairs={{0,4},{4,0},{8,12},{12,8},{16,20},{20,16},{24,28},{28,24},{1,5},{5... | collective-permute-start | bytes 786440 | tf_op jit(solution)/shard_map/ppermute | solution.py:523
  68.5 17.6 %collective-permute-start.31 = (f16[1040,128]{1,0:T(8,128)(2,1)S(1)}, f16[1040,128]{1,0:T(8,128)(2,1)S(1)}, u32[]{:S(2)}, u32[]{:S(2)}) collective-permute-start(f16[1040,128]{1,0:T(8,128)(2,1)S(1)} %convert_element_type.124), channel_id=1, source_target_pairs={{0,16},{4,20},{8,24},{12,28},{16,0},{20,4},{24,8},{28,12},{1,17},{... | collective-permute-start | bytes 798728 | tf_op jit(solution)/shard_map/ppermute | solution.py:523
  76.0 3.0 %collective-permute-start.24 = (bf16[256,512]{1,0:T(8,128)(2,1)S(1)}, bf16[256,512]{1,0:T(8,128)(2,1)S(1)}, u32[]{:S(2)}, u32[]{:S(2)}) collective-permute-start(bf16[256,512]{1,0:T(8,128)(2,1)S(1)} %get-tuple-element.104.refs_1_), channel_id=1, source_target_pairs={{0,4},{4,0},{8,12},{12,8},{16,20},{20,16},{24,28},{28,24},{1,5},{5... | collective-permute-start | bytes 786440 | tf_op jit(solution)/shard_map/ppermute | solution.py:523
  76.5 4.0 %collective-permute-start.25 = (bf16[256,512]{1,0:T(8,128)(2,1)S(1)}, bf16[256,512]{1,0:T(8,128)(2,1)S(1)}, u32[]{:S(2)}, u32[]{:S(2)}) collective-permute-start(bf16[256,512]{1,0:T(8,128)(2,1)S(1)} %get-tuple-element.105.refs_2_), channel_id=1, source_target_pairs={{0,4},{4,0},{8,12},{12,8},{16,20},{20,16},{24,28},{28,24},{1,5},{5... | collective-permute-start | bytes 786440 | tf_op jit(solution)/shard_map/ppermute | solution.py:523
  76.6 3.9 %collective-permute-start.26 = (bf16[256,512]{1,0:T(8,128)(2,1)S(1)}, bf16[256,512]{1,0:T(8,128)(2,1)S(1)}, u32[]{:S(2)}, u32[]{:S(2)}) collective-permute-start(bf16[256,512]{1,0:T(8,128)(2,1)S(1)} %get-tuple-element.106.refs_3_), channel_id=1, source_target_pairs={{0,4},{4,0},{8,12},{12,8},{16,20},{20,16},{24,28},{28,24},{1,5},{5... | collective-permute-start | bytes 786440 | tf_op jit(solution)/shard_map/ppermute | solution.py:523
  77.5 10.1 %collective-permute-start.32 = (f16[1040,128]{1,0:T(8,128)(2,1)S(1)}, f16[1040,128]{1,0:T(8,128)(2,1)S(1)}, u32[]{:S(2)}, u32[]{:S(2)}) collective-permute-start(f16[1040,128]{1,0:T(8,128)(2,1)S(1)} %convert_element_type.126), channel_id=1, source_target_pairs={{0,24},{4,28},{8,16},{12,20},{16,8},{20,12},{24,0},{28,4},{1,25},{... | collective-permute-start | bytes 798728 | tf_op jit(solution)/shard_map/ppermute | solution.py:523
  79.0 14.4 %collective-permute-start.30 = (f16[1040,128]{1,0:T(8,128)(2,1)S(1)}, f16[1040,128]{1,0:T(8,128)(2,1)S(1)}, u32[]{:S(2)}, u32[]{:S(2)}) collective-permute-start(f16[1040,128]{1,0:T(8,128)(2,1)S(1)} %convert_element_type.122), channel_id=1, source_target_pairs={{0,8},{4,12},{8,0},{12,4},{16,24},{20,28},{24,16},{28,20},{1,9},{5... | collective-permute-start | bytes 798728 | tf_op jit(solution)/shard_map/ppermute | solution.py:523
  82.2 13.8 %collective-permute-start.28 = (f16[1040,128]{1,0:T(8,128)(2,1)S(1)}, f16[1040,128]{1,0:T(8,128)(2,1)S(1)}, u32[]{:S(2)}, u32[]{:S(2)}) collective-permute-start(f16[1040,128]{1,0:T(8,128)(2,1)S(1)} %convert_element_type.118), channel_id=1, source_target_pairs={{0,16},{4,20},{8,24},{12,28},{16,0},{20,4},{24,8},{28,12},{1,17},{... | collective-permute-start | bytes 798728 | tf_op jit(solution)/shard_map/ppermute | solution.py:523
  84.5 14.6 %collective-permute-start.29 = (f16[1040,128]{1,0:T(8,128)(2,1)S(1)}, f16[1040,128]{1,0:T(8,128)(2,1)S(1)}, u32[]{:S(2)}, u32[]{:S(2)}) collective-permute-start(f16[1040,128]{1,0:T(8,128)(2,1)S(1)} %convert_element_type.120), channel_id=1, source_target_pairs={{0,24},{4,28},{8,16},{12,20},{16,8},{20,12},{24,0},{28,4},{1,25},{... | collective-permute-start | bytes 798728 | tf_op jit(solution)/shard_map/ppermute | solution.py:523
  86.1 18.0 %collective-permute-start.27 = (f16[1040,128]{1,0:T(8,128)(2,1)S(1)}, f16[1040,128]{1,0:T(8,128)(2,1)S(1)}, u32[]{:S(2)}, u32[]{:S(2)}) collective-permute-start(f16[1040,128]{1,0:T(8,128)(2,1)S(1)} %convert_element_type.116), channel_id=1, source_target_pairs={{0,8},{4,12},{8,0},{12,4},{16,24},{20,28},{24,16},{28,20},{1,9},{5... | collective-permute-start | bytes 798728 | tf_op jit(solution)/shard_map/ppermute | solution.py:523
  (13 other events, 35.1 us)

commit v5 on v4

--- a/solution.py
+++ b/solution.py
@@ -10,7 +10,7 @@
 STEPS = 2
 HALO = 4
 WIDE = 2 * HALO
-HEAD = 16
+HEAD = 8
 CHUNKS = 2
 LANES = 128
 QUARTERS = 4
@@ -118,8 +118,7 @@
     return pl.BlockSpec(memory_space=pl.ANY)
 
 
-def cost(flops, moved):
-    return pl.CostEstimate(flops=1000, bytes_accessed=1000, transcendentals=0)
+LIGHT = pl.CostEstimate(flops=1000, bytes_accessed=1000, transcendentals=0)
 
 
 def exponent_of(largest):
@@ -150,7 +149,7 @@
 
             def write(x, carry):
                 start = place_of(x, cells)
-                out[pl.ds(pl.multiple_of(start, 16), cells), :] = (
+                out[pl.ds(pl.multiple_of(start, HEAD), cells), :] = (
                     scratch[x, pl.ds(first, cells), :] * scale
                 )
                 return carry
@@ -184,7 +183,7 @@
         ),
         out_shape=[jax.ShapeDtypeStruct(shape, jnp.float32) for _ in order],
         compiler_params=params(),
-        cost_estimate=cost(1e6, 8 * LANES * planes * width),
+        cost_estimate=LIGHT,
         name="pack",
     )(chip, pltpu.with_memory_space_constraint(distribution, pltpu.HBM), after)
 
@@ -204,7 +203,7 @@
         out_specs=resident(),
         out_shape=jax.ShapeDtypeStruct(shape, jnp.float32),
         compiler_params=params([True] * len(pieces) + [False]),
-        cost_estimate=cost(1e5, 8 * shape[0] * shape[1]),
+        cost_estimate=LIGHT,
         name="message",
     )(*pieces, after)
 
@@ -229,7 +228,7 @@
         out_specs=resident(),
         out_shape=jax.ShapeDtypeStruct(shape, jnp.float32),
         compiler_params=params([True] * len(pieces) + [False]),
-        cost_estimate=cost(1e6, 8 * shape[0] * shape[1]),
+        cost_estimate=LIGHT,
         name="spread",
     )(*pieces, after)
 
@@ -282,7 +281,7 @@
         + [rate] * (2 * CHUNKS),
         scratch_shapes=[pltpu.VMEM((plane, LANES), jnp.float32)],
         compiler_params=params(grid=False),
-        cost_estimate=cost(1e5, 12 * shape[0] * shape[1]),
+        cost_estimate=LIGHT,
         name="arrange",
     )(word, courant.reshape(-1, LANES), collision_rate, next_rate, gain_matrix, product_matrix, after)
     return results[0], results[1], results[2], results[3::2], results[4::2]
@@ -299,59 +298,65 @@
     return [u - (b - a) for u, a, b in zip(values[2:-2], faces[:-1], faces[1:])]
 
 
-def advect_kernel(cells, tile, before, c_ref, extra_ref, *refs):
-    bodies, smoothed_ref, pieces = refs[: -2 - QUARTERS], refs[-1 - QUARTERS], refs[-QUARTERS:]
+def advect_kernel(cells, tile, before, count, parts, c_ref, *refs):
+    extras, bodies = refs[:parts], refs[parts : -2 - count]
+    smoothed_ref, pieces = refs[-1 - count], refs[-count:]
     rows = WIDE * cells
-    sources = [(extra_ref, x * cells) for x in range(WIDE)] if before else []
-    for ref in bodies:
-        sources += [(ref, x * cells) for x in range(ref.shape[0] // cells)]
-    if not before:
-        sources += [(extra_ref, x * cells) for x in range(WIDE)]
-    planes = len(sources) - WIDE
-    share = planes // QUARTERS
-
-    def column(j, outer):
-        lanes = pl.ds(pl.multiple_of(j * LANES, LANES), LANES)
-        speed = c_ref[0:1, lanes]
-        size = jnp.abs(speed)
-        bend = 0.5 * size * (1.0 - size)
-        positive = jnp.broadcast_to(speed, (tile, LANES)) > 0.0
-        back = jnp.exp2(-extra_ref[rows : rows + 1, lanes])
-
-        def body(t, carry):
-            start = t * tile
-
-            def read(x):
-                ref, first = sources[x]
-                value = ref[pl.ds(pl.multiple_of(first + start, tile), tile), lanes]
-                return value * back if ref is extra_ref else value
-
-            section = stage([read(x) for x in range(len(sources))], speed, bend, positive)
-            moved = stage(section, speed, bend, positive)
-            for x in range(planes):
-                result = 0.5 * read(x + HALO) + 0.5 * moved[x]
-                smoothed_ref[pl.ds(pl.multiple_of(x * cells + start, tile), tile), lanes] = result
-                where = pl.ds(pl.multiple_of((x % share) * cells + start, tile), tile)
-                pieces[x // share][where, lanes] = result.astype(jnp.bfloat16)
-            return carry
-
-        return lax.fori_loop(0, cells // tile, body, outer)
-
-    lax.fori_loop(0, extra_ref.shape[1] // LANES, column, 0)
-
-
-def transport(speeds, extra, bodies, before, planes, cells, after):
-    rows, width = planes * cells, extra.shape[1]
+    planes = sum(ref.shape[0] for ref in bodies) // cells
+    share = planes // count
+    base = 0
+    for extra_ref in extras:
+        sources = [(extra_ref, x * cells) for x in range(WIDE)] if before else []
+        for ref in bodies:
+            sources += [(ref, x * cells) for x in range(ref.shape[0] // cells)]
+        if not before:
+            sources += [(extra_ref, x * cells) for x in range(WIDE)]
+
+        def column(j, outer, extra_ref=extra_ref, sources=sources, base=base):
+            lanes = pl.ds(pl.multiple_of(base + j * LANES, LANES), LANES)
+            near = pl.ds(pl.multiple_of(j * LANES, LANES), LANES)
+            speed = c_ref[0:1, lanes]
+            size = jnp.abs(speed)
+            bend = 0.5 * size * (1.0 - size)
+            positive = jnp.broadcast_to(speed, (tile, LANES)) > 0.0
+            back = jnp.exp2(-extra_ref[rows : rows + 1, near])
+
+            def body(t, carry):
+                start = t * tile
+
+                def read(x):
+                    ref, first = sources[x]
+                    where = pl.ds(pl.multiple_of(first + start, tile), tile)
+                    return ref[where, near] * back if ref is extra_ref else ref[where, lanes]
+
+                section = stage([read(x) for x in range(len(sources))], speed, bend, positive)
+                moved = stage(section, speed, bend, positive)
+                for x in range(planes):
+                    result = 0.5 * read(x + HALO) + 0.5 * moved[x]
+                    smoothed_ref[pl.ds(pl.multiple_of(x * cells + start, tile), tile), lanes] = result
+                    where = pl.ds(pl.multiple_of((x % share) * cells + start, tile), tile)
+                    pieces[x // share][where, lanes] = result.astype(jnp.bfloat16)
+                return carry
+
+            return lax.fori_loop(0, cells // tile, body, outer)
+
+        lax.fori_loop(0, extra_ref.shape[1] // LANES, column, 0)
+        base += extra_ref.shape[1]
+
+
+def transport(speeds, extras, bodies, before, planes, cells, after):
+    count = QUARTERS
+    rows, width = planes * cells, speeds.shape[1]
     results = pl.pallas_call(
-        functools.partial(advect_kernel, cells, 16, before),
-        in_specs=[resident()] * (2 + len(bodies)) + [anywhere()],
-        out_specs=[resident()] * (1 + QUARTERS),
+        functools.partial(advect_kernel, cells, 16, before, count, len(extras)),
+        in_specs=[resident()] * (1 + len(extras) + len(bodies)) + [anywhere()],
+        out_specs=[resident()] * (1 + count),
         out_shape=[jax.ShapeDtypeStruct((rows, width), jnp.float32)]
-        + [jax.ShapeDtypeStruct((rows // QUARTERS, width), jnp.bfloat16)] * QUARTERS,
+        + [jax.ShapeDtypeStruct((rows // count, width), jnp.bfloat16)] * count,
         compiler_params=params(grid=False),
-        cost_estimate=cost(40 * rows * width, 12 * rows * width),
+        cost_estimate=LIGHT,
         name="transport",
-    )(speeds, extra, *bodies, after)
+    )(speeds, *extras, *bodies, after)
     return results[0], results[1:]
 
 
@@ -409,18 +414,18 @@
         out_specs=[resident()] * len(shapes),
         out_shape=shapes,
         compiler_params=params(grid=False),
-        cost_estimate=cost(8 * rows * width * width, 20 * rows * width),
+        cost_estimate=LIGHT,
         name="faces" if sends else "inside",
     )(*own, *other, smoothed, rate, gain, product, after)
 
 
-def final_kernel(part, *refs):
-    own, other = refs[:QUARTERS], refs[QUARTERS : 2 * QUARTERS]
-    smoothed_ref, rate_ref, gain_ref, product_ref = refs[2 * QUARTERS : 2 * QUARTERS + 4]
-    outs, scratch = refs[2 * QUARTERS + 5 : -1], refs[-1]
+def final_kernel(part, count, *refs):
+    own, other = refs[:count], refs[count : 2 * count]
+    smoothed_ref, rate_ref, gain_ref, product_ref = refs[2 * count : 2 * count + 4]
+    outs, scratch = refs[2 * count + 5 : -1], refs[-1]
     rows, group = scratch.shape
     columns = slice(part * group, (part + 1) * group)
-    half = QUARTERS // 2
+    half = count // 2
     size = rows // 2
     for index in range(2):
         lines = slice(index * size, (index + 1) * size)
@@ -455,13 +460,13 @@
     group = 2 * LANES
     shape = jax.ShapeDtypeStruct((rows + HEAD, LANES), jnp.float32)
     return pl.pallas_call(
-        functools.partial(final_kernel, part),
-        in_specs=[resident()] * (2 * QUARTERS + 4) + [anywhere()],
+        functools.partial(final_kernel, part, len(own)),
+        in_specs=[resident()] * (2 * len(own) + 4) + [anywhere()],
         out_specs=[resident()] * 2,
         out_shape=[shape] * 2,
         scratch_shapes=[pltpu.VMEM((rows, group), jnp.float32)],
         compiler_params=params(grid=False),
-        cost_estimate=cost(8 * rows * width * group, 20 * rows * group),
+        cost_estimate=LIGHT,
         name="final",
     )(*own, *other, smoothed, rate, gain, product, after)
 
@@ -513,7 +518,7 @@
         out_shape=jax.ShapeDtypeStruct(shape, jnp.float32),
         input_output_aliases=aliases,
         compiler_params=params([False] + [True] * count + [False] * (len(operands) - count)),
-        cost_estimate=cost(1e6, 8 * LANES * planes * width),
+        cost_estimate=LIGHT,
         name="unpack",
     )(chip, *operands)
 
@@ -534,6 +539,11 @@
 
 def full(array):
     return array.astype(jnp.float32)
+
+
+def across(message, step, widths):
+    cuts = [sum(widths[:i]) for i in range(len(widths) + 1)]
+    return [shift(half(message[:, a:b]), step) for a, b in zip(cuts[:-1], cuts[1:])]
 
 
 def body(distribution, courant, gain_matrix, product_matrix, collision_rate):
@@ -543,56 +553,70 @@
     chip, core = lax.shift_right_logical(member, 1), member & 1
     order = list(range(1, chips)) + [0]
     cells = plane // (chips * CHUNKS)
-    span = cells * chips
+    width = chips * LANES
+    rows = WIDE * cells + HEAD
     word = jnp.stack([chip, core])
-
     every = range(CHUNKS)
-    sent, extra, local, state = {}, {}, {}, {}
+    sent, extra, local, state, packed = {}, {}, {}, {}, {}
+
     after = distribution
     for k in every:
         pieces = pack(distribution, word, order, k, cells, after)
-        after = pieces[-1]
-        sent[k] = [
-            a if m == 0 else full(exchange(half(a), 2 * m)) for a, m in zip(pieces, order)
-        ]
+        after = packed[k] = pieces[-1]
+        sent[k] = [a if m == 0 else exchange(half(a), 2 * m) for a, m in zip(pieces, order)]
+    near_rate, packed[0] = lax.optimization_barrier((collision_rate[:8], packed[0]))
     speeds, gain, product, shifted_rates, rates = arrange(
-        courant, collision_rate, shift(collision_rate[:8], -1), gain_matrix, product_matrix,
+        courant, collision_rate, shift(near_rate, -1), gain_matrix, product_matrix,
         word, order, cells, after,
     )
-    after = product
+
+    soon, after = lax.optimization_barrier((shift(half(packed[0][:rows]), -1), product))
     for k in every:
-        message = message_of(sent[k], cells, after)
-        extra[k] = shift(half(message), -1)
-        local[k] = after = spread(sent[k], planes, cells, message)
+        whole = [a if m == 0 else full(a) for a, m in zip(sent[k], order)]
+        if k == 0:
+            message = message_of(whole[:-1], cells, after)
+            extra[k] = across(message, -1, [2 * LANES, width - 3 * LANES]) + [soon]
+        else:
+            message = message_of(whole, cells, after)
+            extra[k] = across(message, -1, [width])
+        local[k] = after = spread(whole, planes, cells, message)
+
     middle = QUARTERS // 2
     for k in every:
-        arrived, after = lax.optimization_barrier((extra[k], after))
-        smoothed, own = transport(speeds, full(arrived), [local[k]], False, planes, cells, after)
+        extra[k], after = lax.optimization_barrier((extra[k], after))
+        arrived = [full(e) for e in extra[k]]
+        smoothed, own = transport(speeds, arrived, [local[k]], False, planes, cells, after)
         other = [exchange(a, 1) for a in own]
         upper, message = collide_half(
             own[middle:], other[middle:], smoothed, shifted_rates[k], gain, product,
-            WIDE * cells, True, after,
+            WIDE * cells, True, smoothed,
         )
-        extra[k] = shift(half(message), 1)
+        extra[k] = across(message, 1, [width])
         (lower,) = collide_half(
             own[:middle], other[:middle], smoothed, shifted_rates[k], gain, product,
             0, False, message,
         )
         state[k] = [lower, upper]
         after = lower
+
     back = {}
     for k in every:
-        arrived, after = lax.optimization_barrier((extra[k], after))
-        smoothed, own = transport(speeds, full(arrived), state[k], True, planes, cells, after)
+        extra[k], after = lax.optimization_barrier((extra[k], after))
+        arrived = [full(e) for e in extra[k]]
+        smoothed, own = transport(speeds, arrived, state[k], True, planes, cells, after)
+        if k:
+            own, ahead = lax.optimization_barrier((own, back[k - 1][:2]))
+            back[k - 1] = [*ahead, *back[k - 1][2:]]
         other = [exchange(a, 1) for a in own]
         ready = []
         for part in range(chips // 2):
             ready += final(own, other, smoothed, rates[k], gain, product, part, after)
             after = ready[-1]
-        back[k] = [a if m == 0 else full(exchange(half(a), 2 * m)) for a, m in zip(ready, order)]
+        back[k] = [a if m == 0 else exchange(half(a), 2 * m) for a, m in zip(ready, order)]
     result = None
     for k in every:
-        result = unpack(back[k], result, word, order, k, planes, cells, after)
+        pieces = [a if m == 0 else full(a) for a, m in zip(back[k], order)]
+        result = unpack(pieces, result, word, order, k, planes, cells, after)
     return result
 
 
@@ -601,7 +625,7 @@
     local, planes = shape[0] // groups, shape[1] // spaces
     chips = groups // 2
     return (
-        groups % 4 == 0
+        groups == 8
         and chips & (chips - 1) == 0
         and local == LANES
         and planes == 2 * WIDE

time: 107 us -> 101 us (0.944)
  waiting for transfers between devices: 33.8 us -> 28.3 us
    ppermute x28, waiting for transfers between devices: 25.5 us -> 22 us  [exchange(): return lax.ppermute(array, 'vel', [(i, i ^ mask) for i in range(count)])]
    ppermute x5 -> x7, waiting for transfers between devices: 8.33 us -> 6.31 us  [shift(): lax.ppermute(array, 'space', [(i, (i + step) % count) for i in range(coun...]
    ppermute x5 -> x7, starting transfers between devices: 11.9 us -> 11.9 us  [shift(): lax.ppermute(array, 'space', [(i, (i + step) % count) for i in range(coun...]
  transfers between devices with their start and end apart: 33 -> 35, of which waited for: 22 -> 20; matrix products, arithmetic and copies ran while one was open for 2% -> 2% of each run, Pallas kernels for 30% -> 32%
where the time goes in v5:
time: 101 us
  Pallas kernels  37.7 us (37%)
  starting transfers between devices  32 us (32%)
  waiting for transfers between devices  28.3 us (28%)
  other arithmetic  1.82 us (2%)
    ppermute x28, waiting for transfers between devices, exchange(): return lax.ppermute(array, 'vel', [(i, i ^ mask) for i in range(count)])  22 us
    ppermute x28, starting transfers between devices, exchange(): return lax.ppermute(array, 'vel', [(i, i ^ mask) for i in range(count)])  20.2 us
    ppermute x7, starting transfers between devices, shift(): lax.ppermute(array, 'space', [(i, (i + step) % count) for i in range(coun...  11.9 us
    pallas_call x4, Pallas kernels, transport(): pl.pallas_call(functools.partial(advect_kernel, cells, 16, before, count,...  11.2 us
    pallas_call x2, Pallas kernels, pack(): pl.pallas_call(functools.partial(pack_kernel, order, planes, cells), grid...  7.04 us
    pallas_call x4, Pallas kernels, final(): pl.pallas_call(functools.partial(final_kernel, part, len(own)), in_specs=...  6.53 us
    ppermute x7, waiting for transfers between devices, shift(): lax.ppermute(array, 'space', [(i, (i + step) % count) for i in range(coun...  6.31 us
    pallas_call x4, Pallas kernels, collide_half(): pl.pallas_call(functools.partial(half_kernel, len(own), first, sends), in...  5.66 us
  transfers between devices with their start and end apart: 35, of which 20 were waited for; matrix products, arithmetic and copies ran while one was open for 2% of the time, Pallas kernels for 32%

profile of v5, /device:TPU:0, one launch (start us, length us, event | category | flops | bytes accessed | tf_op | source)
XLA Modules:
  0.0 100.6 jit_solution(12175734130579188709)
XLA Ops:
  0.1 3.5 %pack.2 = (f32[1032,128]{1,0:T(8,128)S(1)}, f32[1032,128]{1,0:T(8,128)S(1)}, f32[1032,128]{1,0:T(8,128)S(1)}, f32[1032,128]{1,0:T(8,128)S(1)}) custom-call(s32[2]{0:T(128)S(1)} %pad_add_fusion.chip_ref.word_ref, f32[128,16,512]{2,1,0:T(8,128)} %d_ref.3, f32[128,16,512]{2,1,0:T(8,128)} %d_ref.3), custom_call_target="tpu_custom_call" | custom-call | flops 1000 | bytes 1000 | tf_op jit(solution)/shard_map/pack/pallas_call | solution.py:172
  3.6 4.0 %collective-permute-start.6 = (f16[1032,128]{1,0:T(8,128)(2,1)S(1)}, f16[1032,128]{1,0:T(8,128)(2,1)S(1)}, u32[]{:S(2)}, u32[]{:S(2)}) collective-permute-start(f16[1032,128]{1,0:T(8,128)(2,1)S(1)} %convert_element_type.112), channel_id=1, source_target_pairs={{0,24},{4,28},{8,16},{12,20},{16,8},{20,12},{24,0},{28,4},{1,25},{... | collective-permute-start | bytes 792584 | tf_op jit(solution)/shard_map/ppermute | solution.py:528
  8.4 4.1 %collective-permute-start.7 = (f16[520,128]{1,0:T(8,128)(2,1)S(1)}, f16[520,128]{1,0:T(8,128)(2,1)S(1)}, u32[]{:S(2)}, u32[]{:S(2)}) collective-permute-start(f16[520,128]{1,0:T(8,128)(2,1)S(1)} %slice_convert_fusion), channel_id=1, source_target_pairs={{0,3},{1,0},{2,1},{3,2},{4,7},{5,4},{6,5},{7,6},{8,11},{9,8},{10,9... | collective-permute-start | bytes 399368 | tf_op jit(solution)/shard_map/ppermute | solution.py:533
  13.0 3.6 %pack.3 = (f32[1032,128]{1,0:T(8,128)S(1)}, f32[1032,128]{1,0:T(8,128)S(1)}, f32[1032,128]{1,0:T(8,128)S(1)}, f32[1032,128]{1,0:T(8,128)S(1)}) custom-call(s32[2]{0:T(128)S(1)} %pad_add_fusion.chip_ref.word_ref, f32[128,16,512]{2,1,0:T(8,128)} %d_ref.3, f32[1032,128]{1,0:T(8,128)S(1)} %get-tuple-element.82.after_ref.refs_3_), custom_call_target="tpu_custom_call" | custom-call | flops 1000 | bytes 1000 | tf_op jit(solution)/shard_map/pack/pallas_call | solution.py:172
  16.7 2.5 %collective-permute-start.3 = (f16[1032,128]{1,0:T(8,128)(2,1)S(1)}, f16[1032,128]{1,0:T(8,128)(2,1)S(1)}, u32[]{:S(2)}, u32[]{:S(2)}) collective-permute-start(f16[1032,128]{1,0:T(8,128)(2,1)S(1)} %convert_element_type.106), channel_id=1, source_target_pairs={{0,24},{4,28},{8,16},{12,20},{16,8},{20,12},{24,0},{28,4},{1,25},{... | collective-permute-start | bytes 792584 | tf_op jit(solution)/shard_map/ppermute | solution.py:528
  22.1 2.9 %collective-permute-start.9 = (f16[520,256]{1,0:T(8,128)(2,1)S(1)}, f16[520,256]{1,0:T(8,128)(2,1)S(1)}, u32[]{:S(2)}, u32[]{:S(2)}) collective-permute-start(f16[520,256]{1,0:T(8,128)(2,1)S(1)} %slice.20), channel_id=1, source_target_pairs={{0,3},{1,0},{2,1},{3,2},{4,7},{5,4},{6,5},{7,6},{8,11},{9,8},{10,9... | collective-permute-start | bytes 798728 | tf_op jit(solution)/shard_map/ppermute | solution.py:533
  27.1 3.9 %collective-permute-done.2 = f16[1032,128]{1,0:T(8,128)(2,1)S(1)} collective-permute-done((f16[1032,128]{1,0:T(8,128)(2,1)S(1)}, f16[1032,128]{1,0:T(8,128)(2,1)S(1)}, u32[]{:S(2)}, u32[]{:S(2)}) %collective-permute-start.2) | collective-permute-done | bytes 264224 | tf_op jit(solution)/shard_map/ppermute | solution.py:528
  31.5 3.7 %collective-permute-start.8 = (f16[520,512]{1,0:T(8,128)(2,1)S(1)}, f16[520,512]{1,0:T(8,128)(2,1)S(1)}, u32[]{:S(2)}, u32[]{:S(2)}) collective-permute-start(f16[520,512]{1,0:T(8,128)(2,1)S(1)} %convert_element_type.114), channel_id=1, source_target_pairs={{0,3},{1,0},{2,1},{3,2},{4,7},{5,4},{6,5},{7,6},{8,11},{9,8},{10,9... | collective-permute-start | bytes 1597448 | tf_op jit(solution)/shard_map/ppermute | solution.py:533
  35.6 2.7 %transport.4 = (f32[1024,512]{1,0:T(8,128)S(1)}, bf16[256,512]{1,0:T(8,128)(2,1)S(1)}, bf16[256,512]{1,0:T(8,128)(2,1)S(1)}, bf16[256,512]{1,0:T(8,128)(2,1)S(1)}, bf16[256,512]{1,0:T(8,128)(2,1)S(1)}) custom-call(f32[8,512]{1,0:T(8,128)S(1)} %get-tuple-element.75.c_ref, f32[520,256]{1,0:T(8,128)S(1)} %convert_element_type.115.refs_0_, ...), custom_call_target="tpu_custom_call" | custom-call | flops 1000 | bytes 1000 | tf_op jit(solution)/shard_map/transport/pallas_call | solution.py:350
  45.3 2.5 %collective-permute-done.8 = f16[520,512]{1,0:T(8,128)(2,1)S(1)} collective-permute-done((f16[520,512]{1,0:T(8,128)(2,1)S(1)}, f16[520,512]{1,0:T(8,128)(2,1)S(1)}, u32[]{:S(2)}, u32[]{:S(2)}) %collective-permute-start.8) | collective-permute-done | bytes 532512 | tf_op jit(solution)/shard_map/ppermute | solution.py:533
  47.9 2.8 %transport.5 = (f32[1024,512]{1,0:T(8,128)S(1)}, bf16[256,512]{1,0:T(8,128)(2,1)S(1)}, bf16[256,512]{1,0:T(8,128)(2,1)S(1)}, bf16[256,512]{1,0:T(8,128)(2,1)S(1)}, bf16[256,512]{1,0:T(8,128)(2,1)S(1)}) custom-call(f32[8,512]{1,0:T(8,128)S(1)} %get-tuple-element.75.c_ref, f32[520,512]{1,0:T(8,128)S(1)} %convert_element_type.118.refs_0_, ...), custom_call_target="tpu_custom_call" | custom-call | flops 1000 | bytes 1000 | tf_op jit(solution)/shard_map/transport/pallas_call | solution.py:350
  52.7 1.5 %faces.3 = (f32[512,512]{1,0:T(8,128)S(1)}, f32[520,512]{1,0:T(8,128)S(1)}) custom-call(bf16[256,512]{1,0:T(8,128)(2,1)S(1)} %get-tuple-element.100.refs_0_, bf16[256,512]{1,0:T(8,128)(2,1)S(1)} %get-tuple-element.101.refs_1_, bf16[256,512]{1,0:T(8,128)(2,1)S(1)} %collective-permute-done.15.refs_2_, bf16[256,512]{1,0:T(8,128)(2,1)S(1)} %collective-permute-done.16.refs_3_, ...), custom_call_target="tpu_custom_call" | custom-call | flops 1000 | bytes 1000 | tf_op jit(solution)/shard_map/faces/pallas_call | solution.py:411
  55.9 3.3 %collective-permute-done.18 = f16[520,512]{1,0:T(8,128)(2,1)S(1)} collective-permute-done((f16[520,512]{1,0:T(8,128)(2,1)S(1)}, f16[520,512]{1,0:T(8,128)(2,1)S(1)}, u32[]{:S(2)}, u32[]{:S(2)}) %collective-permute-start.18) | collective-permute-done | bytes 532512 | tf_op jit(solution)/shard_map/ppermute | solution.py:533
  59.3 2.9 %transport.6 = (f32[1024,512]{1,0:T(8,128)S(1)}, bf16[256,512]{1,0:T(8,128)(2,1)S(1)}, bf16[256,512]{1,0:T(8,128)(2,1)S(1)}, bf16[256,512]{1,0:T(8,128)(2,1)S(1)}, bf16[256,512]{1,0:T(8,128)(2,1)S(1)}) custom-call(f32[8,512]{1,0:T(8,128)S(1)} %get-tuple-element.75.c_ref, f32[520,512]{1,0:T(8,128)S(1)} %convert_element_type.121.refs_0_, ...), custom_call_target="tpu_custom_call" | custom-call | flops 1000 | bytes 1000 | tf_op jit(solution)/shard_map/transport/pallas_call | solution.py:350
  64.9 1.6 %final.4 = (f32[1032,128]{1,0:T(8,128)S(1)}, f32[1032,128]{1,0:T(8,128)S(1)}) custom-call(bf16[256,512]{1,0:T(8,128)(2,1)S(1)} %get-tuple-element.110.refs_0_, bf16[256,512]{1,0:T(8,128)(2,1)S(1)} %get-tuple-element.111.refs_1_, bf16[256,512]{1,0:T(8,128)(2,1)S(1)} %get-tuple-element.112.refs_2_, bf16[256,512]{1,0:T(8,128)(2,1)S(1)} %get-tuple-element.113.refs_3_, ...), custom_call_target="tpu_custom_call" | custom-call | flops 1000 | bytes 1000 | tf_op jit(solution)/shard_map/final/pallas_call | solution.py:462
  69.1 1.6 %final.5 = (f32[1032,128]{1,0:T(8,128)S(1)}, f32[1032,128]{1,0:T(8,128)S(1)}) custom-call(bf16[256,512]{1,0:T(8,128)(2,1)S(1)} %get-tuple-element.110.refs_0_, bf16[256,512]{1,0:T(8,128)(2,1)S(1)} %get-tuple-element.111.refs_1_, bf16[256,512]{1,0:T(8,128)(2,1)S(1)} %get-tuple-element.112.refs_2_, bf16[256,512]{1,0:T(8,128)(2,1)S(1)} %get-tuple-element.113.refs_3_, ...), custom_call_target="tpu_custom_call" | custom-call | flops 1000 | bytes 1000 | tf_op jit(solution)/shard_map/final/pallas_call | solution.py:462
  71.3 2.9 %transport.7 = (f32[1024,512]{1,0:T(8,128)S(1)}, bf16[256,512]{1,0:T(8,128)(2,1)S(1)}, bf16[256,512]{1,0:T(8,128)(2,1)S(1)}, bf16[256,512]{1,0:T(8,128)(2,1)S(1)}, bf16[256,512]{1,0:T(8,128)(2,1)S(1)}) custom-call(f32[8,512]{1,0:T(8,128)S(1)} %get-tuple-element.75.c_ref, f32[520,512]{1,0:T(8,128)S(1)} %convert_element_type.122.refs_0_, ...), custom_call_target="tpu_custom_call" | custom-call | flops 1000 | bytes 1000 | tf_op jit(solution)/shard_map/transport/pallas_call | solution.py:350
  77.3 1.6 %collective-permute-start.34 = (f16[1032,128]{1,0:T(8,128)(2,1)S(1)}, f16[1032,128]{1,0:T(8,128)(2,1)S(1)}, u32[]{:S(2)}, u32[]{:S(2)}) collective-permute-start(f16[1032,128]{1,0:T(8,128)(2,1)S(1)} %convert_element_type.133), channel_id=1, source_target_pairs={{0,24},{4,28},{8,16},{12,20},{16,8},{20,12},{24,0},{28,4},{1,25},{... | collective-permute-start | bytes 792584 | tf_op jit(solution)/shard_map/ppermute | solution.py:528
  79.0 1.6 %final.6 = (f32[1032,128]{1,0:T(8,128)S(1)}, f32[1032,128]{1,0:T(8,128)S(1)}) custom-call(bf16[256,512]{1,0:T(8,128)(2,1)S(1)} %get-tuple-element.126.refs_0_, bf16[256,512]{1,0:T(8,128)(2,1)S(1)} %get-tuple-element.127.refs_1_, bf16[256,512]{1,0:T(8,128)(2,1)S(1)} %get-tuple-element.128.refs_2_, bf16[256,512]{1,0:T(8,128)(2,1)S(1)} %get-tuple-element.129.refs_3_, ...), custom_call_target="tpu_custom_call" | custom-call | flops 1000 | bytes 1000 | tf_op jit(solution)/shard_map/final/pallas_call | solution.py:462
  80.6 1.6 %final.7 = (f32[1032,128]{1,0:T(8,128)S(1)}, f32[1032,128]{1,0:T(8,128)S(1)}) custom-call(bf16[256,512]{1,0:T(8,128)(2,1)S(1)} %get-tuple-element.126.refs_0_, bf16[256,512]{1,0:T(8,128)(2,1)S(1)} %get-tuple-element.127.refs_1_, bf16[256,512]{1,0:T(8,128)(2,1)S(1)} %get-tuple-element.128.refs_2_, bf16[256,512]{1,0:T(8,128)(2,1)S(1)} %get-tuple-element.129.refs_3_, ...), custom_call_target="tpu_custom_call" | custom-call | flops 1000 | bytes 1000 | tf_op jit(solution)/shard_map/final/pallas_call | solution.py:462
  83.2 1.5 %collective-permute-start.33 = (f16[1032,128]{1,0:T(8,128)(2,1)S(1)}, f16[1032,128]{1,0:T(8,128)(2,1)S(1)}, u32[]{:S(2)}, u32[]{:S(2)}) collective-permute-start(f16[1032,128]{1,0:T(8,128)(2,1)S(1)} %convert_element_type.129), channel_id=1, source_target_pairs={{0,24},{4,28},{8,16},{12,20},{16,8},{20,12},{24,0},{28,4},{1,25},{... | collective-permute-start | bytes 792584 | tf_op jit(solution)/shard_map/ppermute | solution.py:528
  86.9 2.5 %unpack.2.refs_5_ = f32[128,16,512]{2,1,0:T(8,128)} custom-call(s32[2]{0:T(128)S(1)} %pad_add_fusion.chip_ref.word_ref, f32[1032,128]{1,0:T(8,128)S(1)} %convert_element_type.131.refs_0_, f32[1032,128]{1,0:T(8,128)S(1)} %convert_element_type.132.refs_1_, f32[1032,128]{1,0:T(8,128)S(1)} %convert_element_type.134.refs_2_, ...), custom_call_target="tpu_custom_call" | custom-call | flops 1000 | bytes 1000 | tf_op jit(solution)/shard_map/unpack/pallas_call | solution.py:509
  89.4 8.5 %collective-permute-done.32 = f16[1032,128]{1,0:T(8,128)(2,1)S(1)} collective-permute-done((f16[1032,128]{1,0:T(8,128)(2,1)S(1)}, f16[1032,128]{1,0:T(8,128)(2,1)S(1)}, u32[]{:S(2)}, u32[]{:S(2)}) %collective-permute-start.32) | collective-permute-done | bytes 264224 | tf_op jit(solution)/shard_map/ppermute | solution.py:528
  98.0 2.5 %unpack.3 = f32[128,16,512]{2,1,0:T(8,128)} custom-call(s32[2]{0:T(128)S(1)} %pad_add_fusion.chip_ref.word_ref, f32[1032,128]{1,0:T(8,128)S(1)} %convert_element_type.126.refs_0_, f32[1032,128]{1,0:T(8,128)S(1)} %convert_element_type.128.refs_1_, f32[1032,128]{1,0:T(8,128)S(1)} %convert_element_type.130.refs_2_, ...), custom_call_target="tpu_custom_call", output_to_operand_aliasing={{}: (6, {})} | custom-call | flops 1000 | bytes 1000 | tf_op jit(solution)/shard_map/unpack/pallas_call | solution.py:509
  (114 shorter events, 30.3 us)
Async XLA Ops:
  3.6 16.1 %collective-permute-start.6 = (f16[1032,128]{1,0:T(8,128)(2,1)S(1)}, f16[1032,128]{1,0:T(8,128)(2,1)S(1)}, u32[]{:S(2)}, u32[]{:S(2)}) collective-permute-start(f16[1032,128]{1,0:T(8,128)(2,1)S(1)} %convert_element_type.112), channel_id=1, source_target_pairs={{0,24},{4,28},{8,16},{12,20},{16,8},{20,12},{24,0},{28,4},{1,25},{... | collective-permute-start | bytes 792584 | tf_op jit(solution)/shard_map/ppermute | solution.py:528
  7.6 14.2 %collective-permute-start.5 = (f16[1032,128]{1,0:T(8,128)(2,1)S(1)}, f16[1032,128]{1,0:T(8,128)(2,1)S(1)}, u32[]{:S(2)}, u32[]{:S(2)}) collective-permute-start(f16[1032,128]{1,0:T(8,128)(2,1)S(1)} %convert_element_type.110), channel_id=1, source_target_pairs={{0,16},{4,20},{8,24},{12,28},{16,0},{20,4},{24,8},{28,12},{1,17},{... | collective-permute-start | bytes 792584 | tf_op jit(solution)/shard_map/ppermute | solution.py:528
  8.2 13.6 %collective-permute-start.4 = (f16[1032,128]{1,0:T(8,128)(2,1)S(1)}, f16[1032,128]{1,0:T(8,128)(2,1)S(1)}, u32[]{:S(2)}, u32[]{:S(2)}) collective-permute-start(f16[1032,128]{1,0:T(8,128)(2,1)S(1)} %convert_element_type.108), channel_id=1, source_target_pairs={{0,8},{4,12},{8,0},{12,4},{16,24},{20,28},{24,16},{28,20},{1,9},{5... | collective-permute-start | bytes 792584 | tf_op jit(solution)/shard_map/ppermute | solution.py:528
  8.4 10.8 %collective-permute-start.7 = (f16[520,128]{1,0:T(8,128)(2,1)S(1)}, f16[520,128]{1,0:T(8,128)(2,1)S(1)}, u32[]{:S(2)}, u32[]{:S(2)}) collective-permute-start(f16[520,128]{1,0:T(8,128)(2,1)S(1)} %slice_convert_fusion), channel_id=1, source_target_pairs={{0,3},{1,0},{2,1},{3,2},{4,7},{5,4},{6,5},{7,6},{8,11},{9,8},{10,9... | collective-permute-start | bytes 399368 | tf_op jit(solution)/shard_map/ppermute | solution.py:533
  12.5 4.2 %collective-permute-start = (f32[8,512]{1,0:T(8,128)S(1)}, f32[8,512]{1,0:T(8,128)S(1)}, u32[]{:S(2)}, u32[]{:S(2)}) collective-permute-start(f32[8,512]{1,0:T(8,128)S(1)} %slice.15), channel_id=1, source_target_pairs={{0,3},{1,0},{2,1},{3,2},{4,7},{5,4},{6,5},{7,6},{8,11},{9,8},{10,9... | collective-permute-start | bytes 49160 | tf_op jit(solution)/shard_map/ppermute | solution.py:533
  16.7 10.3 %collective-permute-start.3 = (f16[1032,128]{1,0:T(8,128)(2,1)S(1)}, f16[1032,128]{1,0:T(8,128)(2,1)S(1)}, u32[]{:S(2)}, u32[]{:S(2)}) collective-permute-start(f16[1032,128]{1,0:T(8,128)(2,1)S(1)} %convert_element_type.106), channel_id=1, source_target_pairs={{0,24},{4,28},{8,16},{12,20},{16,8},{20,12},{24,0},{28,4},{1,25},{... | collective-permute-start | bytes 792584 | tf_op jit(solution)/shard_map/ppermute | solution.py:528
  19.2 11.7 %collective-permute-start.2 = (f16[1032,128]{1,0:T(8,128)(2,1)S(1)}, f16[1032,128]{1,0:T(8,128)(2,1)S(1)}, u32[]{:S(2)}, u32[]{:S(2)}) collective-permute-start(f16[1032,128]{1,0:T(8,128)(2,1)S(1)} %convert_element_type.104), channel_id=1, source_target_pairs={{0,16},{4,20},{8,24},{12,28},{16,0},{20,4},{24,8},{28,12},{1,17},{... | collective-permute-start | bytes 792584 | tf_op jit(solution)/shard_map/ppermute | solution.py:528
  19.7 11.5 %collective-permute-start.1 = (f16[1032,128]{1,0:T(8,128)(2,1)S(1)}, f16[1032,128]{1,0:T(8,128)(2,1)S(1)}, u32[]{:S(2)}, u32[]{:S(2)}) collective-permute-start(f16[1032,128]{1,0:T(8,128)(2,1)S(1)} %convert_element_type.102), channel_id=1, source_target_pairs={{0,8},{4,12},{8,0},{12,4},{16,24},{20,28},{24,16},{28,20},{1,9},{5... | collective-permute-start | bytes 792584 | tf_op jit(solution)/shard_map/ppermute | solution.py:528
  22.1 13.4 %collective-permute-start.9 = (f16[520,256]{1,0:T(8,128)(2,1)S(1)}, f16[520,256]{1,0:T(8,128)(2,1)S(1)}, u32[]{:S(2)}, u32[]{:S(2)}) collective-permute-start(f16[520,256]{1,0:T(8,128)(2,1)S(1)} %slice.20), channel_id=1, source_target_pairs={{0,3},{1,0},{2,1},{3,2},{4,7},{5,4},{6,5},{7,6},{8,11},{9,8},{10,9... | collective-permute-start | bytes 798728 | tf_op jit(solution)/shard_map/ppermute | solution.py:533
  25.0 10.5 %collective-permute-start.10 = (f16[520,128]{1,0:T(8,128)(2,1)S(1)}, f16[520,128]{1,0:T(8,128)(2,1)S(1)}, u32[]{:S(2)}, u32[]{:S(2)}) collective-permute-start(f16[520,128]{1,0:T(8,128)(2,1)S(1)} %slice.21), channel_id=1, source_target_pairs={{0,3},{1,0},{2,1},{3,2},{4,7},{5,4},{6,5},{7,6},{8,11},{9,8},{10,9... | collective-permute-start | bytes 399368 | tf_op jit(solution)/shard_map/ppermute | solution.py:533
  31.5 16.3 %collective-permute-start.8 = (f16[520,512]{1,0:T(8,128)(2,1)S(1)}, f16[520,512]{1,0:T(8,128)(2,1)S(1)}, u32[]{:S(2)}, u32[]{:S(2)}) collective-permute-start(f16[520,512]{1,0:T(8,128)(2,1)S(1)} %convert_element_type.114), channel_id=1, source_target_pairs={{0,3},{1,0},{2,1},{3,2},{4,7},{5,4},{6,5},{7,6},{8,11},{9,8},{10,9... | collective-permute-start | bytes 1597448 | tf_op jit(solution)/shard_map/ppermute | solution.py:533
  41.9 17.3 %collective-permute-start.18 = (f16[520,512]{1,0:T(8,128)(2,1)S(1)}, f16[520,512]{1,0:T(8,128)(2,1)S(1)}, u32[]{:S(2)}, u32[]{:S(2)}) collective-permute-start(f16[520,512]{1,0:T(8,128)(2,1)S(1)} %convert_element_type.120), channel_id=1, source_target_pairs={{0,1},{1,2},{2,3},{3,0},{4,5},{5,6},{6,7},{7,4},{8,9},{9,10},{10,1... | collective-permute-start | bytes 1597448 | tf_op jit(solution)/shard_map/ppermute | solution.py:533
  51.3 3.3 %collective-permute-start.19 = (bf16[256,512]{1,0:T(8,128)(2,1)S(1)}, bf16[256,512]{1,0:T(8,128)(2,1)S(1)}, u32[]{:S(2)}, u32[]{:S(2)}) collective-permute-start(bf16[256,512]{1,0:T(8,128)(2,1)S(1)} %get-tuple-element.105.refs_0_), channel_id=1, source_target_pairs={{0,4},{4,0},{8,12},{12,8},{16,20},{20,16},{24,28},{28,24},{1,5},{5... | collective-permute-start | bytes 786440 | tf_op jit(solution)/shard_map/ppermute | solution.py:528
  51.3 3.2 %collective-permute-start.20 = (bf16[256,512]{1,0:T(8,128)(2,1)S(1)}, bf16[256,512]{1,0:T(8,128)(2,1)S(1)}, u32[]{:S(2)}, u32[]{:S(2)}) collective-permute-start(bf16[256,512]{1,0:T(8,128)(2,1)S(1)} %get-tuple-element.106.refs_1_), channel_id=1, source_target_pairs={{0,4},{4,0},{8,12},{12,8},{16,20},{20,16},{24,28},{28,24},{1,5},{5... | collective-permute-start | bytes 786440 | tf_op jit(solution)/shard_map/ppermute | solution.py:528
  54.3 16.9 %collective-permute-start.17 = (f16[520,512]{1,0:T(8,128)(2,1)S(1)}, f16[520,512]{1,0:T(8,128)(2,1)S(1)}, u32[]{:S(2)}, u32[]{:S(2)}) collective-permute-start(f16[520,512]{1,0:T(8,128)(2,1)S(1)} %convert_element_type.119), channel_id=1, source_target_pairs={{0,1},{1,2},{2,3},{3,0},{4,5},{5,6},{6,7},{7,4},{8,9},{9,10},{10,1... | collective-permute-start | bytes 1597448 | tf_op jit(solution)/shard_map/ppermute | solution.py:533
  66.7 8.5 %collective-permute-start.26 = (f16[1032,128]{1,0:T(8,128)(2,1)S(1)}, f16[1032,128]{1,0:T(8,128)(2,1)S(1)}, u32[]{:S(2)}, u32[]{:S(2)}) collective-permute-start(f16[1032,128]{1,0:T(8,128)(2,1)S(1)} %convert_element_type.124), channel_id=1, source_target_pairs={{0,16},{4,20},{8,24},{12,28},{16,0},{20,4},{24,8},{28,12},{1,17},{... | collective-permute-start | bytes 792584 | tf_op jit(solution)/shard_map/ppermute | solution.py:528
  68.2 8.1 %collective-permute-start.25 = (f16[1032,128]{1,0:T(8,128)(2,1)S(1)}, f16[1032,128]{1,0:T(8,128)(2,1)S(1)}, u32[]{:S(2)}, u32[]{:S(2)}) collective-permute-start(f16[1032,128]{1,0:T(8,128)(2,1)S(1)} %convert_element_type.123), channel_id=1, source_target_pairs={{0,8},{4,12},{8,0},{12,4},{16,24},{20,28},{24,16},{28,20},{1,9},{5... | collective-permute-start | bytes 792584 | tf_op jit(solution)/shard_map/ppermute | solution.py:528
  76.3 2.7 %collective-permute-start.27 = (bf16[256,512]{1,0:T(8,128)(2,1)S(1)}, bf16[256,512]{1,0:T(8,128)(2,1)S(1)}, u32[]{:S(2)}, u32[]{:S(2)}) collective-permute-start(bf16[256,512]{1,0:T(8,128)(2,1)S(1)} %get-tuple-element.126.refs_0_), channel_id=1, source_target_pairs={{0,4},{4,0},{8,12},{12,8},{16,20},{20,16},{24,28},{28,24},{1,5},{5... | collective-permute-start | bytes 786440 | tf_op jit(solution)/shard_map/ppermute | solution.py:528
  76.3 2.7 %collective-permute-start.28 = (bf16[256,512]{1,0:T(8,128)(2,1)S(1)}, bf16[256,512]{1,0:T(8,128)(2,1)S(1)}, u32[]{:S(2)}, u32[]{:S(2)}) collective-permute-start(bf16[256,512]{1,0:T(8,128)(2,1)S(1)} %get-tuple-element.127.refs_1_), channel_id=1, source_target_pairs={{0,4},{4,0},{8,12},{12,8},{16,20},{20,16},{24,28},{28,24},{1,5},{5... | collective-permute-start | bytes 786440 | tf_op jit(solution)/shard_map/ppermute | solution.py:528
  76.8 2.2 %collective-permute-start.30 = (bf16[256,512]{1,0:T(8,128)(2,1)S(1)}, bf16[256,512]{1,0:T(8,128)(2,1)S(1)}, u32[]{:S(2)}, u32[]{:S(2)}) collective-permute-start(bf16[256,512]{1,0:T(8,128)(2,1)S(1)} %get-tuple-element.129.refs_3_), channel_id=1, source_target_pairs={{0,4},{4,0},{8,12},{12,8},{16,20},{20,16},{24,28},{28,24},{1,5},{5... | collective-permute-start | bytes 786440 | tf_op jit(solution)/shard_map/ppermute | solution.py:528
  77.3 9.5 %collective-permute-start.34 = (f16[1032,128]{1,0:T(8,128)(2,1)S(1)}, f16[1032,128]{1,0:T(8,128)(2,1)S(1)}, u32[]{:S(2)}, u32[]{:S(2)}) collective-permute-start(f16[1032,128]{1,0:T(8,128)(2,1)S(1)} %convert_element_type.133), channel_id=1, source_target_pairs={{0,24},{4,28},{8,16},{12,20},{16,8},{20,12},{24,0},{28,4},{1,25},{... | collective-permute-start | bytes 792584 | tf_op jit(solution)/shard_map/ppermute | solution.py:528
  82.3 15.6 %collective-permute-start.32 = (f16[1032,128]{1,0:T(8,128)(2,1)S(1)}, f16[1032,128]{1,0:T(8,128)(2,1)S(1)}, u32[]{:S(2)}, u32[]{:S(2)}) collective-permute-start(f16[1032,128]{1,0:T(8,128)(2,1)S(1)} %convert_element_type.127), channel_id=1, source_target_pairs={{0,16},{4,20},{8,24},{12,28},{16,0},{20,4},{24,8},{28,12},{1,17},{... | collective-permute-start | bytes 792584 | tf_op jit(solution)/shard_map/ppermute | solution.py:528
  83.2 14.7 %collective-permute-start.33 = (f16[1032,128]{1,0:T(8,128)(2,1)S(1)}, f16[1032,128]{1,0:T(8,128)(2,1)S(1)}, u32[]{:S(2)}, u32[]{:S(2)}) collective-permute-start(f16[1032,128]{1,0:T(8,128)(2,1)S(1)} %convert_element_type.129), channel_id=1, source_target_pairs={{0,24},{4,28},{8,16},{12,20},{16,8},{20,12},{24,0},{28,4},{1,25},{... | collective-permute-start | bytes 792584 | tf_op jit(solution)/shard_map/ppermute | solution.py:528
  84.8 13.2 %collective-permute-start.31 = (f16[1032,128]{1,0:T(8,128)(2,1)S(1)}, f16[1032,128]{1,0:T(8,128)(2,1)S(1)}, u32[]{:S(2)}, u32[]{:S(2)}) collective-permute-start(f16[1032,128]{1,0:T(8,128)(2,1)S(1)} %convert_element_type.125), channel_id=1, source_target_pairs={{0,8},{4,12},{8,0},{12,4},{16,24},{20,28},{24,16},{28,20},{1,9},{5... | collective-permute-start | bytes 792584 | tf_op jit(solution)/shard_map/ppermute | solution.py:528
  (15 other events, 39.5 us)

commit v6 on v5

--- a/solution.py
+++ b/solution.py
@@ -551,7 +551,7 @@
     chips = lax.axis_size("vel") // 2
     member = lax.axis_index("vel").astype(jnp.int32)
     chip, core = lax.shift_right_logical(member, 1), member & 1
-    order = list(range(1, chips)) + [0]
+    order = [chips - 1] + list(range(1, chips - 1)) + [0]
     cells = plane // (chips * CHUNKS)
     width = chips * LANES
     rows = WIDE * cells + HEAD
@@ -605,8 +605,8 @@
         arrived = [full(e) for e in extra[k]]
         smoothed, own = transport(speeds, arrived, state[k], True, planes, cells, after)
         if k:
-            own, ahead = lax.optimization_barrier((own, back[k - 1][:2]))
-            back[k - 1] = [*ahead, *back[k - 1][2:]]
+            own, ahead = lax.optimization_barrier((own, back[k - 1][:1]))
+            back[k - 1] = [*ahead, *back[k - 1][1:]]
         other = [exchange(a, 1) for a in own]
         ready = []
         for part in range(chips // 2):

time: 101 us -> 100 us (0.990)
  waiting for transfers between devices: 28.3 us -> 25.6 us
  starting transfers between devices: 32 us -> 34.4 us
    ppermute x28, waiting for transfers between devices: 22 us -> 19.3 us  [exchange(): return lax.ppermute(array, 'vel', [(i, i ^ mask) for i in range(count)])]
    ppermute x28, starting transfers between devices: 20.2 us -> 21.7 us  [exchange(): return lax.ppermute(array, 'vel', [(i, i ^ mask) for i in range(count)])]
  transfers between devices with their start and end apart: 35 -> 35, of which waited for: 20 -> 18; matrix products, arithmetic and copies ran while one was open for 2% -> 2% of each run, Pallas kernels for 32% -> 32%
where the time goes in v6:
time: 100 us
  Pallas kernels  37.7 us (38%)
  starting transfers between devices  34.4 us (34%)
  waiting for transfers between devices  25.6 us (26%)
  other arithmetic  1.81 us (2%)
    ppermute x28, starting transfers between devices, exchange(): return lax.ppermute(array, 'vel', [(i, i ^ mask) for i in range(count)])  21.7 us
    ppermute x28, waiting for transfers between devices, exchange(): return lax.ppermute(array, 'vel', [(i, i ^ mask) for i in range(count)])  19.3 us
    ppermute x7, starting transfers between devices, shift(): lax.ppermute(array, 'space', [(i, (i + step) % count) for i in range(coun...  12.7 us
    pallas_call x4, Pallas kernels, transport(): pl.pallas_call(functools.partial(advect_kernel, cells, 16, before, count,...  11.2 us
    pallas_call x2, Pallas kernels, pack(): pl.pallas_call(functools.partial(pack_kernel, order, planes, cells), grid...  7.04 us
    pallas_call x4, Pallas kernels, final(): pl.pallas_call(functools.partial(final_kernel, part, len(own)), in_specs=...  6.53 us
    ppermute x7, waiting for transfers between devices, shift(): lax.ppermute(array, 'space', [(i, (i + step) % count) for i in range(coun...  6.25 us
    pallas_call x4, Pallas kernels, collide_half(): pl.pallas_call(functools.partial(half_kernel, len(own), first, sends), in...  5.65 us
  transfers between devices with their start and end apart: 35, of which 18 were waited for; matrix products, arithmetic and copies ran while one was open for 2% of the time, Pallas kernels for 32%

profile of v6, /device:TPU:0, one launch (start us, length us, event | category | flops | bytes accessed | tf_op | source)
XLA Modules:
  0.0 100.2 jit_solution(4860617803285029771)
XLA Ops:
  0.1 3.5 %pack.2 = (f32[1032,128]{1,0:T(8,128)S(1)}, f32[1032,128]{1,0:T(8,128)S(1)}, f32[1032,128]{1,0:T(8,128)S(1)}, f32[1032,128]{1,0:T(8,128)S(1)}) custom-call(s32[2]{0:T(128)S(1)} %pad_add_fusion.chip_ref.word_ref, f32[128,16,512]{2,1,0:T(8,128)} %d_ref.3, f32[128,16,512]{2,1,0:T(8,128)} %d_ref.3), custom_call_target="tpu_custom_call" | custom-call | flops 1000 | bytes 1000 | tf_op jit(solution)/shard_map/pack/pallas_call | solution.py:172
  3.6 3.0 %collective-permute-start.6 = (f16[1032,128]{1,0:T(8,128)(2,1)S(1)}, f16[1032,128]{1,0:T(8,128)(2,1)S(1)}, u32[]{:S(2)}, u32[]{:S(2)}) collective-permute-start(f16[1032,128]{1,0:T(8,128)(2,1)S(1)} %convert_element_type.112), channel_id=1, source_target_pairs={{0,16},{4,20},{8,24},{12,28},{16,0},{20,4},{24,8},{28,12},{1,17},{... | collective-permute-start | bytes 792584 | tf_op jit(solution)/shard_map/ppermute | solution.py:528
  8.4 4.1 %collective-permute-start.7 = (f16[520,128]{1,0:T(8,128)(2,1)S(1)}, f16[520,128]{1,0:T(8,128)(2,1)S(1)}, u32[]{:S(2)}, u32[]{:S(2)}) collective-permute-start(f16[520,128]{1,0:T(8,128)(2,1)S(1)} %slice_convert_fusion), channel_id=1, source_target_pairs={{0,3},{1,0},{2,1},{3,2},{4,7},{5,4},{6,5},{7,6},{8,11},{9,8},{10,9... | collective-permute-start | bytes 399368 | tf_op jit(solution)/shard_map/ppermute | solution.py:533
  13.0 3.6 %pack.3 = (f32[1032,128]{1,0:T(8,128)S(1)}, f32[1032,128]{1,0:T(8,128)S(1)}, f32[1032,128]{1,0:T(8,128)S(1)}, f32[1032,128]{1,0:T(8,128)S(1)}) custom-call(s32[2]{0:T(128)S(1)} %pad_add_fusion.chip_ref.word_ref, f32[128,16,512]{2,1,0:T(8,128)} %d_ref.3, f32[1032,128]{1,0:T(8,128)S(1)} %get-tuple-element.81.after_ref.refs_3_), custom_call_target="tpu_custom_call" | custom-call | flops 1000 | bytes 1000 | tf_op jit(solution)/shard_map/pack/pallas_call | solution.py:172
  16.7 1.6 %collective-permute-start.3 = (f16[1032,128]{1,0:T(8,128)(2,1)S(1)}, f16[1032,128]{1,0:T(8,128)(2,1)S(1)}, u32[]{:S(2)}, u32[]{:S(2)}) collective-permute-start(f16[1032,128]{1,0:T(8,128)(2,1)S(1)} %convert_element_type.106), channel_id=1, source_target_pairs={{0,16},{4,20},{8,24},{12,28},{16,0},{20,4},{24,8},{28,12},{1,17},{... | collective-permute-start | bytes 792584 | tf_op jit(solution)/shard_map/ppermute | solution.py:528
  22.1 3.5 %collective-permute-start.9 = (f16[520,256]{1,0:T(8,128)(2,1)S(1)}, f16[520,256]{1,0:T(8,128)(2,1)S(1)}, u32[]{:S(2)}, u32[]{:S(2)}) collective-permute-start(f16[520,256]{1,0:T(8,128)(2,1)S(1)} %slice.20), channel_id=1, source_target_pairs={{0,3},{1,0},{2,1},{3,2},{4,7},{5,4},{6,5},{7,6},{8,11},{9,8},{10,9... | collective-permute-start | bytes 798728 | tf_op jit(solution)/shard_map/ppermute | solution.py:533
  27.6 3.7 %collective-permute-done.1 = f16[1032,128]{1,0:T(8,128)(2,1)S(1)} collective-permute-done((f16[1032,128]{1,0:T(8,128)(2,1)S(1)}, f16[1032,128]{1,0:T(8,128)(2,1)S(1)}, u32[]{:S(2)}, u32[]{:S(2)}) %collective-permute-start.1) | collective-permute-done | bytes 264224 | tf_op jit(solution)/shard_map/ppermute | solution.py:528
  31.6 3.9 %collective-permute-start.8 = (f16[520,512]{1,0:T(8,128)(2,1)S(1)}, f16[520,512]{1,0:T(8,128)(2,1)S(1)}, u32[]{:S(2)}, u32[]{:S(2)}) collective-permute-start(f16[520,512]{1,0:T(8,128)(2,1)S(1)} %convert_element_type.114), channel_id=1, source_target_pairs={{0,3},{1,0},{2,1},{3,2},{4,7},{5,4},{6,5},{7,6},{8,11},{9,8},{10,9... | collective-permute-start | bytes 1597448 | tf_op jit(solution)/shard_map/ppermute | solution.py:533
  35.9 2.7 %transport.4 = (f32[1024,512]{1,0:T(8,128)S(1)}, bf16[256,512]{1,0:T(8,128)(2,1)S(1)}, bf16[256,512]{1,0:T(8,128)(2,1)S(1)}, bf16[256,512]{1,0:T(8,128)(2,1)S(1)}, bf16[256,512]{1,0:T(8,128)(2,1)S(1)}) custom-call(f32[8,512]{1,0:T(8,128)S(1)} %get-tuple-element.74.c_ref, f32[520,256]{1,0:T(8,128)S(1)} %convert_element_type.115.refs_0_, ...), custom_call_target="tpu_custom_call" | custom-call | flops 1000 | bytes 1000 | tf_op jit(solution)/shard_map/transport/pallas_call | solution.py:350
  45.5 2.5 %collective-permute-done.8 = f16[520,512]{1,0:T(8,128)(2,1)S(1)} collective-permute-done((f16[520,512]{1,0:T(8,128)(2,1)S(1)}, f16[520,512]{1,0:T(8,128)(2,1)S(1)}, u32[]{:S(2)}, u32[]{:S(2)}) %collective-permute-start.8) | collective-permute-done | bytes 532512 | tf_op jit(solution)/shard_map/ppermute | solution.py:533
  48.2 2.8 %transport.5 = (f32[1024,512]{1,0:T(8,128)S(1)}, bf16[256,512]{1,0:T(8,128)(2,1)S(1)}, bf16[256,512]{1,0:T(8,128)(2,1)S(1)}, bf16[256,512]{1,0:T(8,128)(2,1)S(1)}, bf16[256,512]{1,0:T(8,128)(2,1)S(1)}) custom-call(f32[8,512]{1,0:T(8,128)S(1)} %get-tuple-element.74.c_ref, f32[520,512]{1,0:T(8,128)S(1)} %convert_element_type.118.refs_0_, ...), custom_call_target="tpu_custom_call" | custom-call | flops 1000 | bytes 1000 | tf_op jit(solution)/shard_map/transport/pallas_call | solution.py:350
  56.2 2.6 %collective-permute-done.18 = f16[520,512]{1,0:T(8,128)(2,1)S(1)} collective-permute-done((f16[520,512]{1,0:T(8,128)(2,1)S(1)}, f16[520,512]{1,0:T(8,128)(2,1)S(1)}, u32[]{:S(2)}, u32[]{:S(2)}) %collective-permute-start.18) | collective-permute-done | bytes 532512 | tf_op jit(solution)/shard_map/ppermute | solution.py:533
  58.9 2.9 %transport.6 = (f32[1024,512]{1,0:T(8,128)S(1)}, bf16[256,512]{1,0:T(8,128)(2,1)S(1)}, bf16[256,512]{1,0:T(8,128)(2,1)S(1)}, bf16[256,512]{1,0:T(8,128)(2,1)S(1)}, bf16[256,512]{1,0:T(8,128)(2,1)S(1)}) custom-call(f32[8,512]{1,0:T(8,128)S(1)} %get-tuple-element.74.c_ref, f32[520,512]{1,0:T(8,128)S(1)} %convert_element_type.121.refs_0_, ...), custom_call_target="tpu_custom_call" | custom-call | flops 1000 | bytes 1000 | tf_op jit(solution)/shard_map/transport/pallas_call | solution.py:350
  64.6 1.6 %final.4 = (f32[1032,128]{1,0:T(8,128)S(1)}, f32[1032,128]{1,0:T(8,128)S(1)}) custom-call(bf16[256,512]{1,0:T(8,128)(2,1)S(1)} %get-tuple-element.109.refs_0_, bf16[256,512]{1,0:T(8,128)(2,1)S(1)} %get-tuple-element.110.refs_1_, bf16[256,512]{1,0:T(8,128)(2,1)S(1)} %get-tuple-element.111.refs_2_, bf16[256,512]{1,0:T(8,128)(2,1)S(1)} %get-tuple-element.112.refs_3_, ...), custom_call_target="tpu_custom_call" | custom-call | flops 1000 | bytes 1000 | tf_op jit(solution)/shard_map/final/pallas_call | solution.py:462
  66.2 2.5 %collective-permute-start.25 = (f16[1032,128]{1,0:T(8,128)(2,1)S(1)}, f16[1032,128]{1,0:T(8,128)(2,1)S(1)}, u32[]{:S(2)}, u32[]{:S(2)}) collective-permute-start(f16[1032,128]{1,0:T(8,128)(2,1)S(1)} %convert_element_type.123), channel_id=1, source_target_pairs={{0,24},{4,28},{8,16},{12,20},{16,8},{20,12},{24,0},{28,4},{1,25},{... | collective-permute-start | bytes 792584 | tf_op jit(solution)/shard_map/ppermute | solution.py:528
  68.8 1.6 %final.5 = (f32[1032,128]{1,0:T(8,128)S(1)}, f32[1032,128]{1,0:T(8,128)S(1)}) custom-call(bf16[256,512]{1,0:T(8,128)(2,1)S(1)} %get-tuple-element.109.refs_0_, bf16[256,512]{1,0:T(8,128)(2,1)S(1)} %get-tuple-element.110.refs_1_, bf16[256,512]{1,0:T(8,128)(2,1)S(1)} %get-tuple-element.111.refs_2_, bf16[256,512]{1,0:T(8,128)(2,1)S(1)} %get-tuple-element.112.refs_3_, ...), custom_call_target="tpu_custom_call" | custom-call | flops 1000 | bytes 1000 | tf_op jit(solution)/shard_map/final/pallas_call | solution.py:462
  71.6 2.9 %transport.7 = (f32[1024,512]{1,0:T(8,128)S(1)}, bf16[256,512]{1,0:T(8,128)(2,1)S(1)}, bf16[256,512]{1,0:T(8,128)(2,1)S(1)}, bf16[256,512]{1,0:T(8,128)(2,1)S(1)}, bf16[256,512]{1,0:T(8,128)(2,1)S(1)}) custom-call(f32[8,512]{1,0:T(8,128)S(1)} %get-tuple-element.74.c_ref, f32[520,512]{1,0:T(8,128)S(1)} %convert_element_type.122.refs_0_, ...), custom_call_target="tpu_custom_call" | custom-call | flops 1000 | bytes 1000 | tf_op jit(solution)/shard_map/transport/pallas_call | solution.py:350
  79.8 1.6 %final.6 = (f32[1032,128]{1,0:T(8,128)S(1)}, f32[1032,128]{1,0:T(8,128)S(1)}) custom-call(bf16[256,512]{1,0:T(8,128)(2,1)S(1)} %get-tuple-element.125.refs_0_, bf16[256,512]{1,0:T(8,128)(2,1)S(1)} %get-tuple-element.126.refs_1_, bf16[256,512]{1,0:T(8,128)(2,1)S(1)} %get-tuple-element.127.refs_2_, bf16[256,512]{1,0:T(8,128)(2,1)S(1)} %get-tuple-element.128.refs_3_, ...), custom_call_target="tpu_custom_call" | custom-call | flops 1000 | bytes 1000 | tf_op jit(solution)/shard_map/final/pallas_call | solution.py:462
  81.4 1.6 %final.7 = (f32[1032,128]{1,0:T(8,128)S(1)}, f32[1032,128]{1,0:T(8,128)S(1)}) custom-call(bf16[256,512]{1,0:T(8,128)(2,1)S(1)} %get-tuple-element.125.refs_0_, bf16[256,512]{1,0:T(8,128)(2,1)S(1)} %get-tuple-element.126.refs_1_, bf16[256,512]{1,0:T(8,128)(2,1)S(1)} %get-tuple-element.127.refs_2_, bf16[256,512]{1,0:T(8,128)(2,1)S(1)} %get-tuple-element.128.refs_3_, ...), custom_call_target="tpu_custom_call" | custom-call | flops 1000 | bytes 1000 | tf_op jit(solution)/shard_map/final/pallas_call | solution.py:462
  84.7 2.1 %collective-permute-start.30 = (f16[1032,128]{1,0:T(8,128)(2,1)S(1)}, f16[1032,128]{1,0:T(8,128)(2,1)S(1)}, u32[]{:S(2)}, u32[]{:S(2)}) collective-permute-start(f16[1032,128]{1,0:T(8,128)(2,1)S(1)} %convert_element_type.124), channel_id=1, source_target_pairs={{0,24},{4,28},{8,16},{12,20},{16,8},{20,12},{24,0},{28,4},{1,25},{... | collective-permute-start | bytes 792584 | tf_op jit(solution)/shard_map/ppermute | solution.py:528
  87.0 2.5 %unpack.2.refs_5_ = f32[128,16,512]{2,1,0:T(8,128)} custom-call(s32[2]{0:T(128)S(1)} %pad_add_fusion.chip_ref.word_ref, f32[1032,128]{1,0:T(8,128)S(1)} %convert_element_type.130.refs_0_, f32[1032,128]{1,0:T(8,128)S(1)} %convert_element_type.132.refs_1_, f32[1032,128]{1,0:T(8,128)S(1)} %convert_element_type.134.refs_2_, ...), custom_call_target="tpu_custom_call" | custom-call | flops 1000 | bytes 1000 | tf_op jit(solution)/shard_map/unpack/pallas_call | solution.py:509
  89.5 3.0 %collective-permute-done.31 = f16[1032,128]{1,0:T(8,128)(2,1)S(1)} collective-permute-done((f16[1032,128]{1,0:T(8,128)(2,1)S(1)}, f16[1032,128]{1,0:T(8,128)(2,1)S(1)}, u32[]{:S(2)}, u32[]{:S(2)}) %collective-permute-start.31) | collective-permute-done | bytes 264224 | tf_op jit(solution)/shard_map/ppermute | solution.py:528
  92.6 5.0 %collective-permute-done.32 = f16[1032,128]{1,0:T(8,128)(2,1)S(1)} collective-permute-done((f16[1032,128]{1,0:T(8,128)(2,1)S(1)}, f16[1032,128]{1,0:T(8,128)(2,1)S(1)}, u32[]{:S(2)}, u32[]{:S(2)}) %collective-permute-start.32) | collective-permute-done | bytes 264224 | tf_op jit(solution)/shard_map/ppermute | solution.py:528
  97.7 2.5 %unpack.3 = f32[128,16,512]{2,1,0:T(8,128)} custom-call(s32[2]{0:T(128)S(1)} %pad_add_fusion.chip_ref.word_ref, f32[1032,128]{1,0:T(8,128)S(1)} %convert_element_type.125.refs_0_, f32[1032,128]{1,0:T(8,128)S(1)} %convert_element_type.127.refs_1_, f32[1032,128]{1,0:T(8,128)S(1)} %convert_element_type.129.refs_2_, ...), custom_call_target="tpu_custom_call", output_to_operand_aliasing={{}: (6, {})} | custom-call | flops 1000 | bytes 1000 | tf_op jit(solution)/shard_map/unpack/pallas_call | solution.py:509
  (114 shorter events, 32.3 us)
Async XLA Ops:
  3.6 16.2 %collective-permute-start.6 = (f16[1032,128]{1,0:T(8,128)(2,1)S(1)}, f16[1032,128]{1,0:T(8,128)(2,1)S(1)}, u32[]{:S(2)}, u32[]{:S(2)}) collective-permute-start(f16[1032,128]{1,0:T(8,128)(2,1)S(1)} %convert_element_type.112), channel_id=1, source_target_pairs={{0,16},{4,20},{8,24},{12,28},{16,0},{20,4},{24,8},{28,12},{1,17},{... | collective-permute-start | bytes 792584 | tf_op jit(solution)/shard_map/ppermute | solution.py:528
  6.7 15.1 %collective-permute-start.5 = (f16[1032,128]{1,0:T(8,128)(2,1)S(1)}, f16[1032,128]{1,0:T(8,128)(2,1)S(1)}, u32[]{:S(2)}, u32[]{:S(2)}) collective-permute-start(f16[1032,128]{1,0:T(8,128)(2,1)S(1)} %convert_element_type.110), channel_id=1, source_target_pairs={{0,8},{4,12},{8,0},{12,4},{16,24},{20,28},{24,16},{28,20},{1,9},{5... | collective-permute-start | bytes 792584 | tf_op jit(solution)/shard_map/ppermute | solution.py:528
  8.3 13.6 %collective-permute-start.4 = (f16[1032,128]{1,0:T(8,128)(2,1)S(1)}, f16[1032,128]{1,0:T(8,128)(2,1)S(1)}, u32[]{:S(2)}, u32[]{:S(2)}) collective-permute-start(f16[1032,128]{1,0:T(8,128)(2,1)S(1)} %convert_element_type.108), channel_id=1, source_target_pairs={{0,24},{4,28},{8,16},{12,20},{16,8},{20,12},{24,0},{28,4},{1,25},{... | collective-permute-start | bytes 792584 | tf_op jit(solution)/shard_map/ppermute | solution.py:528
  8.4 9.9 %collective-permute-start.7 = (f16[520,128]{1,0:T(8,128)(2,1)S(1)}, f16[520,128]{1,0:T(8,128)(2,1)S(1)}, u32[]{:S(2)}, u32[]{:S(2)}) collective-permute-start(f16[520,128]{1,0:T(8,128)(2,1)S(1)} %slice_convert_fusion), channel_id=1, source_target_pairs={{0,3},{1,0},{2,1},{3,2},{4,7},{5,4},{6,5},{7,6},{8,11},{9,8},{10,9... | collective-permute-start | bytes 399368 | tf_op jit(solution)/shard_map/ppermute | solution.py:533
  12.5 4.2 %collective-permute-start = (f32[8,512]{1,0:T(8,128)S(1)}, f32[8,512]{1,0:T(8,128)S(1)}, u32[]{:S(2)}, u32[]{:S(2)}) collective-permute-start(f32[8,512]{1,0:T(8,128)S(1)} %slice.15), channel_id=1, source_target_pairs={{0,3},{1,0},{2,1},{3,2},{4,7},{5,4},{6,5},{7,6},{8,11},{9,8},{10,9... | collective-permute-start | bytes 49160 | tf_op jit(solution)/shard_map/ppermute | solution.py:533
  16.7 10.8 %collective-permute-start.3 = (f16[1032,128]{1,0:T(8,128)(2,1)S(1)}, f16[1032,128]{1,0:T(8,128)(2,1)S(1)}, u32[]{:S(2)}, u32[]{:S(2)}) collective-permute-start(f16[1032,128]{1,0:T(8,128)(2,1)S(1)} %convert_element_type.106), channel_id=1, source_target_pairs={{0,16},{4,20},{8,24},{12,28},{16,0},{20,4},{24,8},{28,12},{1,17},{... | collective-permute-start | bytes 792584 | tf_op jit(solution)/shard_map/ppermute | solution.py:528
  18.3 9.3 %collective-permute-start.2 = (f16[1032,128]{1,0:T(8,128)(2,1)S(1)}, f16[1032,128]{1,0:T(8,128)(2,1)S(1)}, u32[]{:S(2)}, u32[]{:S(2)}) collective-permute-start(f16[1032,128]{1,0:T(8,128)(2,1)S(1)} %convert_element_type.104), channel_id=1, source_target_pairs={{0,8},{4,12},{8,0},{12,4},{16,24},{20,28},{24,16},{28,20},{1,9},{5... | collective-permute-start | bytes 792584 | tf_op jit(solution)/shard_map/ppermute | solution.py:528
  19.8 11.5 %collective-permute-start.1 = (f16[1032,128]{1,0:T(8,128)(2,1)S(1)}, f16[1032,128]{1,0:T(8,128)(2,1)S(1)}, u32[]{:S(2)}, u32[]{:S(2)}) collective-permute-start(f16[1032,128]{1,0:T(8,128)(2,1)S(1)} %convert_element_type.102), channel_id=1, source_target_pairs={{0,24},{4,28},{8,16},{12,20},{16,8},{20,12},{24,0},{28,4},{1,25},{... | collective-permute-start | bytes 792584 | tf_op jit(solution)/shard_map/ppermute | solution.py:528
  22.1 13.7 %collective-permute-start.9 = (f16[520,256]{1,0:T(8,128)(2,1)S(1)}, f16[520,256]{1,0:T(8,128)(2,1)S(1)}, u32[]{:S(2)}, u32[]{:S(2)}) collective-permute-start(f16[520,256]{1,0:T(8,128)(2,1)S(1)} %slice.20), channel_id=1, source_target_pairs={{0,3},{1,0},{2,1},{3,2},{4,7},{5,4},{6,5},{7,6},{8,11},{9,8},{10,9... | collective-permute-start | bytes 798728 | tf_op jit(solution)/shard_map/ppermute | solution.py:533
  25.6 10.2 %collective-permute-start.10 = (f16[520,128]{1,0:T(8,128)(2,1)S(1)}, f16[520,128]{1,0:T(8,128)(2,1)S(1)}, u32[]{:S(2)}, u32[]{:S(2)}) collective-permute-start(f16[520,128]{1,0:T(8,128)(2,1)S(1)} %slice.21), channel_id=1, source_target_pairs={{0,3},{1,0},{2,1},{3,2},{4,7},{5,4},{6,5},{7,6},{8,11},{9,8},{10,9... | collective-permute-start | bytes 399368 | tf_op jit(solution)/shard_map/ppermute | solution.py:533
  31.6 16.5 %collective-permute-start.8 = (f16[520,512]{1,0:T(8,128)(2,1)S(1)}, f16[520,512]{1,0:T(8,128)(2,1)S(1)}, u32[]{:S(2)}, u32[]{:S(2)}) collective-permute-start(f16[520,512]{1,0:T(8,128)(2,1)S(1)} %convert_element_type.114), channel_id=1, source_target_pairs={{0,3},{1,0},{2,1},{3,2},{4,7},{5,4},{6,5},{7,6},{8,11},{9,8},{10,9... | collective-permute-start | bytes 1597448 | tf_op jit(solution)/shard_map/ppermute | solution.py:533
  42.2 16.7 %collective-permute-start.18 = (f16[520,512]{1,0:T(8,128)(2,1)S(1)}, f16[520,512]{1,0:T(8,128)(2,1)S(1)}, u32[]{:S(2)}, u32[]{:S(2)}) collective-permute-start(f16[520,512]{1,0:T(8,128)(2,1)S(1)} %convert_element_type.120), channel_id=1, source_target_pairs={{0,1},{1,2},{2,3},{3,0},{4,5},{5,6},{6,7},{7,4},{8,9},{9,10},{10,1... | collective-permute-start | bytes 1597448 | tf_op jit(solution)/shard_map/ppermute | solution.py:533
  51.6 3.3 %collective-permute-start.19 = (bf16[256,512]{1,0:T(8,128)(2,1)S(1)}, bf16[256,512]{1,0:T(8,128)(2,1)S(1)}, u32[]{:S(2)}, u32[]{:S(2)}) collective-permute-start(bf16[256,512]{1,0:T(8,128)(2,1)S(1)} %get-tuple-element.104.refs_0_), channel_id=1, source_target_pairs={{0,4},{4,0},{8,12},{12,8},{16,20},{20,16},{24,28},{28,24},{1,5},{5... | collective-permute-start | bytes 786440 | tf_op jit(solution)/shard_map/ppermute | solution.py:528
  51.6 3.2 %collective-permute-start.20 = (bf16[256,512]{1,0:T(8,128)(2,1)S(1)}, bf16[256,512]{1,0:T(8,128)(2,1)S(1)}, u32[]{:S(2)}, u32[]{:S(2)}) collective-permute-start(bf16[256,512]{1,0:T(8,128)(2,1)S(1)} %get-tuple-element.105.refs_1_), channel_id=1, source_target_pairs={{0,4},{4,0},{8,12},{12,8},{16,20},{20,16},{24,28},{28,24},{1,5},{5... | collective-permute-start | bytes 786440 | tf_op jit(solution)/shard_map/ppermute | solution.py:528
  54.6 16.9 %collective-permute-start.17 = (f16[520,512]{1,0:T(8,128)(2,1)S(1)}, f16[520,512]{1,0:T(8,128)(2,1)S(1)}, u32[]{:S(2)}, u32[]{:S(2)}) collective-permute-start(f16[520,512]{1,0:T(8,128)(2,1)S(1)} %convert_element_type.119), channel_id=1, source_target_pairs={{0,1},{1,2},{2,3},{3,0},{4,5},{5,6},{6,7},{7,4},{8,9},{9,10},{10,1... | collective-permute-start | bytes 1597448 | tf_op jit(solution)/shard_map/ppermute | solution.py:533
  66.2 9.4 %collective-permute-start.25 = (f16[1032,128]{1,0:T(8,128)(2,1)S(1)}, f16[1032,128]{1,0:T(8,128)(2,1)S(1)}, u32[]{:S(2)}, u32[]{:S(2)}) collective-permute-start(f16[1032,128]{1,0:T(8,128)(2,1)S(1)} %convert_element_type.123), channel_id=1, source_target_pairs={{0,24},{4,28},{8,16},{12,20},{16,8},{20,12},{24,0},{28,4},{1,25},{... | collective-permute-start | bytes 792584 | tf_op jit(solution)/shard_map/ppermute | solution.py:528
  75.6 4.2 %collective-permute-start.27 = (bf16[256,512]{1,0:T(8,128)(2,1)S(1)}, bf16[256,512]{1,0:T(8,128)(2,1)S(1)}, u32[]{:S(2)}, u32[]{:S(2)}) collective-permute-start(bf16[256,512]{1,0:T(8,128)(2,1)S(1)} %get-tuple-element.126.refs_1_), channel_id=1, source_target_pairs={{0,4},{4,0},{8,12},{12,8},{16,20},{20,16},{24,28},{28,24},{1,5},{5... | collective-permute-start | bytes 786440 | tf_op jit(solution)/shard_map/ppermute | solution.py:528
  76.1 3.7 %collective-permute-start.28 = (bf16[256,512]{1,0:T(8,128)(2,1)S(1)}, bf16[256,512]{1,0:T(8,128)(2,1)S(1)}, u32[]{:S(2)}, u32[]{:S(2)}) collective-permute-start(bf16[256,512]{1,0:T(8,128)(2,1)S(1)} %get-tuple-element.127.refs_2_), channel_id=1, source_target_pairs={{0,4},{4,0},{8,12},{12,8},{16,20},{20,16},{24,28},{28,24},{1,5},{5... | collective-permute-start | bytes 786440 | tf_op jit(solution)/shard_map/ppermute | solution.py:528
  76.1 3.7 %collective-permute-start.29 = (bf16[256,512]{1,0:T(8,128)(2,1)S(1)}, bf16[256,512]{1,0:T(8,128)(2,1)S(1)}, u32[]{:S(2)}, u32[]{:S(2)}) collective-permute-start(bf16[256,512]{1,0:T(8,128)(2,1)S(1)} %get-tuple-element.128.refs_3_), channel_id=1, source_target_pairs={{0,4},{4,0},{8,12},{12,8},{16,20},{20,16},{24,28},{28,24},{1,5},{5... | collective-permute-start | bytes 786440 | tf_op jit(solution)/shard_map/ppermute | solution.py:528
  76.7 10.2 %collective-permute-start.33 = (f16[1032,128]{1,0:T(8,128)(2,1)S(1)}, f16[1032,128]{1,0:T(8,128)(2,1)S(1)}, u32[]{:S(2)}, u32[]{:S(2)}) collective-permute-start(f16[1032,128]{1,0:T(8,128)(2,1)S(1)} %convert_element_type.131), channel_id=1, source_target_pairs={{0,8},{4,12},{8,0},{12,4},{16,24},{20,28},{24,16},{28,20},{1,9},{5... | collective-permute-start | bytes 792584 | tf_op jit(solution)/shard_map/ppermute | solution.py:528
  78.3 8.6 %collective-permute-start.34 = (f16[1032,128]{1,0:T(8,128)(2,1)S(1)}, f16[1032,128]{1,0:T(8,128)(2,1)S(1)}, u32[]{:S(2)}, u32[]{:S(2)}) collective-permute-start(f16[1032,128]{1,0:T(8,128)(2,1)S(1)} %convert_element_type.133), channel_id=1, source_target_pairs={{0,16},{4,20},{8,24},{12,28},{16,0},{20,4},{24,8},{28,12},{1,17},{... | collective-permute-start | bytes 792584 | tf_op jit(solution)/shard_map/ppermute | solution.py:528
  83.2 9.4 %collective-permute-start.31 = (f16[1032,128]{1,0:T(8,128)(2,1)S(1)}, f16[1032,128]{1,0:T(8,128)(2,1)S(1)}, u32[]{:S(2)}, u32[]{:S(2)}) collective-permute-start(f16[1032,128]{1,0:T(8,128)(2,1)S(1)} %convert_element_type.126), channel_id=1, source_target_pairs={{0,8},{4,12},{8,0},{12,4},{16,24},{20,28},{24,16},{28,20},{1,9},{5... | collective-permute-start | bytes 792584 | tf_op jit(solution)/shard_map/ppermute | solution.py:528
  83.8 13.8 %collective-permute-start.32 = (f16[1032,128]{1,0:T(8,128)(2,1)S(1)}, f16[1032,128]{1,0:T(8,128)(2,1)S(1)}, u32[]{:S(2)}, u32[]{:S(2)}) collective-permute-start(f16[1032,128]{1,0:T(8,128)(2,1)S(1)} %convert_element_type.128), channel_id=1, source_target_pairs={{0,16},{4,20},{8,24},{12,28},{16,0},{20,4},{24,8},{28,12},{1,17},{... | collective-permute-start | bytes 792584 | tf_op jit(solution)/shard_map/ppermute | solution.py:528
  84.7 12.9 %collective-permute-start.30 = (f16[1032,128]{1,0:T(8,128)(2,1)S(1)}, f16[1032,128]{1,0:T(8,128)(2,1)S(1)}, u32[]{:S(2)}, u32[]{:S(2)}) collective-permute-start(f16[1032,128]{1,0:T(8,128)(2,1)S(1)} %convert_element_type.124), channel_id=1, source_target_pairs={{0,24},{4,28},{8,16},{12,20},{16,8},{20,12},{24,0},{28,4},{1,25},{... | collective-permute-start | bytes 792584 | tf_op jit(solution)/shard_map/ppermute | solution.py:528
  (15 other events, 40.0 us)

commit v7 on v6

--- a/solution.py
+++ b/solution.py
@@ -348,7 +348,7 @@
     count = QUARTERS
     rows, width = planes * cells, speeds.shape[1]
     results = pl.pallas_call(
-        functools.partial(advect_kernel, cells, 16, before, count, len(extras)),
+        functools.partial(advect_kernel, cells, 32 if cells % 32 == 0 else 16, before, count, len(extras)),
         in_specs=[resident()] * (1 + len(extras) + len(bodies)) + [anywhere()],
         out_specs=[resident()] * (1 + count),
         out_shape=[jax.ShapeDtypeStruct((rows, width), jnp.float32)]

time: 100 us -> 100 us (level)
  transfers between devices with their start and end apart: 35 -> 35, of which waited for: 18 -> 18; matrix products, arithmetic and copies ran while one was open for 2% -> 2% of each run, Pallas kernels for 32% -> 31%
where the time goes in v7:
time: 100 us
  Pallas kernels  37.3 us (37%)
  starting transfers between devices  34.5 us (34%)
  waiting for transfers between devices  25.8 us (26%)
  other arithmetic  1.81 us (2%)
    ppermute x28, starting transfers between devices, exchange(): return lax.ppermute(array, 'vel', [(i, i ^ mask) for i in range(count)])  21.8 us
    ppermute x28, waiting for transfers between devices, exchange(): return lax.ppermute(array, 'vel', [(i, i ^ mask) for i in range(count)])  19.4 us
    ppermute x7, starting transfers between devices, shift(): lax.ppermute(array, 'space', [(i, (i + step) % count) for i in range(coun...  12.7 us
    pallas_call x4, Pallas kernels, transport(): pl.pallas_call(functools.partial(advect_kernel, cells, 32 if cells % 32 =...  10.8 us
    pallas_call x2, Pallas kernels, pack(): pl.pallas_call(functools.partial(pack_kernel, order, planes, cells), grid...  7.04 us
    pallas_call x4, Pallas kernels, final(): pl.pallas_call(functools.partial(final_kernel, part, len(own)), in_specs=...  6.54 us
    ppermute x7, waiting for transfers between devices, shift(): lax.ppermute(array, 'space', [(i, (i + step) % count) for i in range(coun...  6.42 us
    pallas_call x4, Pallas kernels, collide_half(): pl.pallas_call(functools.partial(half_kernel, len(own), first, sends), in...  5.65 us
  transfers between devices with their start and end apart: 35, of which 18 were waited for; matrix products, arithmetic and copies ran while one was open for 2% of the time, Pallas kernels for 31%

profile of v7, /device:TPU:0, one launch (start us, length us, event | category | flops | bytes accessed | tf_op | source)
XLA Modules:
  0.0 100.1 jit_solution(3389245822181986339)
XLA Ops:
  0.1 3.5 %pack.2 = (f32[1032,128]{1,0:T(8,128)S(1)}, f32[1032,128]{1,0:T(8,128)S(1)}, f32[1032,128]{1,0:T(8,128)S(1)}, f32[1032,128]{1,0:T(8,128)S(1)}) custom-call(s32[2]{0:T(128)S(1)} %pad_add_fusion.chip_ref.word_ref, f32[128,16,512]{2,1,0:T(8,128)} %d_ref.3, f32[128,16,512]{2,1,0:T(8,128)} %d_ref.3), custom_call_target="tpu_custom_call" | custom-call | flops 1000 | bytes 1000 | tf_op jit(solution)/shard_map/pack/pallas_call | solution.py:172
  3.6 3.0 %collective-permute-start.6 = (f16[1032,128]{1,0:T(8,128)(2,1)S(1)}, f16[1032,128]{1,0:T(8,128)(2,1)S(1)}, u32[]{:S(2)}, u32[]{:S(2)}) collective-permute-start(f16[1032,128]{1,0:T(8,128)(2,1)S(1)} %convert_element_type.112), channel_id=1, source_target_pairs={{0,16},{4,20},{8,24},{12,28},{16,0},{20,4},{24,8},{28,12},{1,17},{... | collective-permute-start | bytes 792584 | tf_op jit(solution)/shard_map/ppermute | solution.py:528
  8.4 4.1 %collective-permute-start.7 = (f16[520,128]{1,0:T(8,128)(2,1)S(1)}, f16[520,128]{1,0:T(8,128)(2,1)S(1)}, u32[]{:S(2)}, u32[]{:S(2)}) collective-permute-start(f16[520,128]{1,0:T(8,128)(2,1)S(1)} %slice_convert_fusion), channel_id=1, source_target_pairs={{0,3},{1,0},{2,1},{3,2},{4,7},{5,4},{6,5},{7,6},{8,11},{9,8},{10,9... | collective-permute-start | bytes 399368 | tf_op jit(solution)/shard_map/ppermute | solution.py:533
  13.0 3.6 %pack.3 = (f32[1032,128]{1,0:T(8,128)S(1)}, f32[1032,128]{1,0:T(8,128)S(1)}, f32[1032,128]{1,0:T(8,128)S(1)}, f32[1032,128]{1,0:T(8,128)S(1)}) custom-call(s32[2]{0:T(128)S(1)} %pad_add_fusion.chip_ref.word_ref, f32[128,16,512]{2,1,0:T(8,128)} %d_ref.3, f32[1032,128]{1,0:T(8,128)S(1)} %get-tuple-element.81.after_ref.refs_3_), custom_call_target="tpu_custom_call" | custom-call | flops 1000 | bytes 1000 | tf_op jit(solution)/shard_map/pack/pallas_call | solution.py:172
  16.7 1.6 %collective-permute-start.3 = (f16[1032,128]{1,0:T(8,128)(2,1)S(1)}, f16[1032,128]{1,0:T(8,128)(2,1)S(1)}, u32[]{:S(2)}, u32[]{:S(2)}) collective-permute-start(f16[1032,128]{1,0:T(8,128)(2,1)S(1)} %convert_element_type.106), channel_id=1, source_target_pairs={{0,16},{4,20},{8,24},{12,28},{16,0},{20,4},{24,8},{28,12},{1,17},{... | collective-permute-start | bytes 792584 | tf_op jit(solution)/shard_map/ppermute | solution.py:528
  22.1 3.5 %collective-permute-start.9 = (f16[520,256]{1,0:T(8,128)(2,1)S(1)}, f16[520,256]{1,0:T(8,128)(2,1)S(1)}, u32[]{:S(2)}, u32[]{:S(2)}) collective-permute-start(f16[520,256]{1,0:T(8,128)(2,1)S(1)} %slice.20), channel_id=1, source_target_pairs={{0,3},{1,0},{2,1},{3,2},{4,7},{5,4},{6,5},{7,6},{8,11},{9,8},{10,9... | collective-permute-start | bytes 798728 | tf_op jit(solution)/shard_map/ppermute | solution.py:533
  27.6 3.7 %collective-permute-done.1 = f16[1032,128]{1,0:T(8,128)(2,1)S(1)} collective-permute-done((f16[1032,128]{1,0:T(8,128)(2,1)S(1)}, f16[1032,128]{1,0:T(8,128)(2,1)S(1)}, u32[]{:S(2)}, u32[]{:S(2)}) %collective-permute-start.1) | collective-permute-done | bytes 264224 | tf_op jit(solution)/shard_map/ppermute | solution.py:528
  31.6 3.9 %collective-permute-start.8 = (f16[520,512]{1,0:T(8,128)(2,1)S(1)}, f16[520,512]{1,0:T(8,128)(2,1)S(1)}, u32[]{:S(2)}, u32[]{:S(2)}) collective-permute-start(f16[520,512]{1,0:T(8,128)(2,1)S(1)} %convert_element_type.114), channel_id=1, source_target_pairs={{0,3},{1,0},{2,1},{3,2},{4,7},{5,4},{6,5},{7,6},{8,11},{9,8},{10,9... | collective-permute-start | bytes 1597448 | tf_op jit(solution)/shard_map/ppermute | solution.py:533
  35.9 2.6 %transport.4 = (f32[1024,512]{1,0:T(8,128)S(1)}, bf16[256,512]{1,0:T(8,128)(2,1)S(1)}, bf16[256,512]{1,0:T(8,128)(2,1)S(1)}, bf16[256,512]{1,0:T(8,128)(2,1)S(1)}, bf16[256,512]{1,0:T(8,128)(2,1)S(1)}) custom-call(f32[8,512]{1,0:T(8,128)S(1)} %get-tuple-element.74.c_ref, f32[520,256]{1,0:T(8,128)S(1)} %convert_element_type.115.refs_0_, ...), custom_call_target="tpu_custom_call" | custom-call | flops 1000 | bytes 1000 | tf_op jit(solution)/shard_map/transport/pallas_call | solution.py:350
  45.5 2.6 %collective-permute-done.8 = f16[520,512]{1,0:T(8,128)(2,1)S(1)} collective-permute-done((f16[520,512]{1,0:T(8,128)(2,1)S(1)}, f16[520,512]{1,0:T(8,128)(2,1)S(1)}, u32[]{:S(2)}, u32[]{:S(2)}) %collective-permute-start.8) | collective-permute-done | bytes 532512 | tf_op jit(solution)/shard_map/ppermute | solution.py:533
  48.2 2.7 %transport.5 = (f32[1024,512]{1,0:T(8,128)S(1)}, bf16[256,512]{1,0:T(8,128)(2,1)S(1)}, bf16[256,512]{1,0:T(8,128)(2,1)S(1)}, bf16[256,512]{1,0:T(8,128)(2,1)S(1)}, bf16[256,512]{1,0:T(8,128)(2,1)S(1)}) custom-call(f32[8,512]{1,0:T(8,128)S(1)} %get-tuple-element.74.c_ref, f32[520,512]{1,0:T(8,128)S(1)} %convert_element_type.118.refs_0_, ...), custom_call_target="tpu_custom_call" | custom-call | flops 1000 | bytes 1000 | tf_op jit(solution)/shard_map/transport/pallas_call | solution.py:350
  56.1 2.8 %collective-permute-done.18 = f16[520,512]{1,0:T(8,128)(2,1)S(1)} collective-permute-done((f16[520,512]{1,0:T(8,128)(2,1)S(1)}, f16[520,512]{1,0:T(8,128)(2,1)S(1)}, u32[]{:S(2)}, u32[]{:S(2)}) %collective-permute-start.18) | collective-permute-done | bytes 532512 | tf_op jit(solution)/shard_map/ppermute | solution.py:533
  59.0 2.7 %transport.6 = (f32[1024,512]{1,0:T(8,128)S(1)}, bf16[256,512]{1,0:T(8,128)(2,1)S(1)}, bf16[256,512]{1,0:T(8,128)(2,1)S(1)}, bf16[256,512]{1,0:T(8,128)(2,1)S(1)}, bf16[256,512]{1,0:T(8,128)(2,1)S(1)}) custom-call(f32[8,512]{1,0:T(8,128)S(1)} %get-tuple-element.74.c_ref, f32[520,512]{1,0:T(8,128)S(1)} %convert_element_type.121.refs_0_, ...), custom_call_target="tpu_custom_call" | custom-call | flops 1000 | bytes 1000 | tf_op jit(solution)/shard_map/transport/pallas_call | solution.py:350
  64.5 1.6 %final.4 = (f32[1032,128]{1,0:T(8,128)S(1)}, f32[1032,128]{1,0:T(8,128)S(1)}) custom-call(bf16[256,512]{1,0:T(8,128)(2,1)S(1)} %get-tuple-element.109.refs_0_, bf16[256,512]{1,0:T(8,128)(2,1)S(1)} %get-tuple-element.110.refs_1_, bf16[256,512]{1,0:T(8,128)(2,1)S(1)} %get-tuple-element.111.refs_2_, bf16[256,512]{1,0:T(8,128)(2,1)S(1)} %get-tuple-element.112.refs_3_, ...), custom_call_target="tpu_custom_call" | custom-call | flops 1000 | bytes 1000 | tf_op jit(solution)/shard_map/final/pallas_call | solution.py:462
  66.2 2.5 %collective-permute-start.25 = (f16[1032,128]{1,0:T(8,128)(2,1)S(1)}, f16[1032,128]{1,0:T(8,128)(2,1)S(1)}, u32[]{:S(2)}, u32[]{:S(2)}) collective-permute-start(f16[1032,128]{1,0:T(8,128)(2,1)S(1)} %convert_element_type.123), channel_id=1, source_target_pairs={{0,24},{4,28},{8,16},{12,20},{16,8},{20,12},{24,0},{28,4},{1,25},{... | collective-permute-start | bytes 792584 | tf_op jit(solution)/shard_map/ppermute | solution.py:528
  68.7 1.6 %final.5 = (f32[1032,128]{1,0:T(8,128)S(1)}, f32[1032,128]{1,0:T(8,128)S(1)}) custom-call(bf16[256,512]{1,0:T(8,128)(2,1)S(1)} %get-tuple-element.109.refs_0_, bf16[256,512]{1,0:T(8,128)(2,1)S(1)} %get-tuple-element.110.refs_1_, bf16[256,512]{1,0:T(8,128)(2,1)S(1)} %get-tuple-element.111.refs_2_, bf16[256,512]{1,0:T(8,128)(2,1)S(1)} %get-tuple-element.112.refs_3_, ...), custom_call_target="tpu_custom_call" | custom-call | flops 1000 | bytes 1000 | tf_op jit(solution)/shard_map/final/pallas_call | solution.py:462
  71.6 2.7 %transport.7 = (f32[1024,512]{1,0:T(8,128)S(1)}, bf16[256,512]{1,0:T(8,128)(2,1)S(1)}, bf16[256,512]{1,0:T(8,128)(2,1)S(1)}, bf16[256,512]{1,0:T(8,128)(2,1)S(1)}, bf16[256,512]{1,0:T(8,128)(2,1)S(1)}) custom-call(f32[8,512]{1,0:T(8,128)S(1)} %get-tuple-element.74.c_ref, f32[520,512]{1,0:T(8,128)S(1)} %convert_element_type.122.refs_0_, ...), custom_call_target="tpu_custom_call" | custom-call | flops 1000 | bytes 1000 | tf_op jit(solution)/shard_map/transport/pallas_call | solution.py:350
  79.7 1.6 %final.6 = (f32[1032,128]{1,0:T(8,128)S(1)}, f32[1032,128]{1,0:T(8,128)S(1)}) custom-call(bf16[256,512]{1,0:T(8,128)(2,1)S(1)} %get-tuple-element.125.refs_0_, bf16[256,512]{1,0:T(8,128)(2,1)S(1)} %get-tuple-element.126.refs_1_, bf16[256,512]{1,0:T(8,128)(2,1)S(1)} %get-tuple-element.127.refs_2_, bf16[256,512]{1,0:T(8,128)(2,1)S(1)} %get-tuple-element.128.refs_3_, ...), custom_call_target="tpu_custom_call" | custom-call | flops 1000 | bytes 1000 | tf_op jit(solution)/shard_map/final/pallas_call | solution.py:462
  81.4 1.6 %final.7 = (f32[1032,128]{1,0:T(8,128)S(1)}, f32[1032,128]{1,0:T(8,128)S(1)}) custom-call(bf16[256,512]{1,0:T(8,128)(2,1)S(1)} %get-tuple-element.125.refs_0_, bf16[256,512]{1,0:T(8,128)(2,1)S(1)} %get-tuple-element.126.refs_1_, bf16[256,512]{1,0:T(8,128)(2,1)S(1)} %get-tuple-element.127.refs_2_, bf16[256,512]{1,0:T(8,128)(2,1)S(1)} %get-tuple-element.128.refs_3_, ...), custom_call_target="tpu_custom_call" | custom-call | flops 1000 | bytes 1000 | tf_op jit(solution)/shard_map/final/pallas_call | solution.py:462
  84.7 2.1 %collective-permute-start.30 = (f16[1032,128]{1,0:T(8,128)(2,1)S(1)}, f16[1032,128]{1,0:T(8,128)(2,1)S(1)}, u32[]{:S(2)}, u32[]{:S(2)}) collective-permute-start(f16[1032,128]{1,0:T(8,128)(2,1)S(1)} %convert_element_type.124), channel_id=1, source_target_pairs={{0,24},{4,28},{8,16},{12,20},{16,8},{20,12},{24,0},{28,4},{1,25},{... | collective-permute-start | bytes 792584 | tf_op jit(solution)/shard_map/ppermute | solution.py:528
  86.9 2.5 %unpack.2.refs_5_ = f32[128,16,512]{2,1,0:T(8,128)} custom-call(s32[2]{0:T(128)S(1)} %pad_add_fusion.chip_ref.word_ref, f32[1032,128]{1,0:T(8,128)S(1)} %convert_element_type.130.refs_0_, f32[1032,128]{1,0:T(8,128)S(1)} %convert_element_type.132.refs_1_, f32[1032,128]{1,0:T(8,128)S(1)} %convert_element_type.134.refs_2_, ...), custom_call_target="tpu_custom_call" | custom-call | flops 1000 | bytes 1000 | tf_op jit(solution)/shard_map/unpack/pallas_call | solution.py:509
  89.4 3.0 %collective-permute-done.31 = f16[1032,128]{1,0:T(8,128)(2,1)S(1)} collective-permute-done((f16[1032,128]{1,0:T(8,128)(2,1)S(1)}, f16[1032,128]{1,0:T(8,128)(2,1)S(1)}, u32[]{:S(2)}, u32[]{:S(2)}) %collective-permute-start.31) | collective-permute-done | bytes 264224 | tf_op jit(solution)/shard_map/ppermute | solution.py:528
  92.5 5.0 %collective-permute-done.32 = f16[1032,128]{1,0:T(8,128)(2,1)S(1)} collective-permute-done((f16[1032,128]{1,0:T(8,128)(2,1)S(1)}, f16[1032,128]{1,0:T(8,128)(2,1)S(1)}, u32[]{:S(2)}, u32[]{:S(2)}) %collective-permute-start.32) | collective-permute-done | bytes 264224 | tf_op jit(solution)/shard_map/ppermute | solution.py:528
  97.6 2.5 %unpack.3 = f32[128,16,512]{2,1,0:T(8,128)} custom-call(s32[2]{0:T(128)S(1)} %pad_add_fusion.chip_ref.word_ref, f32[1032,128]{1,0:T(8,128)S(1)} %convert_element_type.125.refs_0_, f32[1032,128]{1,0:T(8,128)S(1)} %convert_element_type.127.refs_1_, f32[1032,128]{1,0:T(8,128)S(1)} %convert_element_type.129.refs_2_, ...), custom_call_target="tpu_custom_call", output_to_operand_aliasing={{}: (6, {})} | custom-call | flops 1000 | bytes 1000 | tf_op jit(solution)/shard_map/unpack/pallas_call | solution.py:509
  (114 shorter events, 32.4 us)
Async XLA Ops:
  3.6 16.2 %collective-permute-start.6 = (f16[1032,128]{1,0:T(8,128)(2,1)S(1)}, f16[1032,128]{1,0:T(8,128)(2,1)S(1)}, u32[]{:S(2)}, u32[]{:S(2)}) collective-permute-start(f16[1032,128]{1,0:T(8,128)(2,1)S(1)} %convert_element_type.112), channel_id=1, source_target_pairs={{0,16},{4,20},{8,24},{12,28},{16,0},{20,4},{24,8},{28,12},{1,17},{... | collective-permute-start | bytes 792584 | tf_op jit(solution)/shard_map/ppermute | solution.py:528
  6.7 15.1 %collective-permute-start.5 = (f16[1032,128]{1,0:T(8,128)(2,1)S(1)}, f16[1032,128]{1,0:T(8,128)(2,1)S(1)}, u32[]{:S(2)}, u32[]{:S(2)}) collective-permute-start(f16[1032,128]{1,0:T(8,128)(2,1)S(1)} %convert_element_type.110), channel_id=1, source_target_pairs={{0,8},{4,12},{8,0},{12,4},{16,24},{20,28},{24,16},{28,20},{1,9},{5... | collective-permute-start | bytes 792584 | tf_op jit(solution)/shard_map/ppermute | solution.py:528
  8.3 13.6 %collective-permute-start.4 = (f16[1032,128]{1,0:T(8,128)(2,1)S(1)}, f16[1032,128]{1,0:T(8,128)(2,1)S(1)}, u32[]{:S(2)}, u32[]{:S(2)}) collective-permute-start(f16[1032,128]{1,0:T(8,128)(2,1)S(1)} %convert_element_type.108), channel_id=1, source_target_pairs={{0,24},{4,28},{8,16},{12,20},{16,8},{20,12},{24,0},{28,4},{1,25},{... | collective-permute-start | bytes 792584 | tf_op jit(solution)/shard_map/ppermute | solution.py:528
  8.4 9.9 %collective-permute-start.7 = (f16[520,128]{1,0:T(8,128)(2,1)S(1)}, f16[520,128]{1,0:T(8,128)(2,1)S(1)}, u32[]{:S(2)}, u32[]{:S(2)}) collective-permute-start(f16[520,128]{1,0:T(8,128)(2,1)S(1)} %slice_convert_fusion), channel_id=1, source_target_pairs={{0,3},{1,0},{2,1},{3,2},{4,7},{5,4},{6,5},{7,6},{8,11},{9,8},{10,9... | collective-permute-start | bytes 399368 | tf_op jit(solution)/shard_map/ppermute | solution.py:533
  12.5 4.2 %collective-permute-start = (f32[8,512]{1,0:T(8,128)S(1)}, f32[8,512]{1,0:T(8,128)S(1)}, u32[]{:S(2)}, u32[]{:S(2)}) collective-permute-start(f32[8,512]{1,0:T(8,128)S(1)} %slice.15), channel_id=1, source_target_pairs={{0,3},{1,0},{2,1},{3,2},{4,7},{5,4},{6,5},{7,6},{8,11},{9,8},{10,9... | collective-permute-start | bytes 49160 | tf_op jit(solution)/shard_map/ppermute | solution.py:533
  16.7 10.8 %collective-permute-start.3 = (f16[1032,128]{1,0:T(8,128)(2,1)S(1)}, f16[1032,128]{1,0:T(8,128)(2,1)S(1)}, u32[]{:S(2)}, u32[]{:S(2)}) collective-permute-start(f16[1032,128]{1,0:T(8,128)(2,1)S(1)} %convert_element_type.106), channel_id=1, source_target_pairs={{0,16},{4,20},{8,24},{12,28},{16,0},{20,4},{24,8},{28,12},{1,17},{... | collective-permute-start | bytes 792584 | tf_op jit(solution)/shard_map/ppermute | solution.py:528
  18.3 9.3 %collective-permute-start.2 = (f16[1032,128]{1,0:T(8,128)(2,1)S(1)}, f16[1032,128]{1,0:T(8,128)(2,1)S(1)}, u32[]{:S(2)}, u32[]{:S(2)}) collective-permute-start(f16[1032,128]{1,0:T(8,128)(2,1)S(1)} %convert_element_type.104), channel_id=1, source_target_pairs={{0,8},{4,12},{8,0},{12,4},{16,24},{20,28},{24,16},{28,20},{1,9},{5... | collective-permute-start | bytes 792584 | tf_op jit(solution)/shard_map/ppermute | solution.py:528
  19.8 11.5 %collective-permute-start.1 = (f16[1032,128]{1,0:T(8,128)(2,1)S(1)}, f16[1032,128]{1,0:T(8,128)(2,1)S(1)}, u32[]{:S(2)}, u32[]{:S(2)}) collective-permute-start(f16[1032,128]{1,0:T(8,128)(2,1)S(1)} %convert_element_type.102), channel_id=1, source_target_pairs={{0,24},{4,28},{8,16},{12,20},{16,8},{20,12},{24,0},{28,4},{1,25},{... | collective-permute-start | bytes 792584 | tf_op jit(solution)/shard_map/ppermute | solution.py:528
  22.1 13.7 %collective-permute-start.9 = (f16[520,256]{1,0:T(8,128)(2,1)S(1)}, f16[520,256]{1,0:T(8,128)(2,1)S(1)}, u32[]{:S(2)}, u32[]{:S(2)}) collective-permute-start(f16[520,256]{1,0:T(8,128)(2,1)S(1)} %slice.20), channel_id=1, source_target_pairs={{0,3},{1,0},{2,1},{3,2},{4,7},{5,4},{6,5},{7,6},{8,11},{9,8},{10,9... | collective-permute-start | bytes 798728 | tf_op jit(solution)/shard_map/ppermute | solution.py:533
  25.6 10.2 %collective-permute-start.10 = (f16[520,128]{1,0:T(8,128)(2,1)S(1)}, f16[520,128]{1,0:T(8,128)(2,1)S(1)}, u32[]{:S(2)}, u32[]{:S(2)}) collective-permute-start(f16[520,128]{1,0:T(8,128)(2,1)S(1)} %slice.21), channel_id=1, source_target_pairs={{0,3},{1,0},{2,1},{3,2},{4,7},{5,4},{6,5},{7,6},{8,11},{9,8},{10,9... | collective-permute-start | bytes 399368 | tf_op jit(solution)/shard_map/ppermute | solution.py:533
  31.6 16.5 %collective-permute-start.8 = (f16[520,512]{1,0:T(8,128)(2,1)S(1)}, f16[520,512]{1,0:T(8,128)(2,1)S(1)}, u32[]{:S(2)}, u32[]{:S(2)}) collective-permute-start(f16[520,512]{1,0:T(8,128)(2,1)S(1)} %convert_element_type.114), channel_id=1, source_target_pairs={{0,3},{1,0},{2,1},{3,2},{4,7},{5,4},{6,5},{7,6},{8,11},{9,8},{10,9... | collective-permute-start | bytes 1597448 | tf_op jit(solution)/shard_map/ppermute | solution.py:533
  42.1 16.8 %collective-permute-start.18 = (f16[520,512]{1,0:T(8,128)(2,1)S(1)}, f16[520,512]{1,0:T(8,128)(2,1)S(1)}, u32[]{:S(2)}, u32[]{:S(2)}) collective-permute-start(f16[520,512]{1,0:T(8,128)(2,1)S(1)} %convert_element_type.120), channel_id=1, source_target_pairs={{0,1},{1,2},{2,3},{3,0},{4,5},{5,6},{6,7},{7,4},{8,9},{9,10},{10,1... | collective-permute-start | bytes 1597448 | tf_op jit(solution)/shard_map/ppermute | solution.py:533
  51.5 3.3 %collective-permute-start.19 = (bf16[256,512]{1,0:T(8,128)(2,1)S(1)}, bf16[256,512]{1,0:T(8,128)(2,1)S(1)}, u32[]{:S(2)}, u32[]{:S(2)}) collective-permute-start(bf16[256,512]{1,0:T(8,128)(2,1)S(1)} %get-tuple-element.104.refs_0_), channel_id=1, source_target_pairs={{0,4},{4,0},{8,12},{12,8},{16,20},{20,16},{24,28},{28,24},{1,5},{5... | collective-permute-start | bytes 786440 | tf_op jit(solution)/shard_map/ppermute | solution.py:528
  51.6 3.2 %collective-permute-start.20 = (bf16[256,512]{1,0:T(8,128)(2,1)S(1)}, bf16[256,512]{1,0:T(8,128)(2,1)S(1)}, u32[]{:S(2)}, u32[]{:S(2)}) collective-permute-start(bf16[256,512]{1,0:T(8,128)(2,1)S(1)} %get-tuple-element.105.refs_1_), channel_id=1, source_target_pairs={{0,4},{4,0},{8,12},{12,8},{16,20},{20,16},{24,28},{28,24},{1,5},{5... | collective-permute-start | bytes 786440 | tf_op jit(solution)/shard_map/ppermute | solution.py:528
  54.5 16.9 %collective-permute-start.17 = (f16[520,512]{1,0:T(8,128)(2,1)S(1)}, f16[520,512]{1,0:T(8,128)(2,1)S(1)}, u32[]{:S(2)}, u32[]{:S(2)}) collective-permute-start(f16[520,512]{1,0:T(8,128)(2,1)S(1)} %convert_element_type.119), channel_id=1, source_target_pairs={{0,1},{1,2},{2,3},{3,0},{4,5},{5,6},{6,7},{7,4},{8,9},{9,10},{10,1... | collective-permute-start | bytes 1597448 | tf_op jit(solution)/shard_map/ppermute | solution.py:533
  66.2 9.3 %collective-permute-start.25 = (f16[1032,128]{1,0:T(8,128)(2,1)S(1)}, f16[1032,128]{1,0:T(8,128)(2,1)S(1)}, u32[]{:S(2)}, u32[]{:S(2)}) collective-permute-start(f16[1032,128]{1,0:T(8,128)(2,1)S(1)} %convert_element_type.123), channel_id=1, source_target_pairs={{0,24},{4,28},{8,16},{12,20},{16,8},{20,12},{24,0},{28,4},{1,25},{... | collective-permute-start | bytes 792584 | tf_op jit(solution)/shard_map/ppermute | solution.py:528
  75.5 4.2 %collective-permute-start.27 = (bf16[256,512]{1,0:T(8,128)(2,1)S(1)}, bf16[256,512]{1,0:T(8,128)(2,1)S(1)}, u32[]{:S(2)}, u32[]{:S(2)}) collective-permute-start(bf16[256,512]{1,0:T(8,128)(2,1)S(1)} %get-tuple-element.126.refs_1_), channel_id=1, source_target_pairs={{0,4},{4,0},{8,12},{12,8},{16,20},{20,16},{24,28},{28,24},{1,5},{5... | collective-permute-start | bytes 786440 | tf_op jit(solution)/shard_map/ppermute | solution.py:528
  76.0 3.7 %collective-permute-start.28 = (bf16[256,512]{1,0:T(8,128)(2,1)S(1)}, bf16[256,512]{1,0:T(8,128)(2,1)S(1)}, u32[]{:S(2)}, u32[]{:S(2)}) collective-permute-start(bf16[256,512]{1,0:T(8,128)(2,1)S(1)} %get-tuple-element.127.refs_2_), channel_id=1, source_target_pairs={{0,4},{4,0},{8,12},{12,8},{16,20},{20,16},{24,28},{28,24},{1,5},{5... | collective-permute-start | bytes 786440 | tf_op jit(solution)/shard_map/ppermute | solution.py:528
  76.0 3.7 %collective-permute-start.29 = (bf16[256,512]{1,0:T(8,128)(2,1)S(1)}, bf16[256,512]{1,0:T(8,128)(2,1)S(1)}, u32[]{:S(2)}, u32[]{:S(2)}) collective-permute-start(bf16[256,512]{1,0:T(8,128)(2,1)S(1)} %get-tuple-element.128.refs_3_), channel_id=1, source_target_pairs={{0,4},{4,0},{8,12},{12,8},{16,20},{20,16},{24,28},{28,24},{1,5},{5... | collective-permute-start | bytes 786440 | tf_op jit(solution)/shard_map/ppermute | solution.py:528
  76.6 10.2 %collective-permute-start.33 = (f16[1032,128]{1,0:T(8,128)(2,1)S(1)}, f16[1032,128]{1,0:T(8,128)(2,1)S(1)}, u32[]{:S(2)}, u32[]{:S(2)}) collective-permute-start(f16[1032,128]{1,0:T(8,128)(2,1)S(1)} %convert_element_type.131), channel_id=1, source_target_pairs={{0,8},{4,12},{8,0},{12,4},{16,24},{20,28},{24,16},{28,20},{1,9},{5... | collective-permute-start | bytes 792584 | tf_op jit(solution)/shard_map/ppermute | solution.py:528
  78.2 8.7 %collective-permute-start.34 = (f16[1032,128]{1,0:T(8,128)(2,1)S(1)}, f16[1032,128]{1,0:T(8,128)(2,1)S(1)}, u32[]{:S(2)}, u32[]{:S(2)}) collective-permute-start(f16[1032,128]{1,0:T(8,128)(2,1)S(1)} %convert_element_type.133), channel_id=1, source_target_pairs={{0,16},{4,20},{8,24},{12,28},{16,0},{20,4},{24,8},{28,12},{1,17},{... | collective-permute-start | bytes 792584 | tf_op jit(solution)/shard_map/ppermute | solution.py:528
  83.1 9.4 %collective-permute-start.31 = (f16[1032,128]{1,0:T(8,128)(2,1)S(1)}, f16[1032,128]{1,0:T(8,128)(2,1)S(1)}, u32[]{:S(2)}, u32[]{:S(2)}) collective-permute-start(f16[1032,128]{1,0:T(8,128)(2,1)S(1)} %convert_element_type.126), channel_id=1, source_target_pairs={{0,8},{4,12},{8,0},{12,4},{16,24},{20,28},{24,16},{28,20},{1,9},{5... | collective-permute-start | bytes 792584 | tf_op jit(solution)/shard_map/ppermute | solution.py:528
  83.7 13.8 %collective-permute-start.32 = (f16[1032,128]{1,0:T(8,128)(2,1)S(1)}, f16[1032,128]{1,0:T(8,128)(2,1)S(1)}, u32[]{:S(2)}, u32[]{:S(2)}) collective-permute-start(f16[1032,128]{1,0:T(8,128)(2,1)S(1)} %convert_element_type.128), channel_id=1, source_target_pairs={{0,16},{4,20},{8,24},{12,28},{16,0},{20,4},{24,8},{28,12},{1,17},{... | collective-permute-start | bytes 792584 | tf_op jit(solution)/shard_map/ppermute | solution.py:528
  84.7 12.9 %collective-permute-start.30 = (f16[1032,128]{1,0:T(8,128)(2,1)S(1)}, f16[1032,128]{1,0:T(8,128)(2,1)S(1)}, u32[]{:S(2)}, u32[]{:S(2)}) collective-permute-start(f16[1032,128]{1,0:T(8,128)(2,1)S(1)} %convert_element_type.124), channel_id=1, source_target_pairs={{0,24},{4,28},{8,16},{12,20},{16,8},{20,12},{24,0},{28,4},{1,25},{... | collective-permute-start | bytes 792584 | tf_op jit(solution)/shard_map/ppermute | solution.py:528
  (15 other events, 40.0 us)

commit v8 on v6

--- a/solution.py
+++ b/solution.py
@@ -199,10 +199,10 @@
     return pl.pallas_call(
         functools.partial(message_kernel, cells),
         grid=(1,),
-        in_specs=[pl.BlockSpec(p.shape, lambda i: (0, 0)) for p in pieces] + [anywhere()],
+        in_specs=[resident() for _ in pieces] + [anywhere()],
         out_specs=resident(),
         out_shape=jax.ShapeDtypeStruct(shape, jnp.float32),
-        compiler_params=params([True] * len(pieces) + [False]),
+        compiler_params=params(),
         cost_estimate=LIGHT,
         name="message",
     )(*pieces, after)
@@ -224,10 +224,10 @@
     return pl.pallas_call(
         functools.partial(spread_kernel, planes, cells),
         grid=(1,),
-        in_specs=[pl.BlockSpec(p.shape, lambda i: (0, 0)) for p in pieces] + [anywhere()],
+        in_specs=[resident() for _ in pieces] + [anywhere()],
         out_specs=resident(),
         out_shape=jax.ShapeDtypeStruct(shape, jnp.float32),
-        compiler_params=params([True] * len(pieces) + [False]),
+        compiler_params=params(),
         cost_estimate=LIGHT,
         name="spread",
     )(*pieces, after)
@@ -496,7 +496,7 @@
     width = cells * len(order)
     steps = width // LANES
     shape = (LANES, planes, width * CHUNKS)
-    specs = [pl.BlockSpec(p.shape, lambda i, s: (0, 0)) for p in pieces]
+    specs = [resident() for _ in pieces]
     operands = list(pieces)
     count = len(pieces)
     specs.append(anywhere())
@@ -517,7 +517,7 @@
         ),
         out_shape=jax.ShapeDtypeStruct(shape, jnp.float32),
         input_output_aliases=aliases,
-        compiler_params=params([False] + [True] * count + [False] * (len(operands) - count)),
+        compiler_params=params(),
         cost_estimate=LIGHT,
         name="unpack",
     )(chip, *operands)

time: 100 us -> 100 us (level)
  no operation moved by 1% of the time
where the time goes in v8:
time: 100 us
  Pallas kernels  37.7 us (38%)
  starting transfers between devices  34.4 us (34%)
  waiting for transfers between devices  25.6 us (26%)
  other arithmetic  1.81 us (2%)
    ppermute x28, starting transfers between devices, exchange(): return lax.ppermute(array, 'vel', [(i, i ^ mask) for i in range(count)])  21.7 us
    ppermute x28, waiting for transfers between devices, exchange(): return lax.ppermute(array, 'vel', [(i, i ^ mask) for i in range(count)])  19.3 us
    ppermute x7, starting transfers between devices, shift(): lax.ppermute(array, 'space', [(i, (i + step) % count) for i in range(coun...  12.7 us
    pallas_call x4, Pallas kernels, transport(): pl.pallas_call(functools.partial(advect_kernel, cells, 16, before, count,...  11.2 us
    pallas_call x2, Pallas kernels, pack(): pl.pallas_call(functools.partial(pack_kernel, order, planes, cells), grid...  7.04 us
    pallas_call x4, Pallas kernels, final(): pl.pallas_call(functools.partial(final_kernel, part, len(own)), in_specs=...  6.53 us
    ppermute x7, waiting for transfers between devices, shift(): lax.ppermute(array, 'space', [(i, (i + step) % count) for i in range(coun...  6.25 us
    pallas_call x4, Pallas kernels, collide_half(): pl.pallas_call(functools.partial(half_kernel, len(own), first, sends), in...  5.65 us
  transfers between devices with their start and end apart: 35, of which 18 were waited for; matrix products, arithmetic and copies ran while one was open for 2% of the time, Pallas kernels for 32%

profile of v8, /device:TPU:0, one launch (start us, length us, event | category | flops | bytes accessed | tf_op | source)
XLA Modules:
  0.0 100.2 jit_solution(4860617803285029771)
XLA Ops:
  0.1 3.5 %pack.2 = (f32[1032,128]{1,0:T(8,128)S(1)}, f32[1032,128]{1,0:T(8,128)S(1)}, f32[1032,128]{1,0:T(8,128)S(1)}, f32[1032,128]{1,0:T(8,128)S(1)}) custom-call(s32[2]{0:T(128)S(1)} %pad_add_fusion.chip_ref.word_ref, f32[128,16,512]{2,1,0:T(8,128)} %d_ref.3, f32[128,16,512]{2,1,0:T(8,128)} %d_ref.3), custom_call_target="tpu_custom_call" | custom-call | flops 1000 | bytes 1000 | tf_op jit(solution)/shard_map/pack/pallas_call | solution.py:172
  3.6 3.0 %collective-permute-start.6 = (f16[1032,128]{1,0:T(8,128)(2,1)S(1)}, f16[1032,128]{1,0:T(8,128)(2,1)S(1)}, u32[]{:S(2)}, u32[]{:S(2)}) collective-permute-start(f16[1032,128]{1,0:T(8,128)(2,1)S(1)} %convert_element_type.112), channel_id=1, source_target_pairs={{0,16},{4,20},{8,24},{12,28},{16,0},{20,4},{24,8},{28,12},{1,17},{... | collective-permute-start | bytes 792584 | tf_op jit(solution)/shard_map/ppermute | solution.py:528
  8.4 4.1 %collective-permute-start.7 = (f16[520,128]{1,0:T(8,128)(2,1)S(1)}, f16[520,128]{1,0:T(8,128)(2,1)S(1)}, u32[]{:S(2)}, u32[]{:S(2)}) collective-permute-start(f16[520,128]{1,0:T(8,128)(2,1)S(1)} %slice_convert_fusion), channel_id=1, source_target_pairs={{0,3},{1,0},{2,1},{3,2},{4,7},{5,4},{6,5},{7,6},{8,11},{9,8},{10,9... | collective-permute-start | bytes 399368 | tf_op jit(solution)/shard_map/ppermute | solution.py:533
  13.0 3.6 %pack.3 = (f32[1032,128]{1,0:T(8,128)S(1)}, f32[1032,128]{1,0:T(8,128)S(1)}, f32[1032,128]{1,0:T(8,128)S(1)}, f32[1032,128]{1,0:T(8,128)S(1)}) custom-call(s32[2]{0:T(128)S(1)} %pad_add_fusion.chip_ref.word_ref, f32[128,16,512]{2,1,0:T(8,128)} %d_ref.3, f32[1032,128]{1,0:T(8,128)S(1)} %get-tuple-element.81.after_ref.refs_3_), custom_call_target="tpu_custom_call" | custom-call | flops 1000 | bytes 1000 | tf_op jit(solution)/shard_map/pack/pallas_call | solution.py:172
  16.7 1.6 %collective-permute-start.3 = (f16[1032,128]{1,0:T(8,128)(2,1)S(1)}, f16[1032,128]{1,0:T(8,128)(2,1)S(1)}, u32[]{:S(2)}, u32[]{:S(2)}) collective-permute-start(f16[1032,128]{1,0:T(8,128)(2,1)S(1)} %convert_element_type.106), channel_id=1, source_target_pairs={{0,16},{4,20},{8,24},{12,28},{16,0},{20,4},{24,8},{28,12},{1,17},{... | collective-permute-start | bytes 792584 | tf_op jit(solution)/shard_map/ppermute | solution.py:528
  22.1 3.5 %collective-permute-start.9 = (f16[520,256]{1,0:T(8,128)(2,1)S(1)}, f16[520,256]{1,0:T(8,128)(2,1)S(1)}, u32[]{:S(2)}, u32[]{:S(2)}) collective-permute-start(f16[520,256]{1,0:T(8,128)(2,1)S(1)} %slice.20), channel_id=1, source_target_pairs={{0,3},{1,0},{2,1},{3,2},{4,7},{5,4},{6,5},{7,6},{8,11},{9,8},{10,9... | collective-permute-start | bytes 798728 | tf_op jit(solution)/shard_map/ppermute | solution.py:533
  27.6 3.7 %collective-permute-done.1 = f16[1032,128]{1,0:T(8,128)(2,1)S(1)} collective-permute-done((f16[1032,128]{1,0:T(8,128)(2,1)S(1)}, f16[1032,128]{1,0:T(8,128)(2,1)S(1)}, u32[]{:S(2)}, u32[]{:S(2)}) %collective-permute-start.1) | collective-permute-done | bytes 264224 | tf_op jit(solution)/shard_map/ppermute | solution.py:528
  31.6 3.9 %collective-permute-start.8 = (f16[520,512]{1,0:T(8,128)(2,1)S(1)}, f16[520,512]{1,0:T(8,128)(2,1)S(1)}, u32[]{:S(2)}, u32[]{:S(2)}) collective-permute-start(f16[520,512]{1,0:T(8,128)(2,1)S(1)} %convert_element_type.114), channel_id=1, source_target_pairs={{0,3},{1,0},{2,1},{3,2},{4,7},{5,4},{6,5},{7,6},{8,11},{9,8},{10,9... | collective-permute-start | bytes 1597448 | tf_op jit(solution)/shard_map/ppermute | solution.py:533
  35.9 2.7 %transport.4 = (f32[1024,512]{1,0:T(8,128)S(1)}, bf16[256,512]{1,0:T(8,128)(2,1)S(1)}, bf16[256,512]{1,0:T(8,128)(2,1)S(1)}, bf16[256,512]{1,0:T(8,128)(2,1)S(1)}, bf16[256,512]{1,0:T(8,128)(2,1)S(1)}) custom-call(f32[8,512]{1,0:T(8,128)S(1)} %get-tuple-element.74.c_ref, f32[520,256]{1,0:T(8,128)S(1)} %convert_element_type.115.refs_0_, ...), custom_call_target="tpu_custom_call" | custom-call | flops 1000 | bytes 1000 | tf_op jit(solution)/shard_map/transport/pallas_call | solution.py:350
  45.5 2.5 %collective-permute-done.8 = f16[520,512]{1,0:T(8,128)(2,1)S(1)} collective-permute-done((f16[520,512]{1,0:T(8,128)(2,1)S(1)}, f16[520,512]{1,0:T(8,128)(2,1)S(1)}, u32[]{:S(2)}, u32[]{:S(2)}) %collective-permute-start.8) | collective-permute-done | bytes 532512 | tf_op jit(solution)/shard_map/ppermute | solution.py:533
  48.2 2.8 %transport.5 = (f32[1024,512]{1,0:T(8,128)S(1)}, bf16[256,512]{1,0:T(8,128)(2,1)S(1)}, bf16[256,512]{1,0:T(8,128)(2,1)S(1)}, bf16[256,512]{1,0:T(8,128)(2,1)S(1)}, bf16[256,512]{1,0:T(8,128)(2,1)S(1)}) custom-call(f32[8,512]{1,0:T(8,128)S(1)} %get-tuple-element.74.c_ref, f32[520,512]{1,0:T(8,128)S(1)} %convert_element_type.118.refs_0_, ...), custom_call_target="tpu_custom_call" | custom-call | flops 1000 | bytes 1000 | tf_op jit(solution)/shard_map/transport/pallas_call | solution.py:350
  56.2 2.6 %collective-permute-done.18 = f16[520,512]{1,0:T(8,128)(2,1)S(1)} collective-permute-done((f16[520,512]{1,0:T(8,128)(2,1)S(1)}, f16[520,512]{1,0:T(8,128)(2,1)S(1)}, u32[]{:S(2)}, u32[]{:S(2)}) %collective-permute-start.18) | collective-permute-done | bytes 532512 | tf_op jit(solution)/shard_map/ppermute | solution.py:533
  58.9 2.9 %transport.6 = (f32[1024,512]{1,0:T(8,128)S(1)}, bf16[256,512]{1,0:T(8,128)(2,1)S(1)}, bf16[256,512]{1,0:T(8,128)(2,1)S(1)}, bf16[256,512]{1,0:T(8,128)(2,1)S(1)}, bf16[256,512]{1,0:T(8,128)(2,1)S(1)}) custom-call(f32[8,512]{1,0:T(8,128)S(1)} %get-tuple-element.74.c_ref, f32[520,512]{1,0:T(8,128)S(1)} %convert_element_type.121.refs_0_, ...), custom_call_target="tpu_custom_call" | custom-call | flops 1000 | bytes 1000 | tf_op jit(solution)/shard_map/transport/pallas_call | solution.py:350
  64.6 1.6 %final.4 = (f32[1032,128]{1,0:T(8,128)S(1)}, f32[1032,128]{1,0:T(8,128)S(1)}) custom-call(bf16[256,512]{1,0:T(8,128)(2,1)S(1)} %get-tuple-element.109.refs_0_, bf16[256,512]{1,0:T(8,128)(2,1)S(1)} %get-tuple-element.110.refs_1_, bf16[256,512]{1,0:T(8,128)(2,1)S(1)} %get-tuple-element.111.refs_2_, bf16[256,512]{1,0:T(8,128)(2,1)S(1)} %get-tuple-element.112.refs_3_, ...), custom_call_target="tpu_custom_call" | custom-call | flops 1000 | bytes 1000 | tf_op jit(solution)/shard_map/final/pallas_call | solution.py:462
  66.2 2.5 %collective-permute-start.25 = (f16[1032,128]{1,0:T(8,128)(2,1)S(1)}, f16[1032,128]{1,0:T(8,128)(2,1)S(1)}, u32[]{:S(2)}, u32[]{:S(2)}) collective-permute-start(f16[1032,128]{1,0:T(8,128)(2,1)S(1)} %convert_element_type.123), channel_id=1, source_target_pairs={{0,24},{4,28},{8,16},{12,20},{16,8},{20,12},{24,0},{28,4},{1,25},{... | collective-permute-start | bytes 792584 | tf_op jit(solution)/shard_map/ppermute | solution.py:528
  68.8 1.6 %final.5 = (f32[1032,128]{1,0:T(8,128)S(1)}, f32[1032,128]{1,0:T(8,128)S(1)}) custom-call(bf16[256,512]{1,0:T(8,128)(2,1)S(1)} %get-tuple-element.109.refs_0_, bf16[256,512]{1,0:T(8,128)(2,1)S(1)} %get-tuple-element.110.refs_1_, bf16[256,512]{1,0:T(8,128)(2,1)S(1)} %get-tuple-element.111.refs_2_, bf16[256,512]{1,0:T(8,128)(2,1)S(1)} %get-tuple-element.112.refs_3_, ...), custom_call_target="tpu_custom_call" | custom-call | flops 1000 | bytes 1000 | tf_op jit(solution)/shard_map/final/pallas_call | solution.py:462
  71.6 2.9 %transport.7 = (f32[1024,512]{1,0:T(8,128)S(1)}, bf16[256,512]{1,0:T(8,128)(2,1)S(1)}, bf16[256,512]{1,0:T(8,128)(2,1)S(1)}, bf16[256,512]{1,0:T(8,128)(2,1)S(1)}, bf16[256,512]{1,0:T(8,128)(2,1)S(1)}) custom-call(f32[8,512]{1,0:T(8,128)S(1)} %get-tuple-element.74.c_ref, f32[520,512]{1,0:T(8,128)S(1)} %convert_element_type.122.refs_0_, ...), custom_call_target="tpu_custom_call" | custom-call | flops 1000 | bytes 1000 | tf_op jit(solution)/shard_map/transport/pallas_call | solution.py:350
  79.8 1.6 %final.6 = (f32[1032,128]{1,0:T(8,128)S(1)}, f32[1032,128]{1,0:T(8,128)S(1)}) custom-call(bf16[256,512]{1,0:T(8,128)(2,1)S(1)} %get-tuple-element.125.refs_0_, bf16[256,512]{1,0:T(8,128)(2,1)S(1)} %get-tuple-element.126.refs_1_, bf16[256,512]{1,0:T(8,128)(2,1)S(1)} %get-tuple-element.127.refs_2_, bf16[256,512]{1,0:T(8,128)(2,1)S(1)} %get-tuple-element.128.refs_3_, ...), custom_call_target="tpu_custom_call" | custom-call | flops 1000 | bytes 1000 | tf_op jit(solution)/shard_map/final/pallas_call | solution.py:462
  81.4 1.6 %final.7 = (f32[1032,128]{1,0:T(8,128)S(1)}, f32[1032,128]{1,0:T(8,128)S(1)}) custom-call(bf16[256,512]{1,0:T(8,128)(2,1)S(1)} %get-tuple-element.125.refs_0_, bf16[256,512]{1,0:T(8,128)(2,1)S(1)} %get-tuple-element.126.refs_1_, bf16[256,512]{1,0:T(8,128)(2,1)S(1)} %get-tuple-element.127.refs_2_, bf16[256,512]{1,0:T(8,128)(2,1)S(1)} %get-tuple-element.128.refs_3_, ...), custom_call_target="tpu_custom_call" | custom-call | flops 1000 | bytes 1000 | tf_op jit(solution)/shard_map/final/pallas_call | solution.py:462
  84.7 2.1 %collective-permute-start.30 = (f16[1032,128]{1,0:T(8,128)(2,1)S(1)}, f16[1032,128]{1,0:T(8,128)(2,1)S(1)}, u32[]{:S(2)}, u32[]{:S(2)}) collective-permute-start(f16[1032,128]{1,0:T(8,128)(2,1)S(1)} %convert_element_type.124), channel_id=1, source_target_pairs={{0,24},{4,28},{8,16},{12,20},{16,8},{20,12},{24,0},{28,4},{1,25},{... | collective-permute-start | bytes 792584 | tf_op jit(solution)/shard_map/ppermute | solution.py:528
  87.0 2.5 %unpack.2.refs_5_ = f32[128,16,512]{2,1,0:T(8,128)} custom-call(s32[2]{0:T(128)S(1)} %pad_add_fusion.chip_ref.word_ref, f32[1032,128]{1,0:T(8,128)S(1)} %convert_element_type.130.refs_0_, f32[1032,128]{1,0:T(8,128)S(1)} %convert_element_type.132.refs_1_, f32[1032,128]{1,0:T(8,128)S(1)} %convert_element_type.134.refs_2_, ...), custom_call_target="tpu_custom_call" | custom-call | flops 1000 | bytes 1000 | tf_op jit(solution)/shard_map/unpack/pallas_call | solution.py:509
  89.5 3.0 %collective-permute-done.31 = f16[1032,128]{1,0:T(8,128)(2,1)S(1)} collective-permute-done((f16[1032,128]{1,0:T(8,128)(2,1)S(1)}, f16[1032,128]{1,0:T(8,128)(2,1)S(1)}, u32[]{:S(2)}, u32[]{:S(2)}) %collective-permute-start.31) | collective-permute-done | bytes 264224 | tf_op jit(solution)/shard_map/ppermute | solution.py:528
  92.6 5.0 %collective-permute-done.32 = f16[1032,128]{1,0:T(8,128)(2,1)S(1)} collective-permute-done((f16[1032,128]{1,0:T(8,128)(2,1)S(1)}, f16[1032,128]{1,0:T(8,128)(2,1)S(1)}, u32[]{:S(2)}, u32[]{:S(2)}) %collective-permute-start.32) | collective-permute-done | bytes 264224 | tf_op jit(solution)/shard_map/ppermute | solution.py:528
  97.7 2.5 %unpack.3 = f32[128,16,512]{2,1,0:T(8,128)} custom-call(s32[2]{0:T(128)S(1)} %pad_add_fusion.chip_ref.word_ref, f32[1032,128]{1,0:T(8,128)S(1)} %convert_element_type.125.refs_0_, f32[1032,128]{1,0:T(8,128)S(1)} %convert_element_type.127.refs_1_, f32[1032,128]{1,0:T(8,128)S(1)} %convert_element_type.129.refs_2_, ...), custom_call_target="tpu_custom_call", output_to_operand_aliasing={{}: (6, {})} | custom-call | flops 1000 | bytes 1000 | tf_op jit(solution)/shard_map/unpack/pallas_call | solution.py:509
  (114 shorter events, 32.3 us)
Async XLA Ops:
  3.6 16.2 %collective-permute-start.6 = (f16[1032,128]{1,0:T(8,128)(2,1)S(1)}, f16[1032,128]{1,0:T(8,128)(2,1)S(1)}, u32[]{:S(2)}, u32[]{:S(2)}) collective-permute-start(f16[1032,128]{1,0:T(8,128)(2,1)S(1)} %convert_element_type.112), channel_id=1, source_target_pairs={{0,16},{4,20},{8,24},{12,28},{16,0},{20,4},{24,8},{28,12},{1,17},{... | collective-permute-start | bytes 792584 | tf_op jit(solution)/shard_map/ppermute | solution.py:528
  6.7 15.1 %collective-permute-start.5 = (f16[1032,128]{1,0:T(8,128)(2,1)S(1)}, f16[1032,128]{1,0:T(8,128)(2,1)S(1)}, u32[]{:S(2)}, u32[]{:S(2)}) collective-permute-start(f16[1032,128]{1,0:T(8,128)(2,1)S(1)} %convert_element_type.110), channel_id=1, source_target_pairs={{0,8},{4,12},{8,0},{12,4},{16,24},{20,28},{24,16},{28,20},{1,9},{5... | collective-permute-start | bytes 792584 | tf_op jit(solution)/shard_map/ppermute | solution.py:528
  8.3 13.6 %collective-permute-start.4 = (f16[1032,128]{1,0:T(8,128)(2,1)S(1)}, f16[1032,128]{1,0:T(8,128)(2,1)S(1)}, u32[]{:S(2)}, u32[]{:S(2)}) collective-permute-start(f16[1032,128]{1,0:T(8,128)(2,1)S(1)} %convert_element_type.108), channel_id=1, source_target_pairs={{0,24},{4,28},{8,16},{12,20},{16,8},{20,12},{24,0},{28,4},{1,25},{... | collective-permute-start | bytes 792584 | tf_op jit(solution)/shard_map/ppermute | solution.py:528
  8.4 9.9 %collective-permute-start.7 = (f16[520,128]{1,0:T(8,128)(2,1)S(1)}, f16[520,128]{1,0:T(8,128)(2,1)S(1)}, u32[]{:S(2)}, u32[]{:S(2)}) collective-permute-start(f16[520,128]{1,0:T(8,128)(2,1)S(1)} %slice_convert_fusion), channel_id=1, source_target_pairs={{0,3},{1,0},{2,1},{3,2},{4,7},{5,4},{6,5},{7,6},{8,11},{9,8},{10,9... | collective-permute-start | bytes 399368 | tf_op jit(solution)/shard_map/ppermute | solution.py:533
  12.5 4.2 %collective-permute-start = (f32[8,512]{1,0:T(8,128)S(1)}, f32[8,512]{1,0:T(8,128)S(1)}, u32[]{:S(2)}, u32[]{:S(2)}) collective-permute-start(f32[8,512]{1,0:T(8,128)S(1)} %slice.15), channel_id=1, source_target_pairs={{0,3},{1,0},{2,1},{3,2},{4,7},{5,4},{6,5},{7,6},{8,11},{9,8},{10,9... | collective-permute-start | bytes 49160 | tf_op jit(solution)/shard_map/ppermute | solution.py:533
  16.7 10.8 %collective-permute-start.3 = (f16[1032,128]{1,0:T(8,128)(2,1)S(1)}, f16[1032,128]{1,0:T(8,128)(2,1)S(1)}, u32[]{:S(2)}, u32[]{:S(2)}) collective-permute-start(f16[1032,128]{1,0:T(8,128)(2,1)S(1)} %convert_element_type.106), channel_id=1, source_target_pairs={{0,16},{4,20},{8,24},{12,28},{16,0},{20,4},{24,8},{28,12},{1,17},{... | collective-permute-start | bytes 792584 | tf_op jit(solution)/shard_map/ppermute | solution.py:528
  18.3 9.3 %collective-permute-start.2 = (f16[1032,128]{1,0:T(8,128)(2,1)S(1)}, f16[1032,128]{1,0:T(8,128)(2,1)S(1)}, u32[]{:S(2)}, u32[]{:S(2)}) collective-permute-start(f16[1032,128]{1,0:T(8,128)(2,1)S(1)} %convert_element_type.104), channel_id=1, source_target_pairs={{0,8},{4,12},{8,0},{12,4},{16,24},{20,28},{24,16},{28,20},{1,9},{5... | collective-permute-start | bytes 792584 | tf_op jit(solution)/shard_map/ppermute | solution.py:528
  19.8 11.5 %collective-permute-start.1 = (f16[1032,128]{1,0:T(8,128)(2,1)S(1)}, f16[1032,128]{1,0:T(8,128)(2,1)S(1)}, u32[]{:S(2)}, u32[]{:S(2)}) collective-permute-start(f16[1032,128]{1,0:T(8,128)(2,1)S(1)} %convert_element_type.102), channel_id=1, source_target_pairs={{0,24},{4,28},{8,16},{12,20},{16,8},{20,12},{24,0},{28,4},{1,25},{... | collective-permute-start | bytes 792584 | tf_op jit(solution)/shard_map/ppermute | solution.py:528
  22.1 13.7 %collective-permute-start.9 = (f16[520,256]{1,0:T(8,128)(2,1)S(1)}, f16[520,256]{1,0:T(8,128)(2,1)S(1)}, u32[]{:S(2)}, u32[]{:S(2)}) collective-permute-start(f16[520,256]{1,0:T(8,128)(2,1)S(1)} %slice.20), channel_id=1, source_target_pairs={{0,3},{1,0},{2,1},{3,2},{4,7},{5,4},{6,5},{7,6},{8,11},{9,8},{10,9... | collective-permute-start | bytes 798728 | tf_op jit(solution)/shard_map/ppermute | solution.py:533
  25.6 10.2 %collective-permute-start.10 = (f16[520,128]{1,0:T(8,128)(2,1)S(1)}, f16[520,128]{1,0:T(8,128)(2,1)S(1)}, u32[]{:S(2)}, u32[]{:S(2)}) collective-permute-start(f16[520,128]{1,0:T(8,128)(2,1)S(1)} %slice.21), channel_id=1, source_target_pairs={{0,3},{1,0},{2,1},{3,2},{4,7},{5,4},{6,5},{7,6},{8,11},{9,8},{10,9... | collective-permute-start | bytes 399368 | tf_op jit(solution)/shard_map/ppermute | solution.py:533
  31.6 16.5 %collective-permute-start.8 = (f16[520,512]{1,0:T(8,128)(2,1)S(1)}, f16[520,512]{1,0:T(8,128)(2,1)S(1)}, u32[]{:S(2)}, u32[]{:S(2)}) collective-permute-start(f16[520,512]{1,0:T(8,128)(2,1)S(1)} %convert_element_type.114), channel_id=1, source_target_pairs={{0,3},{1,0},{2,1},{3,2},{4,7},{5,4},{6,5},{7,6},{8,11},{9,8},{10,9... | collective-permute-start | bytes 1597448 | tf_op jit(solution)/shard_map/ppermute | solution.py:533
  42.2 16.7 %collective-permute-start.18 = (f16[520,512]{1,0:T(8,128)(2,1)S(1)}, f16[520,512]{1,0:T(8,128)(2,1)S(1)}, u32[]{:S(2)}, u32[]{:S(2)}) collective-permute-start(f16[520,512]{1,0:T(8,128)(2,1)S(1)} %convert_element_type.120), channel_id=1, source_target_pairs={{0,1},{1,2},{2,3},{3,0},{4,5},{5,6},{6,7},{7,4},{8,9},{9,10},{10,1... | collective-permute-start | bytes 1597448 | tf_op jit(solution)/shard_map/ppermute | solution.py:533
  51.6 3.3 %collective-permute-start.19 = (bf16[256,512]{1,0:T(8,128)(2,1)S(1)}, bf16[256,512]{1,0:T(8,128)(2,1)S(1)}, u32[]{:S(2)}, u32[]{:S(2)}) collective-permute-start(bf16[256,512]{1,0:T(8,128)(2,1)S(1)} %get-tuple-element.104.refs_0_), channel_id=1, source_target_pairs={{0,4},{4,0},{8,12},{12,8},{16,20},{20,16},{24,28},{28,24},{1,5},{5... | collective-permute-start | bytes 786440 | tf_op jit(solution)/shard_map/ppermute | solution.py:528
  51.6 3.2 %collective-permute-start.20 = (bf16[256,512]{1,0:T(8,128)(2,1)S(1)}, bf16[256,512]{1,0:T(8,128)(2,1)S(1)}, u32[]{:S(2)}, u32[]{:S(2)}) collective-permute-start(bf16[256,512]{1,0:T(8,128)(2,1)S(1)} %get-tuple-element.105.refs_1_), channel_id=1, source_target_pairs={{0,4},{4,0},{8,12},{12,8},{16,20},{20,16},{24,28},{28,24},{1,5},{5... | collective-permute-start | bytes 786440 | tf_op jit(solution)/shard_map/ppermute | solution.py:528
  54.6 16.9 %collective-permute-start.17 = (f16[520,512]{1,0:T(8,128)(2,1)S(1)}, f16[520,512]{1,0:T(8,128)(2,1)S(1)}, u32[]{:S(2)}, u32[]{:S(2)}) collective-permute-start(f16[520,512]{1,0:T(8,128)(2,1)S(1)} %convert_element_type.119), channel_id=1, source_target_pairs={{0,1},{1,2},{2,3},{3,0},{4,5},{5,6},{6,7},{7,4},{8,9},{9,10},{10,1... | collective-permute-start | bytes 1597448 | tf_op jit(solution)/shard_map/ppermute | solution.py:533
  66.2 9.4 %collective-permute-start.25 = (f16[1032,128]{1,0:T(8,128)(2,1)S(1)}, f16[1032,128]{1,0:T(8,128)(2,1)S(1)}, u32[]{:S(2)}, u32[]{:S(2)}) collective-permute-start(f16[1032,128]{1,0:T(8,128)(2,1)S(1)} %convert_element_type.123), channel_id=1, source_target_pairs={{0,24},{4,28},{8,16},{12,20},{16,8},{20,12},{24,0},{28,4},{1,25},{... | collective-permute-start | bytes 792584 | tf_op jit(solution)/shard_map/ppermute | solution.py:528
  75.6 4.2 %collective-permute-start.27 = (bf16[256,512]{1,0:T(8,128)(2,1)S(1)}, bf16[256,512]{1,0:T(8,128)(2,1)S(1)}, u32[]{:S(2)}, u32[]{:S(2)}) collective-permute-start(bf16[256,512]{1,0:T(8,128)(2,1)S(1)} %get-tuple-element.126.refs_1_), channel_id=1, source_target_pairs={{0,4},{4,0},{8,12},{12,8},{16,20},{20,16},{24,28},{28,24},{1,5},{5... | collective-permute-start | bytes 786440 | tf_op jit(solution)/shard_map/ppermute | solution.py:528
  76.1 3.7 %collective-permute-start.28 = (bf16[256,512]{1,0:T(8,128)(2,1)S(1)}, bf16[256,512]{1,0:T(8,128)(2,1)S(1)}, u32[]{:S(2)}, u32[]{:S(2)}) collective-permute-start(bf16[256,512]{1,0:T(8,128)(2,1)S(1)} %get-tuple-element.127.refs_2_), channel_id=1, source_target_pairs={{0,4},{4,0},{8,12},{12,8},{16,20},{20,16},{24,28},{28,24},{1,5},{5... | collective-permute-start | bytes 786440 | tf_op jit(solution)/shard_map/ppermute | solution.py:528
  76.1 3.7 %collective-permute-start.29 = (bf16[256,512]{1,0:T(8,128)(2,1)S(1)}, bf16[256,512]{1,0:T(8,128)(2,1)S(1)}, u32[]{:S(2)}, u32[]{:S(2)}) collective-permute-start(bf16[256,512]{1,0:T(8,128)(2,1)S(1)} %get-tuple-element.128.refs_3_), channel_id=1, source_target_pairs={{0,4},{4,0},{8,12},{12,8},{16,20},{20,16},{24,28},{28,24},{1,5},{5... | collective-permute-start | bytes 786440 | tf_op jit(solution)/shard_map/ppermute | solution.py:528
  76.7 10.2 %collective-permute-start.33 = (f16[1032,128]{1,0:T(8,128)(2,1)S(1)}, f16[1032,128]{1,0:T(8,128)(2,1)S(1)}, u32[]{:S(2)}, u32[]{:S(2)}) collective-permute-start(f16[1032,128]{1,0:T(8,128)(2,1)S(1)} %convert_element_type.131), channel_id=1, source_target_pairs={{0,8},{4,12},{8,0},{12,4},{16,24},{20,28},{24,16},{28,20},{1,9},{5... | collective-permute-start | bytes 792584 | tf_op jit(solution)/shard_map/ppermute | solution.py:528
  78.3 8.6 %collective-permute-start.34 = (f16[1032,128]{1,0:T(8,128)(2,1)S(1)}, f16[1032,128]{1,0:T(8,128)(2,1)S(1)}, u32[]{:S(2)}, u32[]{:S(2)}) collective-permute-start(f16[1032,128]{1,0:T(8,128)(2,1)S(1)} %convert_element_type.133), channel_id=1, source_target_pairs={{0,16},{4,20},{8,24},{12,28},{16,0},{20,4},{24,8},{28,12},{1,17},{... | collective-permute-start | bytes 792584 | tf_op jit(solution)/shard_map/ppermute | solution.py:528
  83.2 9.4 %collective-permute-start.31 = (f16[1032,128]{1,0:T(8,128)(2,1)S(1)}, f16[1032,128]{1,0:T(8,128)(2,1)S(1)}, u32[]{:S(2)}, u32[]{:S(2)}) collective-permute-start(f16[1032,128]{1,0:T(8,128)(2,1)S(1)} %convert_element_type.126), channel_id=1, source_target_pairs={{0,8},{4,12},{8,0},{12,4},{16,24},{20,28},{24,16},{28,20},{1,9},{5... | collective-permute-start | bytes 792584 | tf_op jit(solution)/shard_map/ppermute | solution.py:528
  83.8 13.8 %collective-permute-start.32 = (f16[1032,128]{1,0:T(8,128)(2,1)S(1)}, f16[1032,128]{1,0:T(8,128)(2,1)S(1)}, u32[]{:S(2)}, u32[]{:S(2)}) collective-permute-start(f16[1032,128]{1,0:T(8,128)(2,1)S(1)} %convert_element_type.128), channel_id=1, source_target_pairs={{0,16},{4,20},{8,24},{12,28},{16,0},{20,4},{24,8},{28,12},{1,17},{... | collective-permute-start | bytes 792584 | tf_op jit(solution)/shard_map/ppermute | solution.py:528
  84.7 12.9 %collective-permute-start.30 = (f16[1032,128]{1,0:T(8,128)(2,1)S(1)}, f16[1032,128]{1,0:T(8,128)(2,1)S(1)}, u32[]{:S(2)}, u32[]{:S(2)}) collective-permute-start(f16[1032,128]{1,0:T(8,128)(2,1)S(1)} %convert_element_type.124), channel_id=1, source_target_pairs={{0,24},{4,28},{8,16},{12,20},{16,8},{20,12},{24,0},{28,4},{1,25},{... | collective-permute-start | bytes 792584 | tf_op jit(solution)/shard_map/ppermute | solution.py:528
  (15 other events, 40.0 us)
